TPU v7x, 32 devices: a whole 2x2x4 slice. The times are simulated.
32 devices in a mesh: blk: 16 (over z, y, core), group: 2 (over x).
Axes of the slice: x: 2, y: 2, z: 4, core: 2. Of those that a mesh axis runs over, the one named last changes fastest.
Arguments:
- features: bfloat16 [2, 4096, 2048], P('group', 'blk'), may hold values from -0.29882812 to 0.29882812
- head_weight: bfloat16 [2048, 512], replicated, may hold values from -0.125 to 0.125
- pairs: int32 [2, 4096], P('group', 'blk'), may hold values from 0 to 4095, as said below
Outputs:
- pair_logit: float32 [2, 4096], P('group', 'blk')
- row_lse: float32 [2, 4096], P('group', 'blk')
- proj_grad: float32 [2, 4096, 512], P('group', 'blk')
- head_grad: float32 [2048, 512], replicated
Inputs may be any that keep to these rules, and one draw needn't show every extreme that they name: pairs pairs each view with another view of the same group, and pairs[g, pairs[g, i]] = i.
All inputs are finite; a program needn't handle non-finite values.
Results may differ from a plain program's by a relative error of at most 0.004.
Values may be sent and summed in bfloat16 or wider, within the bound.
No kernel may reach another device: no remote copies, remote signals or barrier semaphores. Data moves between devices by JAX's collectives and lax.ppermute only.
A program may use at most 64 MiB of HBM per device.

v0:
```python
import jax
import jax.numpy as jnp
from jax import lax
from jax.sharding import PartitionSpec as P

logit_divisor = 0.1


def tile_scores(sphere_embeddings, partial_block):
    return (
        jnp.einsum(
            "mx,qx->mq", sphere_embeddings, partial_block, preferred_element_type=jnp.float32
        )
        / logit_divisor
    )


def on_device(features, head_weight, pairs):
    feats = features[0]
    partner = pairs[0]
    lines_per_processor = feats.shape[0]
    z = jnp.dot(feats, head_weight, preferred_element_type=jnp.float32)
    inv = lax.rsqrt(jnp.sum(z * z, axis=1) + 1e-06)
    u = z * inv[:, None]
    sphere_embeddings = u.astype(jnp.bfloat16)
    rows_global = lax.axis_index("blk") * lines_per_processor + jnp.arange(
        lines_per_processor, dtype=jnp.int32
    )

    def masked(scores, count):
        cols = jnp.arange(count, dtype=jnp.int32)
        diagonal_exclusion = rows_global[:, None] == cols[None, :]
        pairmask = partner[:, None] == cols[None, :]
        expo = jnp.where(diagonal_exclusion, jnp.zeros_like(scores), jnp.exp(scores))
        return (expo, pairmask)

    partial_block = lax.all_gather(sphere_embeddings, "blk", axis=0, tiled=True)
    scores = tile_scores(sphere_embeddings, partial_block)
    expo, pairmask = masked(scores, partial_block.shape[0])
    den = jnp.sum(expo, axis=1)
    pos = jnp.sum(jnp.where(pairmask, scores, jnp.zeros_like(scores)), axis=1)
    den_all = lax.all_gather(den, "blk", axis=0, tiled=True)
    partial_block = lax.all_gather(sphere_embeddings, "blk", axis=0, tiled=True)
    count = partial_block.shape[0]
    scores = tile_scores(sphere_embeddings, partial_block)
    expo, pairmask = masked(scores, count)
    linear_map_coefficients = (
        expo / den[:, None] + expo / den_all[None, :] - 2.0 * pairmask.astype(jnp.float32)
    )
    collapsed_total_amount = jnp.dot(
        linear_map_coefficients.astype(jnp.bfloat16),
        partial_block,
        preferred_element_type=jnp.float32,
    )
    rescaled_direction_slope = collapsed_total_amount / logit_divisor
    grad_z = inv[:, None] * (
        rescaled_direction_slope - u * jnp.sum(u * rescaled_direction_slope, axis=1, keepdims=True)
    )
    head_term = jnp.einsum(
        "rh,rp->hp", feats, grad_z.astype(jnp.bfloat16), preferred_element_type=jnp.float32
    )
    head_total = lax.psum(head_term, ("blk", "group"))
    return (pos[None, :], jnp.log(den)[None, :], grad_z[None, :, :], head_total)


def solution(mesh):
    in_specs = (P("group", "blk", None), P(), P("group", "blk"))
    out_specs = (P("group", "blk"), P("group", "blk"), P("group", "blk", None), P())
    return jax.shard_map(
        on_device, mesh=mesh, in_specs=in_specs, out_specs=out_specs, check_vma=False
    )
```

profile of v0, /device:TPU:0, one launch (start us, length us, event | category | flops | bytes accessed | tf_op | source)
XLA Modules:
  0.0 245.5 jit_solution(3415466355050183096)
XLA Ops:
  7.2 0.0 copy-start
  7.2 0.0 copy-start.3
  7.2 0.0 all-gather.3.cloned.1.call-start
  7.2 1.5 copy-done
  8.8 2.0 multiply_reduce_fusion.1
  10.8 0.8 multiply_convert_fusion
  11.6 0.0 all-gather.3.cloned.1.call-update
  11.6 0.0 all-reduce.2.cloned.1.call-start
  11.7 53.4 %all-gather.3.cloned.1.call-done = bf16[4096,512]{1,0:T(8,128)(2,1)} async-done(((bf16[256,512]{1,0:T(8,128)(2,1)}), bf16[4096,512]{1,0:T(8,128)(2,1)}) %all-gather.3.cloned.1.call-update) | async-done | bytes 4194320 | tf_op jit(solution)/shard_map/all_gather | solution.py:37
  65.0 0.0 copy-done.3
  65.0 0.0 copy-start.2
  65.0 5.1 %fusion = (f32[256]{0:T(256)S(1)}, f32[256]{0:T(256)}, f32[256,4096]{1,0:T(8,128)S(1)}) fusion(s32[256]{0:T(256)S(1)} %iota_add_fusion, s32[256]{0:T(256)S(1)} %bitcast.23, bf16[256,512]{1,0:T(8,128)(2,1)} %multiply_convert_fusion, bf16[4096,512]{1,0:T(8,128)(2,1)} %all-gather.3.cloned.1.call-done), kind=kOutput, calls=%fused_computation.6 | convolution fusion | flops 1081081344 | bytes 8654848 | tf_op jit(solution)/shard_map/mx,qx->mq/dot_general | solution.py:11
  70.1 18.9 %all-gather = f32[16,1,256]{2,1,0:T(1,128)S(1)} all-gather(f32[1,1,256]{2,1,0:T(1,128)S(1)} %bitcast.21), channel_id=1, replica_groups=mesh['blk'=16,'group'=2] {'blk'}, dimensions={0}, use_global_device_ids=true | all-gather | bytes 17408 | tf_op jit(solution)/shard_map/all_gather | solution.py:42
  89.0 0.0 copy-done.2
  89.0 0.0 copy-start.1
  89.0 2.2 multiply_reduce_fusion
  91.2 0.0 copy-done.1
  91.2 2.9 %convolution_bitcast_fusion = f32[2048,512]{0,1:T(8,128)} fusion(bf16[1,256,2048]{2,1,0:T(8,128)(2,1)S(1)} %copy-done.1, f32[256,512]{1,0:T(8,128)S(1)} %get-tuple-element.18, f32[256,512]{1,0:T(8,128)S(1)} %get-tuple-element.15, f32[256]{0:T(256)S(1)} %get-tuple-element.17, f32[256]{0:T(256)S(1)} %add_rsqrt_fusion), kind=kOutput, calls=%fused_computation.7 | convolution fusion | flops 537526272 | bytes 6293504 | tf_op jit(solution)/shard_map/rh,rp->hp/dot_general | solution.py:59
  94.1 0.0 all-reduce.2.cloned.1.call-update
  94.1 0.6 log.13
  94.7 1.0 fusion.9
  95.6 137.6 %all-reduce.2.cloned.1.call-done = f32[2048,512]{0,1:T(8,128)} async-done(((f32[2048,512]{0,1:T(8,128)}), f32[2048,512]{0,1:T(8,128)}) %all-reduce.2.cloned.1.call-update) | async-done | bytes 4194320 | tf_op jit(solution)/shard_map/psum | solution.py:62
  233.3 5.3 %copy.8 = f32[2048,512]{1,0:T(8,128)} copy(f32[2048,512]{0,1:T(8,128)} %all-reduce.2.cloned.1.call-done) | data formatting | bytes 8388608
  (2 shorter events, 0.0 us)
Async XLA Ops:
  7.2 1.6 copy-start
  7.2 57.9 %copy-start.3 = (s32[1,256]{1,0:T(1,128)S(1)}, s32[1,256]{1,0:T(1,128)}, u32[]{:S(2)}) copy-start(s32[1,256]{1,0:T(1,128)} %param.5) | copy-start | bytes 3076
  7.2 57.9 %all-gather.3.cloned.1.call-start = ((), (), s32[]{:S(2)}) async-start(), calls=%async_computation | async-start | bytes 4456448 | tf_op jit(solution)/shard_map/all_gather | solution.py:37
  11.6 221.7 %all-reduce.2.cloned.1.call-start = ((), (), s32[]{:S(2)}) async-start(), calls=%async_computation.1 | async-start | bytes 8388608 | tf_op jit(solution)/shard_map/psum | solution.py:62
  65.0 24.0 %copy-start.2 = (bf16[4096,512]{1,0:T(8,128)(2,1)S(1)}, bf16[4096,512]{1,0:T(8,128)(2,1)}, u32[]{:S(2)}) copy-start(bf16[4096,512]{1,0:T(8,128)(2,1)} %all-gather.3.cloned.1.call-done) | copy-start | bytes 12582916
  89.0 2.2 copy-start.1
Sparse Core Ops, SparseCore 0:
  11.7 53.2 all-gather.2
  94.2 139.0 all-reduce.1
where the time goes:
time: 246 us; the launch traced here: 245 us
  waiting for transfers between devices  191 us (78%)
  blocking collectives  18.9 us (8%)
  between operations  14.1 us (6%)
  matrix products  12.1 us (5%)
  local copies, waits for them, and re-layouts  7.45 us (3%)
    psum x1, waiting for transfers between devices, on_device(): head_total = lax.psum(head_term, ('blk', 'group'))  138 us
    all_gather x1, waiting for transfers between devices, on_device(): partial_block = lax.all_gather(sphere_embeddings, 'blk', axis=0, tiled=True)  53.4 us
    all_gather x1, blocking collectives, on_device(): den_all = lax.all_gather(den, 'blk', axis=0, tiled=True)  18.9 us
    unnamed x9, local copies, waits for them, and re-layouts  6.88 us
    dot_general x1, matrix products, tile_scores(): jnp.einsum('mx,qx->mq', sphere_embeddings, partial_block, preferred_eleme...  5.08 us
  transfers between devices with their start and end apart: 2, of which 2 were waited for; matrix products, arithmetic and copies ran while one was open for 1% of the time, Pallas kernels for 0%

commit v1 on v0

v1 whole, which is shorter than its diff:
```python
import functools
import math

import jax
import jax.numpy as jnp
from jax import lax
from jax.experimental import pallas as pl
from jax.experimental.pallas import tpu as pltpu
from jax.sharding import PartitionSpec as P

CORE, Y, Z0 = 1, 2, 4
TEMPERATURE = 0.1
SCALE = 1.0 / TEMPERATURE
SCALE2 = SCALE * math.log2(math.e)
LANES = 128
F32, BF16 = jnp.float32, jnp.bfloat16
VMEM = pl.BlockSpec(memory_space=pltpu.VMEM)
ANY = pl.BlockSpec(memory_space=pl.ANY)


def grant(mib):
    return pltpu.CompilerParams(vmem_limit_bytes=mib * 2**20)


def cost(flops, nbytes, exps=0):
    return pl.CostEstimate(flops=flops, bytes_accessed=nbytes, transcendentals=exps)


def dot_nt(a, b):
    return lax.dot_general(a, b, (((1,), (1,)), ((), ())), preferred_element_type=F32)


def dot_tn(a, b):
    return lax.dot_general(a, b, (((0,), (0,)), ((), ())), preferred_element_type=F32)


def project_kernel(f_hbm, w_hbm, z_ref, ub_ref, f, w, sems):
    parts = sems.shape[0]
    depth = f.shape[1] // parts
    spans = [slice(k * depth, (k + 1) * depth) for k in range(parts)]
    copies = []
    for k, span in enumerate(spans):
        of_f = pltpu.make_async_copy(f_hbm.at[:, span], f.at[:, span], sems.at[k, 0])
        of_w = pltpu.make_async_copy(w_hbm.at[span], w.at[span], sems.at[k, 1])
        of_f.start()
        of_w.start()
        copies.append((of_f, of_w))
    z = jnp.zeros(z_ref.shape, F32)
    for span, (of_f, of_w) in zip(spans, copies):
        of_f.wait()
        of_w.wait()
        z = z + jnp.dot(f[:, span], w[span, :], preferred_element_type=F32)
    z_ref[...] = z
    inv = lax.rsqrt(jnp.sum(z * z, axis=1, keepdims=True) + 1e-06)
    ub_ref[...] = (z * inv).astype(BF16)


def project(feats, weight):
    rows, hid = feats.shape
    proj = weight.shape[1]
    return pl.pallas_call(
        project_kernel,
        in_specs=[ANY] * 2,
        out_specs=[VMEM] * 2,
        out_shape=[
            jax.ShapeDtypeStruct((rows, proj), F32),
            jax.ShapeDtypeStruct((rows, proj), BF16),
        ],
        scratch_shapes=[
            pltpu.VMEM((rows, hid), BF16),
            pltpu.VMEM((hid, proj), BF16),
            pltpu.SemaphoreType.DMA((8, 2)),
        ],
        cost_estimate=cost(2 * rows * hid * proj, 2 * hid * (rows + proj)),
        compiler_params=grant(53),
        name="project",
    )(feats, weight)


def fold_lanes(x):
    out = x[:, :LANES]
    for k in range(1, x.shape[1] // LANES):
        out = out + x[:, k * LANES : (k + 1) * LANES]
    return out


def fold_rows(x):
    return jnp.sum(x.reshape(x.shape[0] // 8, 8, x.shape[1]), axis=0)


def exp_scores(x, refs):
    y = jnp.concatenate([ref[...] for ref in refs], axis=0) if len(refs) > 1 else refs[0][...]
    return jnp.exp2(dot_nt(x, y) * SCALE2)


def den_kernel(n_old, n_new, first, *refs):
    total = n_old + n_new
    blocks = refs[:total]
    out_ref, col_acc, row_acc = refs[-3:]
    rows = blocks[0].shape[0]
    col_acc[...] = jnp.zeros_like(col_acc)
    even, odd = range(n_old, total, 2), range(n_old + 1, total, 2)
    for a in even:
        x = blocks[a][...]
        sums = jnp.zeros((rows, LANES), F32)
        for m in range(0, n_old, 2):
            e = exp_scores(x, blocks[m : m + 2])
            col_acc[:, m * rows : (m + 2) * rows] += fold_rows(e)
            sums = sums + fold_lanes(e)
        for m in odd:
            sums = sums + fold_lanes(exp_scores(x, [blocks[m]]))
        row_acc[(a - n_old) // 2] = sums
        for m in even:
            e = exp_scores(x, [blocks[m]])
            if m == a:
                line = lax.broadcasted_iota(jnp.int32, (rows, 1), 0)
                lane = lax.broadcasted_iota(jnp.int32, (1, rows), 1)
                e = jnp.where(line == lane, 0.0, e)
            col_acc[:, m * rows : (m + 1) * rows] += fold_rows(e)

    lane = lax.broadcasted_iota(jnp.int32, (rows, LANES), 1)
    turned = jnp.zeros((rows, LANES), F32)
    for k in range(len(even)):
        turned = jnp.where(lane == k, jnp.sum(row_acc[k], axis=1, keepdims=True), turned)
    turned = turned.T
    out_ref[...] = jnp.zeros_like(out_ref) if first else refs[total][...]
    for p in range(total):
        line = jnp.sum(col_acc[:, p * rows : (p + 1) * rows], axis=0, keepdims=True)
        if p in even:
            k = (p - n_old) // 2
            line = line + turned[k : k + 1, :]
        if p < n_old or p in even:
            out_ref[p : p + 1, :] += line


def partial_den(n_all, before, old, new):
    blocks = old + new
    rows, proj = blocks[0].shape
    total, n_new = len(blocks), len(new)
    turns = (n_new + 1) // 2
    pairs = turns * total
    return pl.pallas_call(
        functools.partial(den_kernel, len(old), n_new, before is None),
        in_specs=[VMEM] * (total + (before is not None)),
        out_specs=VMEM,
        out_shape=jax.ShapeDtypeStruct((n_all, rows), F32),
        scratch_shapes=[
            pltpu.VMEM((8, total * rows), F32),
            pltpu.VMEM((turns, rows, LANES), F32),
        ],
        cost_estimate=cost(0, 0),
        compiler_params=grant(8),
        name="partial_den",
    )(*blocks, *([] if before is None else [before]))


def as_column(line):
    return jnp.broadcast_to(line, (LANES, line.shape[1])).T[:, :1]


def as_line(column):
    return jnp.broadcast_to(column, (column.shape[0], LANES)).T[:1, :]


def partner_column(partner_ref):
    return as_column(partner_ref[...].astype(F32)).astype(jnp.int32)


def position():
    return lax.axis_index("blk"), lax.axis_index("group") & 1


def block_start(b, r, rows):
    return (b ^ r) * rows


def row_kernel(rs, first, partner_ref, x_ref, *refs):
    b, _ = position()
    n_all = len(rs)
    before, refs = (None, refs) if first == 0 else (refs[0], refs[1:])
    blocks, (e_ref, pos_ref), more = refs[:n_all], refs[n_all : n_all + 2], refs[n_all + 2 :]
    if more:
        cross = exp_scores(blocks[-2][...], blocks[-1:])
        more[0][0:1, :] = as_line(jnp.sum(fold_lanes(cross), axis=1, keepdims=True))
        more[0][1:2, :] = jnp.sum(cross, axis=0, keepdims=True)
    rows = x_ref.shape[0]
    partner = partner_column(partner_ref)
    x = x_ref[...]
    lane = lax.broadcasted_iota(jnp.int32, (1, rows), 1)
    line = lax.broadcasted_iota(jnp.int32, (rows, 1), 0)
    hits = jnp.zeros((rows, LANES), F32)
    for p in range(n_all):
        s = dot_nt(x, blocks[p][...])
        e = jnp.exp2(s * SCALE2)
        if first + p == 0:
            e = jnp.where(line == lane, 0.0, e)
        e_ref[:, p * rows : (p + 1) * rows] = e
        paired = (partner - block_start(b, rs[p], rows)) == lane
        hits = hits + fold_lanes(jnp.where(paired, s, 0.0))
    pos = as_line(jnp.sum(hits, axis=1, keepdims=True) * SCALE)
    pos_ref[...] = pos if before is None else pos + before[...]


def own_row(first, partner, x, before, blocks, rs):
    rows, proj = x.shape
    n = len(blocks)
    more = [] if first == 0 else [before]
    return pl.pallas_call(
        functools.partial(row_kernel, rs, first),
        in_specs=[VMEM] * (2 + len(more) + n),
        out_specs=[VMEM] * (2 + len(more)),
        out_shape=[
            jax.ShapeDtypeStruct((rows, n * rows), F32),
            jax.ShapeDtypeStruct((1, rows), F32),
        ]
        + [jax.ShapeDtypeStruct((2, rows), F32)] * len(more),
        cost_estimate=cost(0, 0),
        compiler_params=grant(8),
        name="own_row",
    )(partner, x, *more, *blocks)


def grad_kernel(rs, sizes, *refs):
    partner_ref, z_ref, mine_ref, theirs_ref, cross_ref = refs[:5]
    e_refs, refs = refs[5 : 5 + len(sizes)], refs[5 + len(sizes) :]
    b, _ = position()
    n_all = sum(sizes)
    e_at = [(ref, k) for ref, size in zip(e_refs, sizes) for k in range(size)]
    blocks, (lse_ref, dz_ref, dzb_ref, coef) = refs[:n_all], refs[n_all:]
    rows = z_ref.shape[0]
    den = [
        mine_ref[p : p + 1, :] + theirs_ref[p ^ 1 : (p ^ 1) + 1, :] for p in range(n_all)
    ]
    den[-2] = den[-2] + cross_ref[0:1, :]
    den[-1] = den[-1] + cross_ref[1:2, :]
    lse_ref[...] = jnp.log(den[0])
    inverse = [1.0 / line for line in den]
    own_inverse = as_column(inverse[0])
    partner = partner_column(partner_ref)
    lane = lax.broadcasted_iota(jnp.int32, (1, rows), 1)
    total = jnp.zeros(z_ref.shape, F32)
    part = 4
    for first in range(0, n_all, part):
        for p in range(first, first + part):
            span = slice(p * rows, (p + 1) * rows)
            paired = (partner - block_start(b, rs[p], rows)) == lane
            ref, k = e_at[p]
            e = ref[:, k * rows : (k + 1) * rows]
            h = e * (own_inverse + inverse[p]) - jnp.where(paired, 2.0, 0.0)
            coef[:, span] = h.astype(BF16)
        span = slice(first * rows, (first + part) * rows)
        x = jnp.concatenate([ref[...] for ref in blocks[first : first + part]], axis=0)
        total = total + jnp.dot(coef[:, span], x, preferred_element_type=F32)

    z = z_ref[...]
    inv = lax.rsqrt(jnp.sum(z * z, axis=1, keepdims=True) + 1e-06)
    u = z * inv
    g = total * SCALE
    dz = inv * (g - u * jnp.sum(u * g, axis=1, keepdims=True))
    dz_ref[...] = dz
    dzb_ref[...] = dz.astype(BF16)


def gradient(partner, z, mine, theirs, cross, es, blocks, rs):
    rows, proj = z.shape
    n = len(blocks)
    sizes = [e.shape[1] // rows for e in es]
    return pl.pallas_call(
        functools.partial(grad_kernel, rs, sizes),
        in_specs=[VMEM] * (5 + len(es) + n),
        out_specs=[VMEM] * 3,
        out_shape=[
            jax.ShapeDtypeStruct((1, rows), F32),
            jax.ShapeDtypeStruct((rows, proj), F32),
            jax.ShapeDtypeStruct((rows, proj), BF16),
        ],
        scratch_shapes=[pltpu.VMEM((rows, n * rows), BF16)],
        cost_estimate=cost(2 * n * rows * rows * proj, 6 * n * rows * proj),
        compiler_params=grant(12),
        name="gradient",
    )(partner, z, mine, theirs, cross, *es, *blocks)


def hand_out_kernel(*refs):
    n = len(refs) // 2
    for ref, out in zip(refs[:n], refs[n:]):
        out[...] = ref[...]


def hand_out(*arrays):
    return pl.pallas_call(
        hand_out_kernel,
        in_specs=[VMEM] * len(arrays),
        out_specs=[VMEM] * len(arrays),
        out_shape=[jax.ShapeDtypeStruct(x.shape, x.dtype) for x in arrays],
        cost_estimate=cost(0, 2 * sum(4 * x.size for x in arrays)),
        compiler_params=grant(4),
        name="hand_out",
    )(*arrays)


def head_kernel(planes, near, *refs):
    f_refs, d_refs = refs[:2], refs[2:4]
    keep, to_x, to_y, to_both = refs[4:]
    size = keep.shape[0]
    b, x = position()
    core, y, upper = b & 1, (b >> 1) & 1, (b // (Z0 * planes // 2)) & 1
    upper = upper if near else 1 - upper

    def product(x, y):
        at = (core * 8 + (x * 2 + y) * 2 + upper) * size
        span = pl.ds(pl.multiple_of(at, size), size)
        out = dot_tn(f_refs[0][:, span], d_refs[0][...])
        return out + dot_tn(f_refs[1][:, span], d_refs[1][...])

    to_both[...] = product(1 - x, 1 - y).astype(BF16)
    to_x[...] = product(1 - x, y).astype(BF16)
    to_y[...] = product(x, 1 - y).astype(BF16)
    keep[...] = product(x, y)


def head_partial(planes, near, fs, ds):
    rows, hid = fs[0].shape
    proj = ds[0].shape[1]
    shape = (hid // 16, proj)
    return pl.pallas_call(
        functools.partial(head_kernel, planes, near),
        in_specs=[VMEM] * 4,
        out_specs=[VMEM] * 4,
        out_shape=[jax.ShapeDtypeStruct(shape, t) for t in (F32, BF16, BF16, BF16)],
        cost_estimate=cost(hid * rows * proj, hid * proj),
        compiler_params=grant(8),
        name="head_partial",
    )(*fs, *ds)


def deal_kernel(near, keep, from_x, from_y, from_both, *refs):
    outs, total = refs[:-1], refs[-1]
    b, _ = position()
    n = len(outs)
    depth = total.shape[0] // n
    there = from_x[...].astype(F32) + from_y[...].astype(F32) + from_both[...].astype(F32)
    total[...] = keep[...] + there
    for k, out in enumerate(outs):
        place = ((b // Z0) ^ k) & (n - 1)
        chunk = total[pl.ds(pl.multiple_of(place * depth, depth), depth), :]
        out[...] = chunk.astype(out.dtype)


def deal(planes, near, keep, *got):
    rows, proj = keep.shape
    n = planes // 2
    kinds = [F32 if near and k == 0 else BF16 for k in range(n)]
    return pl.pallas_call(
        functools.partial(deal_kernel, near),
        in_specs=[VMEM] * 4,
        out_specs=[VMEM] * n,
        out_shape=[jax.ShapeDtypeStruct((rows // n, proj), t) for t in kinds],
        scratch_shapes=[pltpu.VMEM((rows, proj), F32)],
        cost_estimate=cost(0, 0),
        compiler_params=grant(4),
        name="deal",
    )(keep, *got)


def place_kernel(plan, planes, *refs):
    pieces, (out_ref, wide, sem) = refs[: len(plan)], refs[-3:]
    half = out_ref.shape[0] // 2
    b, side = position()
    copies = []
    for ref, (other, keys) in zip(pieces, plan):
        depth = ref.shape[1]
        core = (b & 1) ^ other
        for m, (s, r) in enumerate(keys):
            slot = len(copies)
            wide[slot] = ref[m].astype(F32)
            y = ((b >> 1) & 1) ^ ((r >> 1) & 1)
            plane = (b // Z0) ^ (r // Z0)
            at = core * half + (((side ^ s) * 2 + y) * planes + plane) * depth
            copy = pltpu.make_async_copy(
                wide.at[slot],
                out_ref.at[pl.ds(pl.multiple_of(at, depth), depth)],
                sem.at[slot],
            )
            copy.start()
            copies.append(copy)
    for copy in copies:
        copy.wait()


def place(planes, pieces, plan, shape, before=None):
    n = len(pieces)
    more = [] if before is None else [before]
    chunks = sum(len(keys) for _, keys in plan)
    return pl.pallas_call(
        functools.partial(place_kernel, plan, planes),
        in_specs=[VMEM] * n + [ANY] * len(more),
        out_specs=ANY,
        out_shape=jax.ShapeDtypeStruct(shape, F32),
        input_output_aliases={n: 0} if more else {},
        scratch_shapes=[
            pltpu.VMEM((chunks, *pieces[0].shape[1:]), F32),
            pltpu.SemaphoreType.DMA((chunks,)),
        ],
        cost_estimate=cost(0, 0),
        compiler_params=grant(8),
        name="place",
    )(*pieces, *more)


def gate(x, *after):
    return lax.optimization_barrier((x, *after))[0]


def swap(x, mask, axis, size):
    return lax.ppermute(x, axis, [(i, i ^ mask) for i in range(size)])


def on_device(n_blk, n_group, features, head_weight, pairs):
    feats = features[0]
    rows, hid = feats.shape
    proj = head_weight.shape[1]
    planes = n_blk // Z0

    def blk_swap(x, mask):
        return swap(x, mask, "blk", n_blk)

    def group_swap(x):
        return swap(x, 1, "group", n_group)

    def both_swap(x):
        moves = [
            (i * n_group + k, (i ^ Y) * n_group + (k ^ 1))
            for i in range(n_blk)
            for k in range(n_group)
        ]
        return lax.ppermute(x, ("blk", "group"), moves)

    z, ub = project(feats, head_weight)
    f_core = blk_swap(feats, CORE)

    seen, dens, es, pos = [], [], [], None

    def use(*new):
        before = dens[-1] if dens else None
        new = [item for pair in new for item in pair]
        dens.append(partial_den(n_blk, before, [x for x, _ in seen], [x for x, _ in new]))
        seen.extend(new)

    def take_row(start):
        blocks, rs = zip(*seen[start:])
        e, *rest = own_row(start, pairs, ub, pos, blocks, rs)
        es.append(e)
        return rest

    def pair(x, r, *after):
        return [(x, r), (blk_swap(gate(x, *after), CORE), r | CORE)]

    near, over_y = blk_swap(ub, Z0), blk_swap(ub, Y)
    if planes == 4:
        far = blk_swap(ub, 2 * Z0)
        mid = blk_swap(far, Z0)
        use(pair(ub, 0))
        near_y = blk_swap(gate(near, over_y), Y)
        use(pair(near, Z0))
        far_y = blk_swap(gate(far, dens[1]), Y)
        use(pair(over_y, Y), pair(far, 2 * Z0))
        mid_y = blk_swap(gate(mid, dens[2]), Y)
        use(pair(near_y, Z0 | Y), pair(far_y, 2 * Z0 | Y, mid), pair(mid, 3 * Z0))
        (pos,) = take_row(0)
        ending = pair(mid_y, 3 * Z0 | Y, dens[-1], es[-1])
    else:
        use(pair(ub, 0))
        waiting = pair(over_y, Y)
        for dz in range(1, planes):
            x = blk_swap(ub, dz * Z0)
            use(waiting, pair(x, dz * Z0))
            waiting = pair(blk_swap(x, Y), dz * Z0 | Y)
        (pos,) = take_row(0)
        ending = waiting

    use(ending[:1])
    seen.append(ending[1])
    theirs = blk_swap(dens[-1], CORE)
    pos, cross = take_row(es[0].shape[1] // rows)
    lse, grad_z, dz_own = gradient(
        pairs, z, dens[-1], theirs, cross, es, [x for x, _ in seen], [r for _, r in seen]
    )

    pos, lse, grad_z = hand_out(pos, lse, grad_z)
    fs, ds = [feats, f_core], [dz_own, blk_swap(dz_own, CORE)]
    n_half = planes // 2
    keep, *sends = head_partial(planes, False, fs, ds)
    sent = [group_swap(sends[0]), blk_swap(sends[1], Y), both_swap(sends[2])]
    far_sends = deal(planes, False, gate(keep, grad_z), *sent)
    got = [blk_swap(x, (n_half + k) * Z0) for k, x in enumerate(far_sends)]
    keep, *sends = head_partial(planes, True, fs, [gate(ds[0], keep), ds[1]])
    sent = [group_swap(sends[0]), blk_swap(sends[1], Y), both_swap(sends[2])]
    total, *near_sends = deal(planes, True, gate(keep, got[0]), *sent)
    got += [blk_swap(x, k * Z0) for k, x in enumerate(near_sends, 1)]
    for x in got:
        total = total + x.astype(F32)
    if n_group > 2:
        every = lax.all_gather(total, "group")
        side = lax.axis_index("group") & 1
        total = sum(jnp.where(side == i % 2, every[i], 0.0) for i in range(n_group))
    done = total.astype(BF16)

    line = [done] + [blk_swap(done, dz * Z0) for dz in range(1, planes)]

    def write(some, before):
        return place(
            planes, [x for x, _, _ in some], [some_of[1:] for some_of in some], (hid, proj), before
        )

    def swapped(some, *after):
        return [(blk_swap(gate(x, *after), CORE), 1, keys) for x, _, keys in some]

    head_total, sets = None, []
    for at in (0, n_half):
        part = jnp.stack(line[at : at + n_half])
        rs = [dz * Z0 for dz in range(at, at + n_half)]
        sets.append(
            [
                (part, 0, [(0, r) for r in rs]),
                (group_swap(part), 0, [(1, r) for r in rs]),
                (blk_swap(part, Y), 0, [(0, r | Y) for r in rs]),
                (both_swap(part), 0, [(1, r | Y) for r in rs]),
            ]
        )
    g = sets[0]
    head_total = write(g + swapped(g[:1]) + swapped(g[1:3], g[3][0]) + swapped(g[3:]), None)
    others = swapped(sets[1])
    head_total = write(sets[1] + others, head_total)
    return (pos, lse, grad_z[None, :, :], head_total)


def solution(mesh):
    n_blk, n_group = mesh.shape["blk"], mesh.shape["group"]

    def program(features, head_weight, pairs):
        return on_device(n_blk, n_group, features, head_weight, pairs)

    in_specs = (P("group", "blk", None), P(), P("group", "blk"))
    out_specs = (P("group", "blk"), P("group", "blk"), P("group", "blk", None), P())
    return jax.shard_map(
        program, mesh=mesh, in_specs=in_specs, out_specs=out_specs, check_vma=False
    )
```

time: 246 us -> 91.6 us (0.37)
  waiting for transfers between devices: 191 us -> 34.1 us
  starting transfers between devices: 0.08 us -> 38.2 us
  blocking collectives: 18.9 us -> 0 us
  Pallas kernels: 0 us -> 18.1 us
  between operations: 14.1 us -> 0.98 us
  matrix products: 12.1 us -> 0 us
  local copies, waits for them, and re-layouts: 7.45 us -> 0.01 us
    psum x1 -> x0, waiting for transfers between devices: 138 us -> none  [on_device(): head_total = lax.psum(head_term, ('blk', 'group'))]
    all_gather x1 -> x0, waiting for transfers between devices: 53.4 us -> none  [on_device(): partial_block = lax.all_gather(sphere_embeddings, 'blk', axis=0, tiled=True)]
    ppermute x0 -> x44, starting transfers between devices: none -> 38.2 us  [the longest x40 33.8 us: swap(): return lax.ppermute(x, axis, [(i, i ^ mask) for i in range(size)])]
    ppermute x0 -> x44, waiting for transfers between devices: none -> 34.1 us  [the longest x40 31 us: swap(): return lax.ppermute(x, axis, [(i, i ^ mask) for i in range(size)])]
    all_gather x1 -> x0, blocking collectives: 18.9 us -> none  [on_device(): den_all = lax.all_gather(den, 'blk', axis=0, tiled=True)]
    pallas_call x0 -> x16, Pallas kernels: none -> 18.1 us  [the longest x5 6.89 us: partial_den(): pl.pallas_call(functools.partial(den_kernel, len(old), n_new, before is N...]
    dot_general x4 -> x0, matrix products: 12.1 us -> none  [the longest x1 5.08 us: tile_scores(): jnp.einsum('mx,qx->mq', sphere_embeddings, partial_block, preferred_eleme...]
    unnamed x9 -> x4, local copies, waits for them, and re-layouts: 6.88 us -> 0.01 us
  transfers between devices with their start and end apart: 2 -> 44, of which waited for: 2 -> 21; matrix products, arithmetic and copies ran while one was open for 1% -> 0% of each run, Pallas kernels for 0% -> 15%
where the time goes in v1:
time: 91.6 us; the launch traced here: 91.5 us
  starting transfers between devices  38.2 us (42%)
  waiting for transfers between devices  34.1 us (37%)
  Pallas kernels  18.1 us (20%)
  between operations  0.98 us (1%)
    ppermute x40, starting transfers between devices, swap(): return lax.ppermute(x, axis, [(i, i ^ mask) for i in range(size)])  33.8 us
    ppermute x40, waiting for transfers between devices, swap(): return lax.ppermute(x, axis, [(i, i ^ mask) for i in range(size)])  31 us
    pallas_call x5, Pallas kernels, partial_den(): pl.pallas_call(functools.partial(den_kernel, len(old), n_new, before is N...  6.89 us
    ppermute x4, starting transfers between devices, both_swap(): return lax.ppermute(x, ('blk', 'group'), moves)  4.4 us
    ppermute x4, waiting for transfers between devices, both_swap(): return lax.ppermute(x, ('blk', 'group'), moves)  3.1 us
    pallas_call x2, Pallas kernels, place(): pl.pallas_call(functools.partial(place_kernel, plan, planes), in_specs=[V...  2.92 us
    pallas_call x1, Pallas kernels, project(): pl.pallas_call(project_kernel, in_specs=[ANY] * 2, out_specs=[VMEM] * 2,...  2.46 us
    pallas_call x2, Pallas kernels, own_row(): pl.pallas_call(functools.partial(row_kernel, rs, first), in_specs=[VMEM]...  2.07 us
  transfers between devices with their start and end apart: 44, of which 21 were waited for; matrix products, arithmetic and copies ran while one was open for 0% of the time, Pallas kernels for 15%

profile of v1, /device:TPU:0, one launch (start us, length us, event | category | flops | bytes accessed | tf_op | source)
XLA Modules:
  0.0 91.5 jit_solution(13562831579871281)
XLA Ops:
  0.6 2.5 %project.1 = (f32[256,512]{1,0:T(8,128)S(1)}, bf16[256,512]{1,0:T(8,128)(2,1)S(1)}) custom-call(bf16[256,2048]{1,0:T(8,128)(2,1)} %bitcast.6, bf16[2048,512]{1,0:T(8,128)(2,1)} %w_hbm.1), custom_call_target="tpu_custom_call" | custom-call | flops 536870912 | bytes 3145728 | tf_op jit(solution)/shard_map/project/pallas_call | solution.py:61
  3.1 3.1 %collective-permute-start.1 = (bf16[256,512]{1,0:T(8,128)(2,1)S(1)}, bf16[256,512]{1,0:T(8,128)(2,1)S(1)}, u32[]{:S(2)}, u32[]{:S(2)}) collective-permute-start(bf16[256,512]{1,0:T(8,128)(2,1)S(1)} %get-tuple-element.39.refs_0_.x_ref.refs_7_), channel_id=1, source_target_pairs={{0,8},{2,10},{4,12},{6,14},{8,0},{10,2},{12,4},{14,6},{16,24},{18,... | collective-permute-start | bytes 786440 | tf_op jit(solution)/shard_map/ppermute | solution.py:416
  6.2 1.5 %collective-permute-start.3 = (bf16[256,512]{1,0:T(8,128)(2,1)S(1)}, bf16[256,512]{1,0:T(8,128)(2,1)S(1)}, u32[]{:S(2)}, u32[]{:S(2)}) collective-permute-start(bf16[256,512]{1,0:T(8,128)(2,1)S(1)} %get-tuple-element.39.refs_0_.x_ref.refs_7_), channel_id=1, source_target_pairs={{0,4},{2,6},{4,0},{6,2},{8,12},{10,14},{12,8},{14,10},{16,20},{18,... | collective-permute-start | bytes 786440 | tf_op jit(solution)/shard_map/ppermute | solution.py:416
  7.7 2.6 %collective-permute-start.5 = (bf16[256,512]{1,0:T(8,128)(2,1)S(1)}, bf16[256,512]{1,0:T(8,128)(2,1)S(1)}, u32[]{:S(2)}, u32[]{:S(2)}) collective-permute-start(bf16[256,512]{1,0:T(8,128)(2,1)S(1)} %get-tuple-element.39.refs_0_.x_ref.refs_7_), channel_id=1, source_target_pairs={{0,16},{2,18},{4,20},{6,22},{8,24},{10,26},{12,28},{14,30},{16,0},... | collective-permute-start | bytes 786440 | tf_op jit(solution)/shard_map/ppermute | solution.py:416
  10.3 6.4 %collective-permute-done.1.refs_2_.refs_9_ = bf16[256,512]{1,0:T(8,128)(2,1)S(1)} collective-permute-done((bf16[256,512]{1,0:T(8,128)(2,1)S(1)}, bf16[256,512]{1,0:T(8,128)(2,1)S(1)}, u32[]{:S(2)}, u32[]{:S(2)}) %collective-permute-start.1) | collective-permute-done | bytes 262176 | tf_op jit(solution)/shard_map/ppermute | solution.py:416
  16.8 2.7 %collective-permute-start.7 = (bf16[256,512]{1,0:T(8,128)(2,1)S(1)}, bf16[256,512]{1,0:T(8,128)(2,1)S(1)}, u32[]{:S(2)}, u32[]{:S(2)}) collective-permute-start(bf16[256,512]{1,0:T(8,128)(2,1)S(1)} %collective-permute-done.1.refs_2_.refs_9_), channel_id=1, source_target_pairs={{0,4},{2,6},{4,0},{6,2},{8,12},{10,14},{12,8},{14,10},{16,20},{18,... | collective-permute-start | bytes 786440 | tf_op jit(solution)/shard_map/ppermute | solution.py:416
  19.5 0.2 collective-permute-start.4
  19.7 2.1 %collective-permute-done.5.refs_6_.refs_13_ = bf16[256,512]{1,0:T(8,128)(2,1)S(1)} collective-permute-done((bf16[256,512]{1,0:T(8,128)(2,1)S(1)}, bf16[256,512]{1,0:T(8,128)(2,1)S(1)}, u32[]{:S(2)}, u32[]{:S(2)}) %collective-permute-start.5) | collective-permute-done | bytes 262176 | tf_op jit(solution)/shard_map/ppermute | solution.py:416
  21.8 0.5 partial_den.5.refs_4_
  22.3 0.6 partial_den.6.refs_8_
  22.9 0.7 collective-permute-start.9
  23.6 3.0 %collective-permute-done.7.refs_8_.refs_15_ = bf16[256,512]{1,0:T(8,128)(2,1)S(1)} collective-permute-done((bf16[256,512]{1,0:T(8,128)(2,1)S(1)}, bf16[256,512]{1,0:T(8,128)(2,1)S(1)}, u32[]{:S(2)}, u32[]{:S(2)}) %collective-permute-start.7) | collective-permute-done | bytes 262176 | tf_op jit(solution)/shard_map/ppermute | solution.py:416
  26.6 3.9 %collective-permute-done.10.refs_12_.refs_19_ = bf16[256,512]{1,0:T(8,128)(2,1)S(1)} collective-permute-done((bf16[256,512]{1,0:T(8,128)(2,1)S(1)}, bf16[256,512]{1,0:T(8,128)(2,1)S(1)}, u32[]{:S(2)}, u32[]{:S(2)}) %collective-permute-start.10) | collective-permute-done | bytes 262176 | tf_op jit(solution)/shard_map/ppermute | solution.py:416
  30.5 0.5 collective-permute-start.12
  31.0 1.3 %partial_den.7.refs_14_ = f32[16,256]{1,0:T(8,128)S(1)} custom-call(bf16[256,512]{1,0:T(8,128)(2,1)S(1)} %get-tuple-element.39.refs_0_.x_ref.refs_7_, bf16[256,512]{1,0:T(8,128)(2,1)S(1)} %collective-permute-done.refs_1_.refs_8_, bf16[256,512]{1,0:T(8,128)(2,1)S(1)} %collective-permute-done.1.refs_2_.refs_9_, ...), custom_call_target="tpu_custom_call" | custom-call | tf_op jit(solution)/shard_map/partial_den/pallas_call | solution.py:142
  32.4 1.4 %collective-permute-start.13 = (bf16[256,512]{1,0:T(8,128)(2,1)S(1)}, bf16[256,512]{1,0:T(8,128)(2,1)S(1)}, u32[]{:S(2)}, u32[]{:S(2)}) collective-permute-start(bf16[256,512]{1,0:T(8,128)(2,1)S(1)} %collective-permute-done.10.refs_12_.refs_19_), channel_id=1, source_target_pairs={{0,4},{2,6},{4,0},{6,2},{8,12},{10,14},{12,8},{14,10},{16,20},{18,... | collective-permute-start | bytes 786440 | tf_op jit(solution)/shard_map/ppermute | solution.py:416
  34.0 3.1 %partial_den.8.refs_15_ = f32[16,256]{1,0:T(8,128)S(1)} custom-call(bf16[256,512]{1,0:T(8,128)(2,1)S(1)} %get-tuple-element.39.refs_0_.x_ref.refs_7_, bf16[256,512]{1,0:T(8,128)(2,1)S(1)} %collective-permute-done.refs_1_.refs_8_, bf16[256,512]{1,0:T(8,128)(2,1)S(1)} %collective-permute-done.1.refs_2_.refs_9_, ...), custom_call_target="tpu_custom_call" | custom-call | tf_op jit(solution)/shard_map/partial_den/pallas_call | solution.py:142
  37.1 1.5 %own_row.2 = (f32[256,3584]{1,0:T(8,128)S(1)}, f32[1,256]{1,0:T(1,128)S(1)}) custom-call(s32[1,256]{1,0:T(1,128)S(1)} %copy-done.1, bf16[256,512]{1,0:T(8,128)(2,1)S(1)} %get-tuple-element.39.refs_0_.x_ref.refs_7_, bf16[256,512]{1,0:T(8,128)(2,1)S(1)} %get-tuple-element.39.refs_0_.x_ref.refs_7_, bf16[256,512]{1,0:T(8,128)(2,1)S(1)} %collective-permute-done.refs_1_.refs_8_, ...), custom_call_target="tpu_custom_call" | custom-call | tf_op jit(solution)/shard_map/own_row/pallas_call | solution.py:208
  38.6 2.5 %collective-permute-done.13.refs_1_.refs_14_.refs_21_ = bf16[256,512]{1,0:T(8,128)(2,1)S(1)} collective-permute-done((bf16[256,512]{1,0:T(8,128)(2,1)S(1)}, bf16[256,512]{1,0:T(8,128)(2,1)S(1)}, u32[]{:S(2)}, u32[]{:S(2)}) %collective-permute-start.13) | collective-permute-done | bytes 262176 | tf_op jit(solution)/shard_map/ppermute | solution.py:416
  41.2 1.4 %partial_den.9.refs_2_ = f32[16,256]{1,0:T(8,128)S(1)} custom-call(bf16[256,512]{1,0:T(8,128)(2,1)S(1)} %get-tuple-element.39.refs_0_.x_ref.refs_7_, bf16[256,512]{1,0:T(8,128)(2,1)S(1)} %collective-permute-done.refs_1_.refs_8_, bf16[256,512]{1,0:T(8,128)(2,1)S(1)} %collective-permute-done.1.refs_2_.refs_9_, ...), custom_call_target="tpu_custom_call" | custom-call | tf_op jit(solution)/shard_map/partial_den/pallas_call | solution.py:142
  42.6 0.5 collective-permute-start.15
  43.1 0.5 own_row.3
  43.6 0.3 collective-permute-done.15.refs_3_
  43.9 1.8 %gradient.1 = (f32[1,256]{1,0:T(1,128)S(1)}, f32[256,512]{1,0:T(8,128)S(1)}, bf16[256,512]{1,0:T(8,128)(2,1)S(1)}) custom-call(s32[1,256]{1,0:T(1,128)S(1)} %copy-done.1, f32[256,512]{1,0:T(8,128)S(1)} %get-tuple-element.48.refs_1_, f32[16,256]{1,0:T(8,128)S(1)} %partial_den.9.refs_2_, f32[16,256]{1,0:T(8,128)S(1)} %collective-permute-done.15.refs_3_, ...), custom_call_target="tpu_custom_call" | custom-call | flops 1073741824 | bytes 12582912 | tf_op jit(solution)/shard_map/gradient/pallas_call | solution.py:268
  45.7 0.4 collective-permute-start.17
  46.1 1.2 %collective-permute-done.17.refs_3_ = bf16[256,512]{1,0:T(8,128)(2,1)S(1)} collective-permute-done((bf16[256,512]{1,0:T(8,128)(2,1)S(1)}, bf16[256,512]{1,0:T(8,128)(2,1)S(1)}, u32[]{:S(2)}, u32[]{:S(2)}) %collective-permute-start.17) | collective-permute-done | bytes 262176 | tf_op jit(solution)/shard_map/ppermute | solution.py:416
  47.3 0.5 head_partial.2
  47.8 1.6 %collective-permute-start.18 = (bf16[128,512]{1,0:T(8,128)(2,1)S(1)}, bf16[128,512]{1,0:T(8,128)(2,1)S(1)}, u32[]{:S(2)}, u32[]{:S(2)}) collective-permute-start(bf16[128,512]{1,0:T(8,128)(2,1)S(1)} %get-tuple-element.61), channel_id=1, source_target_pairs={{0,1},{1,0},{2,3},{3,2},{4,5},{5,4},{6,7},{7,6},{8,9},{9,8},{10,11... | collective-permute-start | bytes 393224 | tf_op jit(solution)/shard_map/ppermute | solution.py:416
  49.4 1.4 %collective-permute-start.19 = (bf16[128,512]{1,0:T(8,128)(2,1)S(1)}, bf16[128,512]{1,0:T(8,128)(2,1)S(1)}, u32[]{:S(2)}, u32[]{:S(2)}) collective-permute-start(bf16[128,512]{1,0:T(8,128)(2,1)S(1)} %get-tuple-element.62), channel_id=1, source_target_pairs={{0,4},{2,6},{4,0},{6,2},{8,12},{10,14},{12,8},{14,10},{16,20},{18,... | collective-permute-start | bytes 393224 | tf_op jit(solution)/shard_map/ppermute | solution.py:416
  50.8 0.6 collective-permute-start.20
  51.4 0.5 head_partial.3
  51.9 1.6 %collective-permute-start.22 = (bf16[128,512]{1,0:T(8,128)(2,1)S(1)}, bf16[128,512]{1,0:T(8,128)(2,1)S(1)}, u32[]{:S(2)}, u32[]{:S(2)}) collective-permute-start(bf16[128,512]{1,0:T(8,128)(2,1)S(1)} %get-tuple-element.66), channel_id=1, source_target_pairs={{0,1},{1,0},{2,3},{3,2},{4,5},{5,4},{6,7},{7,6},{8,9},{9,8},{10,11... | collective-permute-start | bytes 393224 | tf_op jit(solution)/shard_map/ppermute | solution.py:416
  53.5 1.4 %collective-permute-start.23 = (bf16[128,512]{1,0:T(8,128)(2,1)S(1)}, bf16[128,512]{1,0:T(8,128)(2,1)S(1)}, u32[]{:S(2)}, u32[]{:S(2)}) collective-permute-start(bf16[128,512]{1,0:T(8,128)(2,1)S(1)} %get-tuple-element.67), channel_id=1, source_target_pairs={{0,4},{2,6},{4,0},{6,2},{8,12},{10,14},{12,8},{14,10},{16,20},{18,... | collective-permute-start | bytes 393224 | tf_op jit(solution)/shard_map/ppermute | solution.py:416
  54.8 1.7 %collective-permute-start.24 = (bf16[128,512]{1,0:T(8,128)(2,1)S(1)}, bf16[128,512]{1,0:T(8,128)(2,1)S(1)}, u32[]{:S(2)}, u32[]{:S(2)}) collective-permute-start(bf16[128,512]{1,0:T(8,128)(2,1)S(1)} %get-tuple-element.68), channel_id=1, source_target_pairs={{0,5},{1,4},{2,7},{3,6},{4,1},{5,0},{6,3},{7,2},{8,13},{9,12},{10,... | collective-permute-start | bytes 393224 | tf_op jit(solution)/shard_map/ppermute | solution.py:437
  56.5 0.8 hand_out.1
  57.4 0.3 collective-permute-done.19.from_y
  57.7 0.4 collective-permute-done.20.from_both
  58.2 2.5 %collective-permute-start.21 = (bf16[64,512]{1,0:T(8,128)(2,1)S(1)}, bf16[64,512]{1,0:T(8,128)(2,1)S(1)}, u32[]{:S(2)}, u32[]{:S(2)}) collective-permute-start(bf16[64,512]{1,0:T(8,128)(2,1)S(1)} %get-tuple-element.64), channel_id=1, source_target_pairs={{0,16},{2,18},{4,20},{6,22},{8,24},{10,26},{12,28},{14,30},{16,0},... | collective-permute-start | bytes 196616 | tf_op jit(solution)/shard_map/ppermute | solution.py:416
  60.7 1.4 %collective-permute-start.25 = (bf16[64,512]{1,0:T(8,128)(2,1)S(1)}, bf16[64,512]{1,0:T(8,128)(2,1)S(1)}, u32[]{:S(2)}, u32[]{:S(2)}) collective-permute-start(bf16[64,512]{1,0:T(8,128)(2,1)S(1)} %get-tuple-element.70), channel_id=1, source_target_pairs={{0,24},{2,26},{4,28},{6,30},{8,16},{10,18},{12,20},{14,22},{16,8},... | collective-permute-start | bytes 196616 | tf_op jit(solution)/shard_map/ppermute | solution.py:416
  62.1 2.6 %collective-permute-done.21 = bf16[64,512]{1,0:T(8,128)(2,1)S(1)} collective-permute-done((bf16[64,512]{1,0:T(8,128)(2,1)S(1)}, bf16[64,512]{1,0:T(8,128)(2,1)S(1)}, u32[]{:S(2)}, u32[]{:S(2)}) %collective-permute-start.21) | collective-permute-done | bytes 65568 | tf_op jit(solution)/shard_map/ppermute | solution.py:416
  64.8 0.3 collective-permute-start.26
  65.1 1.9 %collective-permute-done.25 = bf16[64,512]{1,0:T(8,128)(2,1)S(1)} collective-permute-done((bf16[64,512]{1,0:T(8,128)(2,1)S(1)}, bf16[64,512]{1,0:T(8,128)(2,1)S(1)}, u32[]{:S(2)}, u32[]{:S(2)}) %collective-permute-start.25) | collective-permute-done | bytes 65568 | tf_op jit(solution)/shard_map/ppermute | solution.py:416
  67.0 2.2 %collective-permute-done.26 = bf16[64,512]{1,0:T(8,128)(2,1)S(1)} collective-permute-done((bf16[64,512]{1,0:T(8,128)(2,1)S(1)}, bf16[64,512]{1,0:T(8,128)(2,1)S(1)}, u32[]{:S(2)}, u32[]{:S(2)}) %collective-permute-start.26) | collective-permute-done | bytes 65568 | tf_op jit(solution)/shard_map/ppermute | solution.py:416
  69.2 0.3 collective-permute-start.36
  69.5 2.6 %collective-permute-start.28 = (bf16[64,512]{1,0:T(8,128)(2,1)S(1)}, bf16[64,512]{1,0:T(8,128)(2,1)S(1)}, u32[]{:S(2)}, u32[]{:S(2)}) collective-permute-start(bf16[64,512]{1,0:T(8,128)(2,1)S(1)} %add_convert_fusion), channel_id=1, source_target_pairs={{0,24},{2,26},{4,28},{6,30},{8,16},{10,18},{12,20},{14,22},{16,8},... | collective-permute-start | bytes 196616 | tf_op jit(solution)/shard_map/ppermute | solution.py:416
  72.0 0.7 collective-permute-start.27
  72.8 1.4 %collective-permute-done.36 = bf16[64,512]{1,0:T(8,128)(2,1)S(1)} collective-permute-done((bf16[64,512]{1,0:T(8,128)(2,1)S(1)}, bf16[64,512]{1,0:T(8,128)(2,1)S(1)}, u32[]{:S(2)}, u32[]{:S(2)}) %collective-permute-start.36) | collective-permute-done | bytes 65568 | tf_op jit(solution)/shard_map/ppermute | solution.py:416
  74.2 1.7 %collective-permute-start.37 = (bf16[2,64,512]{2,1,0:T(8,128)(2,1)S(1)}, bf16[2,64,512]{2,1,0:T(8,128)(2,1)S(1)}, u32[]{:S(2)}, u32[]{:S(2)}) collective-permute-start(bf16[2,64,512]{2,1,0:T(8,128)(2,1)S(1)} %pad_maximum_fusion.1.refs_0_), channel_id=1, source_target_pairs={{0,1},{1,0},{2,3},{3,2},{4,5},{5,4},{6,7},{7,6},{8,9},{9,8},{10,11... | collective-permute-start | bytes 393224 | tf_op jit(solution)/shard_map/ppermute | solution.py:416
  75.9 0.4 collective-permute-start.38
  76.3 1.4 %collective-permute-start.39 = (bf16[2,64,512]{2,1,0:T(8,128)(2,1)S(1)}, bf16[2,64,512]{2,1,0:T(8,128)(2,1)S(1)}, u32[]{:S(2)}, u32[]{:S(2)}) collective-permute-start(bf16[2,64,512]{2,1,0:T(8,128)(2,1)S(1)} %pad_maximum_fusion.1.refs_0_), channel_id=1, source_target_pairs={{0,5},{1,4},{2,7},{3,6},{4,1},{5,0},{6,3},{7,2},{8,13},{9,12},{10,... | collective-permute-start | bytes 393224 | tf_op jit(solution)/shard_map/ppermute | solution.py:437
  77.7 0.2 collective-permute-done.27
  77.9 2.0 %collective-permute-start.29 = (bf16[2,64,512]{2,1,0:T(8,128)(2,1)S(1)}, bf16[2,64,512]{2,1,0:T(8,128)(2,1)S(1)}, u32[]{:S(2)}, u32[]{:S(2)}) collective-permute-start(bf16[2,64,512]{2,1,0:T(8,128)(2,1)S(1)} %pad_maximum_fusion.refs_0_), channel_id=1, source_target_pairs={{0,1},{1,0},{2,3},{3,2},{4,5},{5,4},{6,7},{7,6},{8,9},{9,8},{10,11... | collective-permute-start | bytes 393224 | tf_op jit(solution)/shard_map/ppermute | solution.py:416
  79.9 1.2 %collective-permute-start.30 = (bf16[2,64,512]{2,1,0:T(8,128)(2,1)S(1)}, bf16[2,64,512]{2,1,0:T(8,128)(2,1)S(1)}, u32[]{:S(2)}, u32[]{:S(2)}) collective-permute-start(bf16[2,64,512]{2,1,0:T(8,128)(2,1)S(1)} %pad_maximum_fusion.refs_0_), channel_id=1, source_target_pairs={{0,4},{2,6},{4,0},{6,2},{8,12},{10,14},{12,8},{14,10},{16,20},{18,... | collective-permute-start | bytes 393224 | tf_op jit(solution)/shard_map/ppermute | solution.py:416
  81.1 0.7 collective-permute-start.31
  81.9 0.6 collective-permute-done.39.refs_3_
  82.4 0.7 collective-permute-done.38.refs_2_
  83.2 0.6 collective-permute-done.29.refs_1_
  83.7 1.2 %collective-permute-done.30.refs_2_ = bf16[2,64,512]{2,1,0:T(8,128)(2,1)S(1)} collective-permute-done((bf16[2,64,512]{2,1,0:T(8,128)(2,1)S(1)}, bf16[2,64,512]{2,1,0:T(8,128)(2,1)S(1)}, u32[]{:S(2)}, u32[]{:S(2)}) %collective-permute-start.30) | collective-permute-done | bytes 131104 | tf_op jit(solution)/shard_map/ppermute | solution.py:416
  84.9 2.1 %collective-permute-done.31.refs_3_ = bf16[2,64,512]{2,1,0:T(8,128)(2,1)S(1)} collective-permute-done((bf16[2,64,512]{2,1,0:T(8,128)(2,1)S(1)}, bf16[2,64,512]{2,1,0:T(8,128)(2,1)S(1)}, u32[]{:S(2)}, u32[]{:S(2)}) %collective-permute-start.31) | collective-permute-done | bytes 131104 | tf_op jit(solution)/shard_map/ppermute | solution.py:437
  87.0 0.5 collective-permute-start.33
  87.6 0.4 collective-permute-start.35
  88.0 0.3 collective-permute-done.43.refs_7_
  88.4 1.5 %place.2.refs_8_ = f32[2048,512]{1,0:T(8,128)} custom-call(bf16[2,64,512]{2,1,0:T(8,128)(2,1)S(1)} %pad_maximum_fusion.1.refs_0_, bf16[2,64,512]{2,1,0:T(8,128)(2,1)S(1)} %collective-permute-done.37.refs_1_, bf16[2,64,512]{2,1,0:T(8,128)(2,1)S(1)} %collective-permute-done.38.refs_2_, bf16[2,64,512]{2,1,0:T(8,128)(2,1)S(1)} %collective-permute-done.39.refs_3_, ...), custom_call_target="tpu_custom_call" | custom-call | tf_op jit(solution)/shard_map/place/pallas_call | solution.py:395
  89.9 1.5 %place.3 = f32[2048,512]{1,0:T(8,128)} custom-call(bf16[2,64,512]{2,1,0:T(8,128)(2,1)S(1)} %pad_maximum_fusion.refs_0_, bf16[2,64,512]{2,1,0:T(8,128)(2,1)S(1)} %collective-permute-done.29.refs_1_, bf16[2,64,512]{2,1,0:T(8,128)(2,1)S(1)} %collective-permute-done.30.refs_2_, ...), custom_call_target="tpu_custom_call", output_to_operand_aliasing={{}: (8, {})} | custom-call | tf_op jit(solution)/shard_map/place/pallas_call | solution.py:395
  (47 shorter events, 0.6 us)
Async XLA Ops:
  0.6 26.0 %copy-start = (bf16[1,256,2048]{2,1,0:T(8,128)(2,1)S(1)}, bf16[1,256,2048]{2,1,0:T(8,128)(2,1)}, u32[]{:S(2)}) copy-start(bf16[1,256,2048]{2,1,0:T(8,128)(2,1)} %param.3) | copy-start | bytes 3145732
  3.1 34.0 %copy-start.1 = (s32[1,256]{1,0:T(1,128)S(1)}, s32[1,256]{1,0:T(1,128)}, u32[]{:S(2)}) copy-start(s32[1,256]{1,0:T(1,128)} %refs_0_.1) | copy-start | bytes 3076
  3.1 13.6 %collective-permute-start.1 = (bf16[256,512]{1,0:T(8,128)(2,1)S(1)}, bf16[256,512]{1,0:T(8,128)(2,1)S(1)}, u32[]{:S(2)}, u32[]{:S(2)}) collective-permute-start(bf16[256,512]{1,0:T(8,128)(2,1)S(1)} %get-tuple-element.39.refs_0_.x_ref.refs_7_), channel_id=1, source_target_pairs={{0,8},{2,10},{4,12},{6,14},{8,0},{10,2},{12,4},{14,6},{16,24},{18,... | collective-permute-start | bytes 786440 | tf_op jit(solution)/shard_map/ppermute | solution.py:416
  6.2 10.6 %collective-permute-start.3 = (bf16[256,512]{1,0:T(8,128)(2,1)S(1)}, bf16[256,512]{1,0:T(8,128)(2,1)S(1)}, u32[]{:S(2)}, u32[]{:S(2)}) collective-permute-start(bf16[256,512]{1,0:T(8,128)(2,1)S(1)} %get-tuple-element.39.refs_0_.x_ref.refs_7_), channel_id=1, source_target_pairs={{0,4},{2,6},{4,0},{6,2},{8,12},{10,14},{12,8},{14,10},{16,20},{18,... | collective-permute-start | bytes 786440 | tf_op jit(solution)/shard_map/ppermute | solution.py:416
  7.7 14.0 %collective-permute-start.5 = (bf16[256,512]{1,0:T(8,128)(2,1)S(1)}, bf16[256,512]{1,0:T(8,128)(2,1)S(1)}, u32[]{:S(2)}, u32[]{:S(2)}) collective-permute-start(bf16[256,512]{1,0:T(8,128)(2,1)S(1)} %get-tuple-element.39.refs_0_.x_ref.refs_7_), channel_id=1, source_target_pairs={{0,16},{2,18},{4,20},{6,22},{8,24},{10,26},{12,28},{14,30},{16,0},... | collective-permute-start | bytes 786440 | tf_op jit(solution)/shard_map/ppermute | solution.py:416
  10.3 11.5 %collective-permute-start = (bf16[256,512]{1,0:T(8,128)(2,1)S(1)}, bf16[256,512]{1,0:T(8,128)(2,1)S(1)}, u32[]{:S(2)}, u32[]{:S(2)}) collective-permute-start(bf16[256,512]{1,0:T(8,128)(2,1)S(1)} %get-tuple-element.39.refs_0_.x_ref.refs_7_), channel_id=1, source_target_pairs={{0,2},{2,0},{4,6},{6,4},{8,10},{10,8},{12,14},{14,12},{16,18},{18,... | collective-permute-start | bytes 786440 | tf_op jit(solution)/shard_map/ppermute | solution.py:416
  16.8 5.5 %collective-permute-start.2 = (bf16[256,512]{1,0:T(8,128)(2,1)S(1)}, bf16[256,512]{1,0:T(8,128)(2,1)S(1)}, u32[]{:S(2)}, u32[]{:S(2)}) collective-permute-start(bf16[256,512]{1,0:T(8,128)(2,1)S(1)} %collective-permute-done.1.refs_2_.refs_9_), channel_id=1, source_target_pairs={{0,2},{2,0},{4,6},{6,4},{8,10},{10,8},{12,14},{14,12},{16,18},{18,... | collective-permute-start | bytes 786440 | tf_op jit(solution)/shard_map/ppermute | solution.py:416
  16.8 9.9 %collective-permute-start.7 = (bf16[256,512]{1,0:T(8,128)(2,1)S(1)}, bf16[256,512]{1,0:T(8,128)(2,1)S(1)}, u32[]{:S(2)}, u32[]{:S(2)}) collective-permute-start(bf16[256,512]{1,0:T(8,128)(2,1)S(1)} %collective-permute-done.1.refs_2_.refs_9_), channel_id=1, source_target_pairs={{0,4},{2,6},{4,0},{6,2},{8,12},{10,14},{12,8},{14,10},{16,20},{18,... | collective-permute-start | bytes 786440 | tf_op jit(solution)/shard_map/ppermute | solution.py:416
  19.5 11.0 %collective-permute-start.4 = (bf16[256,512]{1,0:T(8,128)(2,1)S(1)}, bf16[256,512]{1,0:T(8,128)(2,1)S(1)}, u32[]{:S(2)}, u32[]{:S(2)}) collective-permute-start(bf16[256,512]{1,0:T(8,128)(2,1)S(1)} %collective-permute-done.3.refs_4_.refs_11_), channel_id=1, source_target_pairs={{0,2},{2,0},{4,6},{6,4},{8,10},{10,8},{12,14},{14,12},{16,18},{18,... | collective-permute-start | bytes 786440 | tf_op jit(solution)/shard_map/ppermute | solution.py:416
  21.8 9.2 %collective-permute-start.6 = (bf16[256,512]{1,0:T(8,128)(2,1)S(1)}, bf16[256,512]{1,0:T(8,128)(2,1)S(1)}, u32[]{:S(2)}, u32[]{:S(2)}) collective-permute-start(bf16[256,512]{1,0:T(8,128)(2,1)S(1)} %collective-permute-done.5.refs_6_.refs_13_), channel_id=1, source_target_pairs={{0,2},{2,0},{4,6},{6,4},{8,10},{10,8},{12,14},{14,12},{16,18},{18,... | collective-permute-start | bytes 786440 | tf_op jit(solution)/shard_map/ppermute | solution.py:416
  21.8 8.7 %collective-permute-start.10 = (bf16[256,512]{1,0:T(8,128)(2,1)S(1)}, bf16[256,512]{1,0:T(8,128)(2,1)S(1)}, u32[]{:S(2)}, u32[]{:S(2)}) collective-permute-start(bf16[256,512]{1,0:T(8,128)(2,1)S(1)} %collective-permute-done.5.refs_6_.refs_13_), channel_id=1, source_target_pairs={{0,8},{2,10},{4,12},{6,14},{8,0},{10,2},{12,4},{14,6},{16,24},{18,... | collective-permute-start | bytes 786440 | tf_op jit(solution)/shard_map/ppermute | solution.py:416
  22.9 9.5 %collective-permute-start.9 = (bf16[256,512]{1,0:T(8,128)(2,1)S(1)}, bf16[256,512]{1,0:T(8,128)(2,1)S(1)}, u32[]{:S(2)}, u32[]{:S(2)}) collective-permute-start(bf16[256,512]{1,0:T(8,128)(2,1)S(1)} %collective-permute-done.5.refs_6_.refs_13_), channel_id=1, source_target_pairs={{0,4},{2,6},{4,0},{6,2},{8,12},{10,14},{12,8},{14,10},{16,20},{18,... | collective-permute-start | bytes 786440 | tf_op jit(solution)/shard_map/ppermute | solution.py:416
  26.6 19.5 %collective-permute-start.16 = (bf16[256,2048]{1,0:T(8,128)(2,1)S(1)}, bf16[256,2048]{1,0:T(8,128)(2,1)S(1)}, u32[]{:S(2)}, u32[]{:S(2)}) collective-permute-start(bf16[256,2048]{1,0:T(8,128)(2,1)S(1)} %bitcast.7), channel_id=1, source_target_pairs={{0,2},{2,0},{4,6},{6,4},{8,10},{10,8},{12,14},{14,12},{16,18},{18,... | collective-permute-start | bytes 3145736 | tf_op jit(solution)/shard_map/ppermute | solution.py:416
  30.5 3.3 %collective-permute-start.8 = (bf16[256,512]{1,0:T(8,128)(2,1)S(1)}, bf16[256,512]{1,0:T(8,128)(2,1)S(1)}, u32[]{:S(2)}, u32[]{:S(2)}) collective-permute-start(bf16[256,512]{1,0:T(8,128)(2,1)S(1)} %collective-permute-done.7.refs_8_.refs_15_), channel_id=1, source_target_pairs={{0,2},{2,0},{4,6},{6,4},{8,10},{10,8},{12,14},{14,12},{16,18},{18,... | collective-permute-start | bytes 786440 | tf_op jit(solution)/shard_map/ppermute | solution.py:416
  30.5 3.3 %collective-permute-start.12 = (bf16[256,512]{1,0:T(8,128)(2,1)S(1)}, bf16[256,512]{1,0:T(8,128)(2,1)S(1)}, u32[]{:S(2)}, u32[]{:S(2)}) collective-permute-start(bf16[256,512]{1,0:T(8,128)(2,1)S(1)} %collective-permute-done.10.refs_12_.refs_19_), channel_id=1, source_target_pairs={{0,2},{2,0},{4,6},{6,4},{8,10},{10,8},{12,14},{14,12},{16,18},{18,... | collective-permute-start | bytes 786440 | tf_op jit(solution)/shard_map/ppermute | solution.py:416
  32.4 1.6 %collective-permute-start.11 = (bf16[256,512]{1,0:T(8,128)(2,1)S(1)}, bf16[256,512]{1,0:T(8,128)(2,1)S(1)}, u32[]{:S(2)}, u32[]{:S(2)}) collective-permute-start(bf16[256,512]{1,0:T(8,128)(2,1)S(1)} %collective-permute-done.9.refs_10_.refs_17_), channel_id=1, source_target_pairs={{0,2},{2,0},{4,6},{6,4},{8,10},{10,8},{12,14},{14,12},{16,18},{18,... | collective-permute-start | bytes 786440 | tf_op jit(solution)/shard_map/ppermute | solution.py:416
  32.4 8.7 %collective-permute-start.13 = (bf16[256,512]{1,0:T(8,128)(2,1)S(1)}, bf16[256,512]{1,0:T(8,128)(2,1)S(1)}, u32[]{:S(2)}, u32[]{:S(2)}) collective-permute-start(bf16[256,512]{1,0:T(8,128)(2,1)S(1)} %collective-permute-done.10.refs_12_.refs_19_), channel_id=1, source_target_pairs={{0,4},{2,6},{4,0},{6,2},{8,12},{10,14},{12,8},{14,10},{16,20},{18,... | collective-permute-start | bytes 786440 | tf_op jit(solution)/shard_map/ppermute | solution.py:416
  41.2 1.9 %collective-permute-start.14 = (bf16[256,512]{1,0:T(8,128)(2,1)S(1)}, bf16[256,512]{1,0:T(8,128)(2,1)S(1)}, u32[]{:S(2)}, u32[]{:S(2)}) collective-permute-start(bf16[256,512]{1,0:T(8,128)(2,1)S(1)} %collective-permute-done.13.refs_1_.refs_14_.refs_21_), channel_id=1, source_target_pairs={{0,2},{2,0},{4,6},{6,4},{8,10},{10,8},{12,14},{14,12},{16,18},{18,... | collective-permute-start | bytes 786440 | tf_op jit(solution)/shard_map/ppermute | solution.py:416
  42.6 1.4 %collective-permute-start.15 = (f32[16,256]{1,0:T(8,128)S(1)}, f32[16,256]{1,0:T(8,128)S(1)}, u32[]{:S(2)}, u32[]{:S(2)}) collective-permute-start(f32[16,256]{1,0:T(8,128)S(1)} %partial_den.9.refs_2_), channel_id=1, source_target_pairs={{0,2},{2,0},{4,6},{6,4},{8,10},{10,8},{12,14},{14,12},{16,18},{18,... | collective-permute-start | bytes 49160 | tf_op jit(solution)/shard_map/ppermute | solution.py:416
  45.7 1.6 %collective-permute-start.17 = (bf16[256,512]{1,0:T(8,128)(2,1)S(1)}, bf16[256,512]{1,0:T(8,128)(2,1)S(1)}, u32[]{:S(2)}, u32[]{:S(2)}) collective-permute-start(bf16[256,512]{1,0:T(8,128)(2,1)S(1)} %get-tuple-element.58.refs_2_), channel_id=1, source_target_pairs={{0,2},{2,0},{4,6},{6,4},{8,10},{10,8},{12,14},{14,12},{16,18},{18,... | collective-permute-start | bytes 786440 | tf_op jit(solution)/shard_map/ppermute | solution.py:416
  47.8 7.0 %collective-permute-start.18 = (bf16[128,512]{1,0:T(8,128)(2,1)S(1)}, bf16[128,512]{1,0:T(8,128)(2,1)S(1)}, u32[]{:S(2)}, u32[]{:S(2)}) collective-permute-start(bf16[128,512]{1,0:T(8,128)(2,1)S(1)} %get-tuple-element.61), channel_id=1, source_target_pairs={{0,1},{1,0},{2,3},{3,2},{4,5},{5,4},{6,7},{7,6},{8,9},{9,8},{10,11... | collective-permute-start | bytes 393224 | tf_op jit(solution)/shard_map/ppermute | solution.py:416
  49.4 8.3 %collective-permute-start.19 = (bf16[128,512]{1,0:T(8,128)(2,1)S(1)}, bf16[128,512]{1,0:T(8,128)(2,1)S(1)}, u32[]{:S(2)}, u32[]{:S(2)}) collective-permute-start(bf16[128,512]{1,0:T(8,128)(2,1)S(1)} %get-tuple-element.62), channel_id=1, source_target_pairs={{0,4},{2,6},{4,0},{6,2},{8,12},{10,14},{12,8},{14,10},{16,20},{18,... | collective-permute-start | bytes 393224 | tf_op jit(solution)/shard_map/ppermute | solution.py:416
  50.8 7.3 %collective-permute-start.20 = (bf16[128,512]{1,0:T(8,128)(2,1)S(1)}, bf16[128,512]{1,0:T(8,128)(2,1)S(1)}, u32[]{:S(2)}, u32[]{:S(2)}) collective-permute-start(bf16[128,512]{1,0:T(8,128)(2,1)S(1)} %get-tuple-element.63), channel_id=1, source_target_pairs={{0,5},{1,4},{2,7},{3,6},{4,1},{5,0},{6,3},{7,2},{8,13},{9,12},{10,... | collective-permute-start | bytes 393224 | tf_op jit(solution)/shard_map/ppermute | solution.py:437
  51.9 12.8 %collective-permute-start.22 = (bf16[128,512]{1,0:T(8,128)(2,1)S(1)}, bf16[128,512]{1,0:T(8,128)(2,1)S(1)}, u32[]{:S(2)}, u32[]{:S(2)}) collective-permute-start(bf16[128,512]{1,0:T(8,128)(2,1)S(1)} %get-tuple-element.66), channel_id=1, source_target_pairs={{0,1},{1,0},{2,3},{3,2},{4,5},{5,4},{6,7},{7,6},{8,9},{9,8},{10,11... | collective-permute-start | bytes 393224 | tf_op jit(solution)/shard_map/ppermute | solution.py:416
  53.5 11.3 %collective-permute-start.23 = (bf16[128,512]{1,0:T(8,128)(2,1)S(1)}, bf16[128,512]{1,0:T(8,128)(2,1)S(1)}, u32[]{:S(2)}, u32[]{:S(2)}) collective-permute-start(bf16[128,512]{1,0:T(8,128)(2,1)S(1)} %get-tuple-element.67), channel_id=1, source_target_pairs={{0,4},{2,6},{4,0},{6,2},{8,12},{10,14},{12,8},{14,10},{16,20},{18,... | collective-permute-start | bytes 393224 | tf_op jit(solution)/shard_map/ppermute | solution.py:416
  54.8 9.9 %collective-permute-start.24 = (bf16[128,512]{1,0:T(8,128)(2,1)S(1)}, bf16[128,512]{1,0:T(8,128)(2,1)S(1)}, u32[]{:S(2)}, u32[]{:S(2)}) collective-permute-start(bf16[128,512]{1,0:T(8,128)(2,1)S(1)} %get-tuple-element.68), channel_id=1, source_target_pairs={{0,5},{1,4},{2,7},{3,6},{4,1},{5,0},{6,3},{7,2},{8,13},{9,12},{10,... | collective-permute-start | bytes 393224 | tf_op jit(solution)/shard_map/ppermute | solution.py:437
  58.2 6.5 %collective-permute-start.21 = (bf16[64,512]{1,0:T(8,128)(2,1)S(1)}, bf16[64,512]{1,0:T(8,128)(2,1)S(1)}, u32[]{:S(2)}, u32[]{:S(2)}) collective-permute-start(bf16[64,512]{1,0:T(8,128)(2,1)S(1)} %get-tuple-element.64), channel_id=1, source_target_pairs={{0,16},{2,18},{4,20},{6,22},{8,24},{10,26},{12,28},{14,30},{16,0},... | collective-permute-start | bytes 196616 | tf_op jit(solution)/shard_map/ppermute | solution.py:416
  60.7 6.3 %collective-permute-start.25 = (bf16[64,512]{1,0:T(8,128)(2,1)S(1)}, bf16[64,512]{1,0:T(8,128)(2,1)S(1)}, u32[]{:S(2)}, u32[]{:S(2)}) collective-permute-start(bf16[64,512]{1,0:T(8,128)(2,1)S(1)} %get-tuple-element.70), channel_id=1, source_target_pairs={{0,24},{2,26},{4,28},{6,30},{8,16},{10,18},{12,20},{14,22},{16,8},... | collective-permute-start | bytes 196616 | tf_op jit(solution)/shard_map/ppermute | solution.py:416
  64.8 4.3 %collective-permute-start.26 = (bf16[64,512]{1,0:T(8,128)(2,1)S(1)}, bf16[64,512]{1,0:T(8,128)(2,1)S(1)}, u32[]{:S(2)}, u32[]{:S(2)}) collective-permute-start(bf16[64,512]{1,0:T(8,128)(2,1)S(1)} %get-tuple-element.71), channel_id=1, source_target_pairs={{0,8},{2,10},{4,12},{6,14},{8,0},{10,2},{12,4},{14,6},{16,24},{18,... | collective-permute-start | bytes 196616 | tf_op jit(solution)/shard_map/ppermute | solution.py:416
  69.2 4.9 %collective-permute-start.36 = (bf16[64,512]{1,0:T(8,128)(2,1)S(1)}, bf16[64,512]{1,0:T(8,128)(2,1)S(1)}, u32[]{:S(2)}, u32[]{:S(2)}) collective-permute-start(bf16[64,512]{1,0:T(8,128)(2,1)S(1)} %add_convert_fusion), channel_id=1, source_target_pairs={{0,8},{2,10},{4,12},{6,14},{8,0},{10,2},{12,4},{14,6},{16,24},{18,... | collective-permute-start | bytes 196616 | tf_op jit(solution)/shard_map/ppermute | solution.py:416
  69.5 8.3 %collective-permute-start.28 = (bf16[64,512]{1,0:T(8,128)(2,1)S(1)}, bf16[64,512]{1,0:T(8,128)(2,1)S(1)}, u32[]{:S(2)}, u32[]{:S(2)}) collective-permute-start(bf16[64,512]{1,0:T(8,128)(2,1)S(1)} %add_convert_fusion), channel_id=1, source_target_pairs={{0,24},{2,26},{4,28},{6,30},{8,16},{10,18},{12,20},{14,22},{16,8},... | collective-permute-start | bytes 196616 | tf_op jit(solution)/shard_map/ppermute | solution.py:416
  72.0 5.9 %collective-permute-start.27 = (bf16[64,512]{1,0:T(8,128)(2,1)S(1)}, bf16[64,512]{1,0:T(8,128)(2,1)S(1)}, u32[]{:S(2)}, u32[]{:S(2)}) collective-permute-start(bf16[64,512]{1,0:T(8,128)(2,1)S(1)} %add_convert_fusion), channel_id=1, source_target_pairs={{0,16},{2,18},{4,20},{6,22},{8,24},{10,26},{12,28},{14,30},{16,0},... | collective-permute-start | bytes 196616 | tf_op jit(solution)/shard_map/ppermute | solution.py:416
  74.2 7.0 %collective-permute-start.37 = (bf16[2,64,512]{2,1,0:T(8,128)(2,1)S(1)}, bf16[2,64,512]{2,1,0:T(8,128)(2,1)S(1)}, u32[]{:S(2)}, u32[]{:S(2)}) collective-permute-start(bf16[2,64,512]{2,1,0:T(8,128)(2,1)S(1)} %pad_maximum_fusion.1.refs_0_), channel_id=1, source_target_pairs={{0,1},{1,0},{2,3},{3,2},{4,5},{5,4},{6,7},{7,6},{8,9},{9,8},{10,11... | collective-permute-start | bytes 393224 | tf_op jit(solution)/shard_map/ppermute | solution.py:416
  75.9 7.3 %collective-permute-start.38 = (bf16[2,64,512]{2,1,0:T(8,128)(2,1)S(1)}, bf16[2,64,512]{2,1,0:T(8,128)(2,1)S(1)}, u32[]{:S(2)}, u32[]{:S(2)}) collective-permute-start(bf16[2,64,512]{2,1,0:T(8,128)(2,1)S(1)} %pad_maximum_fusion.1.refs_0_), channel_id=1, source_target_pairs={{0,4},{2,6},{4,0},{6,2},{8,12},{10,14},{12,8},{14,10},{16,20},{18,... | collective-permute-start | bytes 393224 | tf_op jit(solution)/shard_map/ppermute | solution.py:416
  76.3 6.1 %collective-permute-start.39 = (bf16[2,64,512]{2,1,0:T(8,128)(2,1)S(1)}, bf16[2,64,512]{2,1,0:T(8,128)(2,1)S(1)}, u32[]{:S(2)}, u32[]{:S(2)}) collective-permute-start(bf16[2,64,512]{2,1,0:T(8,128)(2,1)S(1)} %pad_maximum_fusion.1.refs_0_), channel_id=1, source_target_pairs={{0,5},{1,4},{2,7},{3,6},{4,1},{5,0},{6,3},{7,2},{8,13},{9,12},{10,... | collective-permute-start | bytes 393224 | tf_op jit(solution)/shard_map/ppermute | solution.py:437
  77.9 5.8 %collective-permute-start.29 = (bf16[2,64,512]{2,1,0:T(8,128)(2,1)S(1)}, bf16[2,64,512]{2,1,0:T(8,128)(2,1)S(1)}, u32[]{:S(2)}, u32[]{:S(2)}) collective-permute-start(bf16[2,64,512]{2,1,0:T(8,128)(2,1)S(1)} %pad_maximum_fusion.refs_0_), channel_id=1, source_target_pairs={{0,1},{1,0},{2,3},{3,2},{4,5},{5,4},{6,7},{7,6},{8,9},{9,8},{10,11... | collective-permute-start | bytes 393224 | tf_op jit(solution)/shard_map/ppermute | solution.py:416
  79.9 5.0 %collective-permute-start.30 = (bf16[2,64,512]{2,1,0:T(8,128)(2,1)S(1)}, bf16[2,64,512]{2,1,0:T(8,128)(2,1)S(1)}, u32[]{:S(2)}, u32[]{:S(2)}) collective-permute-start(bf16[2,64,512]{2,1,0:T(8,128)(2,1)S(1)} %pad_maximum_fusion.refs_0_), channel_id=1, source_target_pairs={{0,4},{2,6},{4,0},{6,2},{8,12},{10,14},{12,8},{14,10},{16,20},{18,... | collective-permute-start | bytes 393224 | tf_op jit(solution)/shard_map/ppermute | solution.py:416
  81.1 5.9 %collective-permute-start.31 = (bf16[2,64,512]{2,1,0:T(8,128)(2,1)S(1)}, bf16[2,64,512]{2,1,0:T(8,128)(2,1)S(1)}, u32[]{:S(2)}, u32[]{:S(2)}) collective-permute-start(bf16[2,64,512]{2,1,0:T(8,128)(2,1)S(1)} %pad_maximum_fusion.refs_0_), channel_id=1, source_target_pairs={{0,5},{1,4},{2,7},{3,6},{4,1},{5,0},{6,3},{7,2},{8,13},{9,12},{10,... | collective-permute-start | bytes 393224 | tf_op jit(solution)/shard_map/ppermute | solution.py:437
  82.4 4.6 %collective-permute-start.40 = (bf16[2,64,512]{2,1,0:T(8,128)(2,1)S(1)}, bf16[2,64,512]{2,1,0:T(8,128)(2,1)S(1)}, u32[]{:S(2)}, u32[]{:S(2)}) collective-permute-start(bf16[2,64,512]{2,1,0:T(8,128)(2,1)S(1)} %pad_maximum_fusion.1.refs_0_), channel_id=1, source_target_pairs={{0,2},{2,0},{4,6},{6,4},{8,10},{10,8},{12,14},{14,12},{16,18},{18,... | collective-permute-start | bytes 393224 | tf_op jit(solution)/shard_map/ppermute | solution.py:416
  83.2 4.4 %collective-permute-start.41 = (bf16[2,64,512]{2,1,0:T(8,128)(2,1)S(1)}, bf16[2,64,512]{2,1,0:T(8,128)(2,1)S(1)}, u32[]{:S(2)}, u32[]{:S(2)}) collective-permute-start(bf16[2,64,512]{2,1,0:T(8,128)(2,1)S(1)} %collective-permute-done.37.refs_1_), channel_id=1, source_target_pairs={{0,2},{2,0},{4,6},{6,4},{8,10},{10,8},{12,14},{14,12},{16,18},{18,... | collective-permute-start | bytes 393224 | tf_op jit(solution)/shard_map/ppermute | solution.py:416
  83.7 3.9 %collective-permute-start.42 = (bf16[2,64,512]{2,1,0:T(8,128)(2,1)S(1)}, bf16[2,64,512]{2,1,0:T(8,128)(2,1)S(1)}, u32[]{:S(2)}, u32[]{:S(2)}) collective-permute-start(bf16[2,64,512]{2,1,0:T(8,128)(2,1)S(1)} %collective-permute-done.38.refs_2_), channel_id=1, source_target_pairs={{0,2},{2,0},{4,6},{6,4},{8,10},{10,8},{12,14},{14,12},{16,18},{18,... | collective-permute-start | bytes 393224 | tf_op jit(solution)/shard_map/ppermute | solution.py:416
  84.9 4.9 %collective-permute-start.32 = (bf16[2,64,512]{2,1,0:T(8,128)(2,1)S(1)}, bf16[2,64,512]{2,1,0:T(8,128)(2,1)S(1)}, u32[]{:S(2)}, u32[]{:S(2)}) collective-permute-start(bf16[2,64,512]{2,1,0:T(8,128)(2,1)S(1)} %pad_maximum_fusion.refs_0_), channel_id=1, source_target_pairs={{0,2},{2,0},{4,6},{6,4},{8,10},{10,8},{12,14},{14,12},{16,18},{18,... | collective-permute-start | bytes 393224 | tf_op jit(solution)/shard_map/ppermute | solution.py:416
  87.0 1.3 %collective-permute-start.43 = (bf16[2,64,512]{2,1,0:T(8,128)(2,1)S(1)}, bf16[2,64,512]{2,1,0:T(8,128)(2,1)S(1)}, u32[]{:S(2)}, u32[]{:S(2)}) collective-permute-start(bf16[2,64,512]{2,1,0:T(8,128)(2,1)S(1)} %collective-permute-done.39.refs_3_), channel_id=1, source_target_pairs={{0,2},{2,0},{4,6},{6,4},{8,10},{10,8},{12,14},{14,12},{16,18},{18,... | collective-permute-start | bytes 393224 | tf_op jit(solution)/shard_map/ppermute | solution.py:416
  87.0 2.8 %collective-permute-start.33 = (bf16[2,64,512]{2,1,0:T(8,128)(2,1)S(1)}, bf16[2,64,512]{2,1,0:T(8,128)(2,1)S(1)}, u32[]{:S(2)}, u32[]{:S(2)}) collective-permute-start(bf16[2,64,512]{2,1,0:T(8,128)(2,1)S(1)} %collective-permute-done.29.refs_1_), channel_id=1, source_target_pairs={{0,2},{2,0},{4,6},{6,4},{8,10},{10,8},{12,14},{14,12},{16,18},{18,... | collective-permute-start | bytes 393224 | tf_op jit(solution)/shard_map/ppermute | solution.py:416
  87.5 2.3 %collective-permute-start.34 = (bf16[2,64,512]{2,1,0:T(8,128)(2,1)S(1)}, bf16[2,64,512]{2,1,0:T(8,128)(2,1)S(1)}, u32[]{:S(2)}, u32[]{:S(2)}) collective-permute-start(bf16[2,64,512]{2,1,0:T(8,128)(2,1)S(1)} %collective-permute-done.30.refs_2_), channel_id=1, source_target_pairs={{0,2},{2,0},{4,6},{6,4},{8,10},{10,8},{12,14},{14,12},{16,18},{18,... | collective-permute-start | bytes 393224 | tf_op jit(solution)/shard_map/ppermute | solution.py:416
  87.6 2.3 %collective-permute-start.35 = (bf16[2,64,512]{2,1,0:T(8,128)(2,1)S(1)}, bf16[2,64,512]{2,1,0:T(8,128)(2,1)S(1)}, u32[]{:S(2)}, u32[]{:S(2)}) collective-permute-start(bf16[2,64,512]{2,1,0:T(8,128)(2,1)S(1)} %collective-permute-done.31.refs_3_), channel_id=1, source_target_pairs={{0,2},{2,0},{4,6},{6,4},{8,10},{10,8},{12,14},{14,12},{16,18},{18,... | collective-permute-start | bytes 393224 | tf_op jit(solution)/shard_map/ppermute | solution.py:416

commit v2 on v1

--- a/solution.py
+++ b/solution.py
@@ -465,8 +465,8 @@
         use(pair(near, Z0))
         far_y = blk_swap(gate(far, dens[1]), Y)
         use(pair(over_y, Y), pair(far, 2 * Z0))
-        mid_y = blk_swap(gate(mid, dens[2]), Y)
-        use(pair(near_y, Z0 | Y), pair(far_y, 2 * Z0 | Y, mid), pair(mid, 3 * Z0))
+        mid_y = blk_swap(mid, Y)
+        use(pair(near_y, Z0 | Y), pair(far_y, 2 * Z0 | Y, mid), pair(mid, 3 * Z0, dens[2]))
         (pos,) = take_row(0)
         ending = pair(mid_y, 3 * Z0 | Y, dens[-1], es[-1])
     else:
@@ -516,21 +516,22 @@
     def swapped(some, *after):
         return [(blk_swap(gate(x, *after), CORE), 1, keys) for x, _, keys in some]
 
-    head_total, sets = None, []
+    sets = []
     for at in (0, n_half):
         part = jnp.stack(line[at : at + n_half])
         rs = [dz * Z0 for dz in range(at, at + n_half)]
         sets.append(
             [
-                (part, 0, [(0, r) for r in rs]),
                 (group_swap(part), 0, [(1, r) for r in rs]),
                 (blk_swap(part, Y), 0, [(0, r | Y) for r in rs]),
                 (both_swap(part), 0, [(1, r | Y) for r in rs]),
             ]
         )
-    g = sets[0]
-    head_total = write(g + swapped(g[:1]) + swapped(g[1:3], g[3][0]) + swapped(g[3:]), None)
-    others = swapped(sets[1])
+    own = [(jnp.stack(line), 0, [(0, dz * Z0) for dz in range(planes)])]
+    b1, b2 = sets[0][2][0], sets[1][2][0]
+    others = swapped(sets[0][:2], b1) + swapped(sets[0][2:]) + swapped(own, b1)
+    head_total = write(own + sets[0] + others, None)
+    others = swapped(sets[1][:2]) + swapped(sets[1][2:])
     head_total = write(sets[1] + others, head_total)
     return (pos, lse, grad_z[None, :, :], head_total)
 

time: 91.6 us -> 91.5 us (level)
    ppermute x40 -> x39, waiting for transfers between devices: 31 us -> 30.3 us  [swap(): return lax.ppermute(x, axis, [(i, i ^ mask) for i in range(size)])]
    ppermute x40 -> x39, starting transfers between devices: 33.8 us -> 33.6 us  [swap(): return lax.ppermute(x, axis, [(i, i ^ mask) for i in range(size)])]
  transfers between devices with their start and end apart: 44 -> 43, of which waited for: 21 -> 19; matrix products, arithmetic and copies ran while one was open for 0% -> 0% of each run, Pallas kernels for 15% -> 15%
where the time goes in v2:
time: 91.5 us; the launch traced here: 91.4 us
  starting transfers between devices  38.1 us (42%)
  waiting for transfers between devices  34 us (37%)
  Pallas kernels  18.1 us (20%)
  between operations  0.98 us (1%)
    ppermute x39, starting transfers between devices, swap(): return lax.ppermute(x, axis, [(i, i ^ mask) for i in range(size)])  33.6 us
    ppermute x39, waiting for transfers between devices, swap(): return lax.ppermute(x, axis, [(i, i ^ mask) for i in range(size)])  30.3 us
    pallas_call x5, Pallas kernels, partial_den(): pl.pallas_call(functools.partial(den_kernel, len(old), n_new, before is N...  6.89 us
    ppermute x4, starting transfers between devices, both_swap(): return lax.ppermute(x, ('blk', 'group'), moves)  4.53 us
    ppermute x4, waiting for transfers between devices, both_swap(): return lax.ppermute(x, ('blk', 'group'), moves)  3.73 us
    pallas_call x2, Pallas kernels, place(): pl.pallas_call(functools.partial(place_kernel, plan, planes), in_specs=[V...  2.92 us
    pallas_call x1, Pallas kernels, project(): pl.pallas_call(project_kernel, in_specs=[ANY] * 2, out_specs=[VMEM] * 2,...  2.46 us
    pallas_call x2, Pallas kernels, own_row(): pl.pallas_call(functools.partial(row_kernel, rs, first), in_specs=[VMEM]...  2.06 us
  transfers between devices with their start and end apart: 43, of which 19 were waited for; matrix products, arithmetic and copies ran while one was open for 0% of the time, Pallas kernels for 15%

profile of v2, /device:TPU:0, one launch (start us, length us, event | category | flops | bytes accessed | tf_op | source)
XLA Modules:
  0.0 91.4 jit_solution(659040511036423054)
XLA Ops:
  0.6 2.5 %project.1 = (f32[256,512]{1,0:T(8,128)S(1)}, bf16[256,512]{1,0:T(8,128)(2,1)S(1)}) custom-call(bf16[256,2048]{1,0:T(8,128)(2,1)} %bitcast.6, bf16[2048,512]{1,0:T(8,128)(2,1)} %w_hbm.1), custom_call_target="tpu_custom_call" | custom-call | flops 536870912 | bytes 3145728 | tf_op jit(solution)/shard_map/project/pallas_call | solution.py:61
  3.1 3.1 %collective-permute-start.1 = (bf16[256,512]{1,0:T(8,128)(2,1)S(1)}, bf16[256,512]{1,0:T(8,128)(2,1)S(1)}, u32[]{:S(2)}, u32[]{:S(2)}) collective-permute-start(bf16[256,512]{1,0:T(8,128)(2,1)S(1)} %get-tuple-element.40.refs_0_.x_ref.refs_7_), channel_id=1, source_target_pairs={{0,8},{2,10},{4,12},{6,14},{8,0},{10,2},{12,4},{14,6},{16,24},{18,... | collective-permute-start | bytes 786440 | tf_op jit(solution)/shard_map/ppermute | solution.py:416
  6.2 1.5 %collective-permute-start.3 = (bf16[256,512]{1,0:T(8,128)(2,1)S(1)}, bf16[256,512]{1,0:T(8,128)(2,1)S(1)}, u32[]{:S(2)}, u32[]{:S(2)}) collective-permute-start(bf16[256,512]{1,0:T(8,128)(2,1)S(1)} %get-tuple-element.40.refs_0_.x_ref.refs_7_), channel_id=1, source_target_pairs={{0,4},{2,6},{4,0},{6,2},{8,12},{10,14},{12,8},{14,10},{16,20},{18,... | collective-permute-start | bytes 786440 | tf_op jit(solution)/shard_map/ppermute | solution.py:416
  7.7 2.6 %collective-permute-start.5 = (bf16[256,512]{1,0:T(8,128)(2,1)S(1)}, bf16[256,512]{1,0:T(8,128)(2,1)S(1)}, u32[]{:S(2)}, u32[]{:S(2)}) collective-permute-start(bf16[256,512]{1,0:T(8,128)(2,1)S(1)} %get-tuple-element.40.refs_0_.x_ref.refs_7_), channel_id=1, source_target_pairs={{0,16},{2,18},{4,20},{6,22},{8,24},{10,26},{12,28},{14,30},{16,0},... | collective-permute-start | bytes 786440 | tf_op jit(solution)/shard_map/ppermute | solution.py:416
  10.3 6.4 %collective-permute-done.1.refs_2_.refs_9_ = bf16[256,512]{1,0:T(8,128)(2,1)S(1)} collective-permute-done((bf16[256,512]{1,0:T(8,128)(2,1)S(1)}, bf16[256,512]{1,0:T(8,128)(2,1)S(1)}, u32[]{:S(2)}, u32[]{:S(2)}) %collective-permute-start.1) | collective-permute-done | bytes 262176 | tf_op jit(solution)/shard_map/ppermute | solution.py:416
  16.8 2.7 %collective-permute-start.7 = (bf16[256,512]{1,0:T(8,128)(2,1)S(1)}, bf16[256,512]{1,0:T(8,128)(2,1)S(1)}, u32[]{:S(2)}, u32[]{:S(2)}) collective-permute-start(bf16[256,512]{1,0:T(8,128)(2,1)S(1)} %collective-permute-done.1.refs_2_.refs_9_), channel_id=1, source_target_pairs={{0,4},{2,6},{4,0},{6,2},{8,12},{10,14},{12,8},{14,10},{16,20},{18,... | collective-permute-start | bytes 786440 | tf_op jit(solution)/shard_map/ppermute | solution.py:416
  19.5 0.2 collective-permute-start.4
  19.7 2.1 %collective-permute-done.5.refs_6_.refs_13_ = bf16[256,512]{1,0:T(8,128)(2,1)S(1)} collective-permute-done((bf16[256,512]{1,0:T(8,128)(2,1)S(1)}, bf16[256,512]{1,0:T(8,128)(2,1)S(1)}, u32[]{:S(2)}, u32[]{:S(2)}) %collective-permute-start.5) | collective-permute-done | bytes 262176 | tf_op jit(solution)/shard_map/ppermute | solution.py:416
  21.8 0.5 partial_den.5.refs_4_
  22.3 0.6 partial_den.6.refs_8_
  22.9 0.7 collective-permute-start.9
  23.6 3.0 %collective-permute-done.7.refs_8_.refs_15_ = bf16[256,512]{1,0:T(8,128)(2,1)S(1)} collective-permute-done((bf16[256,512]{1,0:T(8,128)(2,1)S(1)}, bf16[256,512]{1,0:T(8,128)(2,1)S(1)}, u32[]{:S(2)}, u32[]{:S(2)}) %collective-permute-start.7) | collective-permute-done | bytes 262176 | tf_op jit(solution)/shard_map/ppermute | solution.py:416
  26.7 0.5 collective-permute-start.8
  27.2 1.3 %partial_den.7.refs_14_ = f32[16,256]{1,0:T(8,128)S(1)} custom-call(bf16[256,512]{1,0:T(8,128)(2,1)S(1)} %get-tuple-element.40.refs_0_.x_ref.refs_7_, bf16[256,512]{1,0:T(8,128)(2,1)S(1)} %collective-permute-done.refs_1_.refs_8_, bf16[256,512]{1,0:T(8,128)(2,1)S(1)} %collective-permute-done.1.refs_2_.refs_9_, ...), custom_call_target="tpu_custom_call" | custom-call | tf_op jit(solution)/shard_map/partial_den/pallas_call | solution.py:142
  28.5 2.0 %collective-permute-done.10.refs_12_.refs_19_ = bf16[256,512]{1,0:T(8,128)(2,1)S(1)} collective-permute-done((bf16[256,512]{1,0:T(8,128)(2,1)S(1)}, bf16[256,512]{1,0:T(8,128)(2,1)S(1)}, u32[]{:S(2)}, u32[]{:S(2)}) %collective-permute-start.10) | collective-permute-done | bytes 262176 | tf_op jit(solution)/shard_map/ppermute | solution.py:416
  30.5 1.6 %collective-permute-done.9.refs_10_.refs_17_ = bf16[256,512]{1,0:T(8,128)(2,1)S(1)} collective-permute-done((bf16[256,512]{1,0:T(8,128)(2,1)S(1)}, bf16[256,512]{1,0:T(8,128)(2,1)S(1)}, u32[]{:S(2)}, u32[]{:S(2)}) %collective-permute-start.9) | collective-permute-done | bytes 262176 | tf_op jit(solution)/shard_map/ppermute | solution.py:416
  32.1 1.7 %collective-permute-start.13 = (bf16[256,512]{1,0:T(8,128)(2,1)S(1)}, bf16[256,512]{1,0:T(8,128)(2,1)S(1)}, u32[]{:S(2)}, u32[]{:S(2)}) collective-permute-start(bf16[256,512]{1,0:T(8,128)(2,1)S(1)} %collective-permute-done.10.refs_12_.refs_19_), channel_id=1, source_target_pairs={{0,4},{2,6},{4,0},{6,2},{8,12},{10,14},{12,8},{14,10},{16,20},{18,... | collective-permute-start | bytes 786440 | tf_op jit(solution)/shard_map/ppermute | solution.py:416
  33.8 3.1 %partial_den.8.refs_15_ = f32[16,256]{1,0:T(8,128)S(1)} custom-call(bf16[256,512]{1,0:T(8,128)(2,1)S(1)} %get-tuple-element.40.refs_0_.x_ref.refs_7_, bf16[256,512]{1,0:T(8,128)(2,1)S(1)} %collective-permute-done.refs_1_.refs_8_, bf16[256,512]{1,0:T(8,128)(2,1)S(1)} %collective-permute-done.1.refs_2_.refs_9_, ...), custom_call_target="tpu_custom_call" | custom-call | tf_op jit(solution)/shard_map/partial_den/pallas_call | solution.py:142
  37.0 1.5 %own_row.2 = (f32[256,3584]{1,0:T(8,128)S(1)}, f32[1,256]{1,0:T(1,128)S(1)}) custom-call(s32[1,256]{1,0:T(1,128)S(1)} %copy-done.1, bf16[256,512]{1,0:T(8,128)(2,1)S(1)} %get-tuple-element.40.refs_0_.x_ref.refs_7_, bf16[256,512]{1,0:T(8,128)(2,1)S(1)} %get-tuple-element.40.refs_0_.x_ref.refs_7_, bf16[256,512]{1,0:T(8,128)(2,1)S(1)} %collective-permute-done.refs_1_.refs_8_, ...), custom_call_target="tpu_custom_call" | custom-call | tf_op jit(solution)/shard_map/own_row/pallas_call | solution.py:208
  38.5 2.3 %collective-permute-done.13.refs_1_.refs_14_.refs_21_ = bf16[256,512]{1,0:T(8,128)(2,1)S(1)} collective-permute-done((bf16[256,512]{1,0:T(8,128)(2,1)S(1)}, bf16[256,512]{1,0:T(8,128)(2,1)S(1)}, u32[]{:S(2)}, u32[]{:S(2)}) %collective-permute-start.13) | collective-permute-done | bytes 262176 | tf_op jit(solution)/shard_map/ppermute | solution.py:416
  40.8 1.4 %partial_den.9.refs_2_ = f32[16,256]{1,0:T(8,128)S(1)} custom-call(bf16[256,512]{1,0:T(8,128)(2,1)S(1)} %get-tuple-element.40.refs_0_.x_ref.refs_7_, bf16[256,512]{1,0:T(8,128)(2,1)S(1)} %collective-permute-done.refs_1_.refs_8_, bf16[256,512]{1,0:T(8,128)(2,1)S(1)} %collective-permute-done.1.refs_2_.refs_9_, ...), custom_call_target="tpu_custom_call" | custom-call | tf_op jit(solution)/shard_map/partial_den/pallas_call | solution.py:142
  42.2 0.5 collective-permute-start.15
  42.7 0.5 own_row.3
  43.3 0.3 collective-permute-done.15.refs_3_
  43.6 1.8 %gradient.1 = (f32[1,256]{1,0:T(1,128)S(1)}, f32[256,512]{1,0:T(8,128)S(1)}, bf16[256,512]{1,0:T(8,128)(2,1)S(1)}) custom-call(s32[1,256]{1,0:T(1,128)S(1)} %copy-done.1, f32[256,512]{1,0:T(8,128)S(1)} %get-tuple-element.49.refs_1_, f32[16,256]{1,0:T(8,128)S(1)} %partial_den.9.refs_2_, f32[16,256]{1,0:T(8,128)S(1)} %collective-permute-done.15.refs_3_, ...), custom_call_target="tpu_custom_call" | custom-call | flops 1073741824 | bytes 12582912 | tf_op jit(solution)/shard_map/gradient/pallas_call | solution.py:268
  45.3 0.4 collective-permute-start.17
  45.8 1.2 %collective-permute-done.17.refs_3_ = bf16[256,512]{1,0:T(8,128)(2,1)S(1)} collective-permute-done((bf16[256,512]{1,0:T(8,128)(2,1)S(1)}, bf16[256,512]{1,0:T(8,128)(2,1)S(1)}, u32[]{:S(2)}, u32[]{:S(2)}) %collective-permute-start.17) | collective-permute-done | bytes 262176 | tf_op jit(solution)/shard_map/ppermute | solution.py:416
  46.9 0.5 head_partial.2
  47.5 1.6 %collective-permute-start.18 = (bf16[128,512]{1,0:T(8,128)(2,1)S(1)}, bf16[128,512]{1,0:T(8,128)(2,1)S(1)}, u32[]{:S(2)}, u32[]{:S(2)}) collective-permute-start(bf16[128,512]{1,0:T(8,128)(2,1)S(1)} %get-tuple-element.62), channel_id=1, source_target_pairs={{0,1},{1,0},{2,3},{3,2},{4,5},{5,4},{6,7},{7,6},{8,9},{9,8},{10,11... | collective-permute-start | bytes 393224 | tf_op jit(solution)/shard_map/ppermute | solution.py:416
  49.0 1.7 %collective-permute-start.19 = (bf16[128,512]{1,0:T(8,128)(2,1)S(1)}, bf16[128,512]{1,0:T(8,128)(2,1)S(1)}, u32[]{:S(2)}, u32[]{:S(2)}) collective-permute-start(bf16[128,512]{1,0:T(8,128)(2,1)S(1)} %get-tuple-element.63), channel_id=1, source_target_pairs={{0,4},{2,6},{4,0},{6,2},{8,12},{10,14},{12,8},{14,10},{16,20},{18,... | collective-permute-start | bytes 393224 | tf_op jit(solution)/shard_map/ppermute | solution.py:416
  50.8 0.2 collective-permute-start.20
  51.0 0.5 head_partial.3
  51.5 1.6 %collective-permute-start.22 = (bf16[128,512]{1,0:T(8,128)(2,1)S(1)}, bf16[128,512]{1,0:T(8,128)(2,1)S(1)}, u32[]{:S(2)}, u32[]{:S(2)}) collective-permute-start(bf16[128,512]{1,0:T(8,128)(2,1)S(1)} %get-tuple-element.67), channel_id=1, source_target_pairs={{0,1},{1,0},{2,3},{3,2},{4,5},{5,4},{6,7},{7,6},{8,9},{9,8},{10,11... | collective-permute-start | bytes 393224 | tf_op jit(solution)/shard_map/ppermute | solution.py:416
  53.1 1.7 %collective-permute-start.23 = (bf16[128,512]{1,0:T(8,128)(2,1)S(1)}, bf16[128,512]{1,0:T(8,128)(2,1)S(1)}, u32[]{:S(2)}, u32[]{:S(2)}) collective-permute-start(bf16[128,512]{1,0:T(8,128)(2,1)S(1)} %get-tuple-element.68), channel_id=1, source_target_pairs={{0,4},{2,6},{4,0},{6,2},{8,12},{10,14},{12,8},{14,10},{16,20},{18,... | collective-permute-start | bytes 393224 | tf_op jit(solution)/shard_map/ppermute | solution.py:416
  54.8 1.7 %collective-permute-start.24 = (bf16[128,512]{1,0:T(8,128)(2,1)S(1)}, bf16[128,512]{1,0:T(8,128)(2,1)S(1)}, u32[]{:S(2)}, u32[]{:S(2)}) collective-permute-start(bf16[128,512]{1,0:T(8,128)(2,1)S(1)} %get-tuple-element.69), channel_id=1, source_target_pairs={{0,5},{1,4},{2,7},{3,6},{4,1},{5,0},{6,3},{7,2},{8,13},{9,12},{10,... | collective-permute-start | bytes 393224 | tf_op jit(solution)/shard_map/ppermute | solution.py:437
  56.5 0.8 hand_out.1
  57.4 0.8 collective-permute-done.20.from_both
  58.1 0.1 deal.2
  58.2 2.5 %collective-permute-start.21 = (bf16[64,512]{1,0:T(8,128)(2,1)S(1)}, bf16[64,512]{1,0:T(8,128)(2,1)S(1)}, u32[]{:S(2)}, u32[]{:S(2)}) collective-permute-start(bf16[64,512]{1,0:T(8,128)(2,1)S(1)} %get-tuple-element.65), channel_id=1, source_target_pairs={{0,16},{2,18},{4,20},{6,22},{8,24},{10,26},{12,28},{14,30},{16,0},... | collective-permute-start | bytes 196616 | tf_op jit(solution)/shard_map/ppermute | solution.py:416
  60.7 1.4 %collective-permute-start.25 = (bf16[64,512]{1,0:T(8,128)(2,1)S(1)}, bf16[64,512]{1,0:T(8,128)(2,1)S(1)}, u32[]{:S(2)}, u32[]{:S(2)}) collective-permute-start(bf16[64,512]{1,0:T(8,128)(2,1)S(1)} %get-tuple-element.71), channel_id=1, source_target_pairs={{0,24},{2,26},{4,28},{6,30},{8,16},{10,18},{12,20},{14,22},{16,8},... | collective-permute-start | bytes 196616 | tf_op jit(solution)/shard_map/ppermute | solution.py:416
  62.1 2.6 %collective-permute-done.21 = bf16[64,512]{1,0:T(8,128)(2,1)S(1)} collective-permute-done((bf16[64,512]{1,0:T(8,128)(2,1)S(1)}, bf16[64,512]{1,0:T(8,128)(2,1)S(1)}, u32[]{:S(2)}, u32[]{:S(2)}) %collective-permute-start.21) | collective-permute-done | bytes 65568 | tf_op jit(solution)/shard_map/ppermute | solution.py:416
  64.7 0.1 deal.3
  64.8 0.3 collective-permute-start.26
  65.1 2.0 %collective-permute-done.25 = bf16[64,512]{1,0:T(8,128)(2,1)S(1)} collective-permute-done((bf16[64,512]{1,0:T(8,128)(2,1)S(1)}, bf16[64,512]{1,0:T(8,128)(2,1)S(1)}, u32[]{:S(2)}, u32[]{:S(2)}) %collective-permute-start.25) | collective-permute-done | bytes 65568 | tf_op jit(solution)/shard_map/ppermute | solution.py:416
  67.1 2.6 %collective-permute-done.26 = bf16[64,512]{1,0:T(8,128)(2,1)S(1)} collective-permute-done((bf16[64,512]{1,0:T(8,128)(2,1)S(1)}, bf16[64,512]{1,0:T(8,128)(2,1)S(1)}, u32[]{:S(2)}, u32[]{:S(2)}) %collective-permute-start.26) | collective-permute-done | bytes 65568 | tf_op jit(solution)/shard_map/ppermute | solution.py:416
  69.7 0.1 collective-permute-start.35
  69.8 2.2 %collective-permute-start.28 = (bf16[64,512]{1,0:T(8,128)(2,1)S(1)}, bf16[64,512]{1,0:T(8,128)(2,1)S(1)}, u32[]{:S(2)}, u32[]{:S(2)}) collective-permute-start(bf16[64,512]{1,0:T(8,128)(2,1)S(1)} %add_convert_fusion), channel_id=1, source_target_pairs={{0,24},{2,26},{4,28},{6,30},{8,16},{10,18},{12,20},{14,22},{16,8},... | collective-permute-start | bytes 196616 | tf_op jit(solution)/shard_map/ppermute | solution.py:416
  72.0 1.2 %collective-permute-start.27 = (bf16[64,512]{1,0:T(8,128)(2,1)S(1)}, bf16[64,512]{1,0:T(8,128)(2,1)S(1)}, u32[]{:S(2)}, u32[]{:S(2)}) collective-permute-start(bf16[64,512]{1,0:T(8,128)(2,1)S(1)} %add_convert_fusion), channel_id=1, source_target_pairs={{0,16},{2,18},{4,20},{6,22},{8,24},{10,26},{12,28},{14,30},{16,0},... | collective-permute-start | bytes 196616 | tf_op jit(solution)/shard_map/ppermute | solution.py:416
  73.2 1.2 %collective-permute-done.35 = bf16[64,512]{1,0:T(8,128)(2,1)S(1)} collective-permute-done((bf16[64,512]{1,0:T(8,128)(2,1)S(1)}, bf16[64,512]{1,0:T(8,128)(2,1)S(1)}, u32[]{:S(2)}, u32[]{:S(2)}) %collective-permute-start.35) | collective-permute-done | bytes 65568 | tf_op jit(solution)/shard_map/ppermute | solution.py:416
  74.5 1.4 %collective-permute-start.36 = (bf16[2,64,512]{2,1,0:T(8,128)(2,1)S(1)}, bf16[2,64,512]{2,1,0:T(8,128)(2,1)S(1)}, u32[]{:S(2)}, u32[]{:S(2)}) collective-permute-start(bf16[2,64,512]{2,1,0:T(8,128)(2,1)S(1)} %pad_maximum_fusion.2), channel_id=1, source_target_pairs={{0,1},{1,0},{2,3},{3,2},{4,5},{5,4},{6,7},{7,6},{8,9},{9,8},{10,11... | collective-permute-start | bytes 393224 | tf_op jit(solution)/shard_map/ppermute | solution.py:416
  75.9 0.4 collective-permute-start.37
  76.3 1.8 %collective-permute-start.38 = (bf16[2,64,512]{2,1,0:T(8,128)(2,1)S(1)}, bf16[2,64,512]{2,1,0:T(8,128)(2,1)S(1)}, u32[]{:S(2)}, u32[]{:S(2)}) collective-permute-start(bf16[2,64,512]{2,1,0:T(8,128)(2,1)S(1)} %pad_maximum_fusion.2), channel_id=1, source_target_pairs={{0,5},{1,4},{2,7},{3,6},{4,1},{5,0},{6,3},{7,2},{8,13},{9,12},{10,... | collective-permute-start | bytes 393224 | tf_op jit(solution)/shard_map/ppermute | solution.py:437
  78.1 1.9 %collective-permute-start.29 = (bf16[2,64,512]{2,1,0:T(8,128)(2,1)S(1)}, bf16[2,64,512]{2,1,0:T(8,128)(2,1)S(1)}, u32[]{:S(2)}, u32[]{:S(2)}) collective-permute-start(bf16[2,64,512]{2,1,0:T(8,128)(2,1)S(1)} %pad_maximum_fusion.1), channel_id=1, source_target_pairs={{0,1},{1,0},{2,3},{3,2},{4,5},{5,4},{6,7},{7,6},{8,9},{9,8},{10,11... | collective-permute-start | bytes 393224 | tf_op jit(solution)/shard_map/ppermute | solution.py:416
  79.9 1.0 %collective-permute-start.30 = (bf16[2,64,512]{2,1,0:T(8,128)(2,1)S(1)}, bf16[2,64,512]{2,1,0:T(8,128)(2,1)S(1)}, u32[]{:S(2)}, u32[]{:S(2)}) collective-permute-start(bf16[2,64,512]{2,1,0:T(8,128)(2,1)S(1)} %pad_maximum_fusion.1), channel_id=1, source_target_pairs={{0,4},{2,6},{4,0},{6,2},{8,12},{10,14},{12,8},{14,10},{16,20},{18,... | collective-permute-start | bytes 393224 | tf_op jit(solution)/shard_map/ppermute | solution.py:416
  81.0 0.8 collective-permute-start.31
  81.8 1.0 %collective-permute-done.38.refs_3_ = bf16[2,64,512]{2,1,0:T(8,128)(2,1)S(1)} collective-permute-done((bf16[2,64,512]{2,1,0:T(8,128)(2,1)S(1)}, bf16[2,64,512]{2,1,0:T(8,128)(2,1)S(1)}, u32[]{:S(2)}, u32[]{:S(2)}) %collective-permute-start.38) | collective-permute-done | bytes 131104 | tf_op jit(solution)/shard_map/ppermute | solution.py:437
  82.8 0.6 collective-permute-done.37.refs_2_
  83.3 0.5 collective-permute-done.29.refs_0_
  83.8 1.1 %collective-permute-done.30.refs_1_ = bf16[2,64,512]{2,1,0:T(8,128)(2,1)S(1)} collective-permute-done((bf16[2,64,512]{2,1,0:T(8,128)(2,1)S(1)}, bf16[2,64,512]{2,1,0:T(8,128)(2,1)S(1)}, u32[]{:S(2)}, u32[]{:S(2)}) %collective-permute-start.30) | collective-permute-done | bytes 131104 | tf_op jit(solution)/shard_map/ppermute | solution.py:416
  84.9 2.0 %collective-permute-done.31.refs_2_ = bf16[2,64,512]{2,1,0:T(8,128)(2,1)S(1)} collective-permute-done((bf16[2,64,512]{2,1,0:T(8,128)(2,1)S(1)}, bf16[2,64,512]{2,1,0:T(8,128)(2,1)S(1)}, u32[]{:S(2)}, u32[]{:S(2)}) %collective-permute-start.31) | collective-permute-done | bytes 131104 | tf_op jit(solution)/shard_map/ppermute | solution.py:437
  86.9 0.5 collective-permute-start.33
  87.5 0.8 collective-permute-done.41.refs_6_
  88.2 1.7 %place.2.refs_6_ = f32[2048,512]{1,0:T(8,128)} custom-call(bf16[4,64,512]{2,1,0:T(8,128)(2,1)S(1)} %pad_maximum_fusion.refs_0_, bf16[2,64,512]{2,1,0:T(8,128)(2,1)S(1)} %collective-permute-done.36.refs_1_, bf16[2,64,512]{2,1,0:T(8,128)(2,1)S(1)} %collective-permute-done.37.refs_2_, bf16[2,64,512]{2,1,0:T(8,128)(2,1)S(1)} %collective-permute-done.38.refs_3_, ...), custom_call_target="tpu_custom_call" | custom-call | tf_op jit(solution)/shard_map/place/pallas_call | solution.py:395
  89.9 1.3 %place.3 = f32[2048,512]{1,0:T(8,128)} custom-call(bf16[2,64,512]{2,1,0:T(8,128)(2,1)S(1)} %collective-permute-done.29.refs_0_, bf16[2,64,512]{2,1,0:T(8,128)(2,1)S(1)} %collective-permute-done.30.refs_1_, bf16[2,64,512]{2,1,0:T(8,128)(2,1)S(1)} %collective-permute-done.31.refs_2_, ...), custom_call_target="tpu_custom_call", output_to_operand_aliasing={{}: (6, {})} | custom-call | tf_op jit(solution)/shard_map/place/pallas_call | solution.py:395
  (46 shorter events, 0.3 us)
Async XLA Ops:
  0.6 26.0 %copy-start = (bf16[1,256,2048]{2,1,0:T(8,128)(2,1)S(1)}, bf16[1,256,2048]{2,1,0:T(8,128)(2,1)}, u32[]{:S(2)}) copy-start(bf16[1,256,2048]{2,1,0:T(8,128)(2,1)} %param.3) | copy-start | bytes 3145732
  3.1 33.9 %copy-start.1 = (s32[1,256]{1,0:T(1,128)S(1)}, s32[1,256]{1,0:T(1,128)}, u32[]{:S(2)}) copy-start(s32[1,256]{1,0:T(1,128)} %refs_0_.1) | copy-start | bytes 3076
  3.1 13.6 %collective-permute-start.1 = (bf16[256,512]{1,0:T(8,128)(2,1)S(1)}, bf16[256,512]{1,0:T(8,128)(2,1)S(1)}, u32[]{:S(2)}, u32[]{:S(2)}) collective-permute-start(bf16[256,512]{1,0:T(8,128)(2,1)S(1)} %get-tuple-element.40.refs_0_.x_ref.refs_7_), channel_id=1, source_target_pairs={{0,8},{2,10},{4,12},{6,14},{8,0},{10,2},{12,4},{14,6},{16,24},{18,... | collective-permute-start | bytes 786440 | tf_op jit(solution)/shard_map/ppermute | solution.py:416
  6.2 10.6 %collective-permute-start.3 = (bf16[256,512]{1,0:T(8,128)(2,1)S(1)}, bf16[256,512]{1,0:T(8,128)(2,1)S(1)}, u32[]{:S(2)}, u32[]{:S(2)}) collective-permute-start(bf16[256,512]{1,0:T(8,128)(2,1)S(1)} %get-tuple-element.40.refs_0_.x_ref.refs_7_), channel_id=1, source_target_pairs={{0,4},{2,6},{4,0},{6,2},{8,12},{10,14},{12,8},{14,10},{16,20},{18,... | collective-permute-start | bytes 786440 | tf_op jit(solution)/shard_map/ppermute | solution.py:416
  7.7 14.0 %collective-permute-start.5 = (bf16[256,512]{1,0:T(8,128)(2,1)S(1)}, bf16[256,512]{1,0:T(8,128)(2,1)S(1)}, u32[]{:S(2)}, u32[]{:S(2)}) collective-permute-start(bf16[256,512]{1,0:T(8,128)(2,1)S(1)} %get-tuple-element.40.refs_0_.x_ref.refs_7_), channel_id=1, source_target_pairs={{0,16},{2,18},{4,20},{6,22},{8,24},{10,26},{12,28},{14,30},{16,0},... | collective-permute-start | bytes 786440 | tf_op jit(solution)/shard_map/ppermute | solution.py:416
  10.3 11.5 %collective-permute-start = (bf16[256,512]{1,0:T(8,128)(2,1)S(1)}, bf16[256,512]{1,0:T(8,128)(2,1)S(1)}, u32[]{:S(2)}, u32[]{:S(2)}) collective-permute-start(bf16[256,512]{1,0:T(8,128)(2,1)S(1)} %get-tuple-element.40.refs_0_.x_ref.refs_7_), channel_id=1, source_target_pairs={{0,2},{2,0},{4,6},{6,4},{8,10},{10,8},{12,14},{14,12},{16,18},{18,... | collective-permute-start | bytes 786440 | tf_op jit(solution)/shard_map/ppermute | solution.py:416
  16.8 5.5 %collective-permute-start.2 = (bf16[256,512]{1,0:T(8,128)(2,1)S(1)}, bf16[256,512]{1,0:T(8,128)(2,1)S(1)}, u32[]{:S(2)}, u32[]{:S(2)}) collective-permute-start(bf16[256,512]{1,0:T(8,128)(2,1)S(1)} %collective-permute-done.1.refs_2_.refs_9_), channel_id=1, source_target_pairs={{0,2},{2,0},{4,6},{6,4},{8,10},{10,8},{12,14},{14,12},{16,18},{18,... | collective-permute-start | bytes 786440 | tf_op jit(solution)/shard_map/ppermute | solution.py:416
  16.8 9.9 %collective-permute-start.7 = (bf16[256,512]{1,0:T(8,128)(2,1)S(1)}, bf16[256,512]{1,0:T(8,128)(2,1)S(1)}, u32[]{:S(2)}, u32[]{:S(2)}) collective-permute-start(bf16[256,512]{1,0:T(8,128)(2,1)S(1)} %collective-permute-done.1.refs_2_.refs_9_), channel_id=1, source_target_pairs={{0,4},{2,6},{4,0},{6,2},{8,12},{10,14},{12,8},{14,10},{16,20},{18,... | collective-permute-start | bytes 786440 | tf_op jit(solution)/shard_map/ppermute | solution.py:416
  19.5 7.2 %collective-permute-start.4 = (bf16[256,512]{1,0:T(8,128)(2,1)S(1)}, bf16[256,512]{1,0:T(8,128)(2,1)S(1)}, u32[]{:S(2)}, u32[]{:S(2)}) collective-permute-start(bf16[256,512]{1,0:T(8,128)(2,1)S(1)} %collective-permute-done.3.refs_4_.refs_11_), channel_id=1, source_target_pairs={{0,2},{2,0},{4,6},{6,4},{8,10},{10,8},{12,14},{14,12},{16,18},{18,... | collective-permute-start | bytes 786440 | tf_op jit(solution)/shard_map/ppermute | solution.py:416
  21.8 5.4 %collective-permute-start.6 = (bf16[256,512]{1,0:T(8,128)(2,1)S(1)}, bf16[256,512]{1,0:T(8,128)(2,1)S(1)}, u32[]{:S(2)}, u32[]{:S(2)}) collective-permute-start(bf16[256,512]{1,0:T(8,128)(2,1)S(1)} %collective-permute-done.5.refs_6_.refs_13_), channel_id=1, source_target_pairs={{0,2},{2,0},{4,6},{6,4},{8,10},{10,8},{12,14},{14,12},{16,18},{18,... | collective-permute-start | bytes 786440 | tf_op jit(solution)/shard_map/ppermute | solution.py:416
  21.8 8.7 %collective-permute-start.10 = (bf16[256,512]{1,0:T(8,128)(2,1)S(1)}, bf16[256,512]{1,0:T(8,128)(2,1)S(1)}, u32[]{:S(2)}, u32[]{:S(2)}) collective-permute-start(bf16[256,512]{1,0:T(8,128)(2,1)S(1)} %collective-permute-done.5.refs_6_.refs_13_), channel_id=1, source_target_pairs={{0,8},{2,10},{4,12},{6,14},{8,0},{10,2},{12,4},{14,6},{16,24},{18,... | collective-permute-start | bytes 786440 | tf_op jit(solution)/shard_map/ppermute | solution.py:416
  22.9 9.2 %collective-permute-start.9 = (bf16[256,512]{1,0:T(8,128)(2,1)S(1)}, bf16[256,512]{1,0:T(8,128)(2,1)S(1)}, u32[]{:S(2)}, u32[]{:S(2)}) collective-permute-start(bf16[256,512]{1,0:T(8,128)(2,1)S(1)} %collective-permute-done.5.refs_6_.refs_13_), channel_id=1, source_target_pairs={{0,4},{2,6},{4,0},{6,2},{8,12},{10,14},{12,8},{14,10},{16,20},{18,... | collective-permute-start | bytes 786440 | tf_op jit(solution)/shard_map/ppermute | solution.py:416
  26.6 19.1 %collective-permute-start.16 = (bf16[256,2048]{1,0:T(8,128)(2,1)S(1)}, bf16[256,2048]{1,0:T(8,128)(2,1)S(1)}, u32[]{:S(2)}, u32[]{:S(2)}) collective-permute-start(bf16[256,2048]{1,0:T(8,128)(2,1)S(1)} %bitcast.7), channel_id=1, source_target_pairs={{0,2},{2,0},{4,6},{6,4},{8,10},{10,8},{12,14},{14,12},{16,18},{18,... | collective-permute-start | bytes 3145736 | tf_op jit(solution)/shard_map/ppermute | solution.py:416
  26.7 7.2 %collective-permute-start.8 = (bf16[256,512]{1,0:T(8,128)(2,1)S(1)}, bf16[256,512]{1,0:T(8,128)(2,1)S(1)}, u32[]{:S(2)}, u32[]{:S(2)}) collective-permute-start(bf16[256,512]{1,0:T(8,128)(2,1)S(1)} %collective-permute-done.7.refs_8_.refs_15_), channel_id=1, source_target_pairs={{0,2},{2,0},{4,6},{6,4},{8,10},{10,8},{12,14},{14,12},{16,18},{18,... | collective-permute-start | bytes 786440 | tf_op jit(solution)/shard_map/ppermute | solution.py:416
  30.5 3.3 %collective-permute-start.12 = (bf16[256,512]{1,0:T(8,128)(2,1)S(1)}, bf16[256,512]{1,0:T(8,128)(2,1)S(1)}, u32[]{:S(2)}, u32[]{:S(2)}) collective-permute-start(bf16[256,512]{1,0:T(8,128)(2,1)S(1)} %collective-permute-done.10.refs_12_.refs_19_), channel_id=1, source_target_pairs={{0,2},{2,0},{4,6},{6,4},{8,10},{10,8},{12,14},{14,12},{16,18},{18,... | collective-permute-start | bytes 786440 | tf_op jit(solution)/shard_map/ppermute | solution.py:416
  32.1 1.8 %collective-permute-start.11 = (bf16[256,512]{1,0:T(8,128)(2,1)S(1)}, bf16[256,512]{1,0:T(8,128)(2,1)S(1)}, u32[]{:S(2)}, u32[]{:S(2)}) collective-permute-start(bf16[256,512]{1,0:T(8,128)(2,1)S(1)} %collective-permute-done.9.refs_10_.refs_17_), channel_id=1, source_target_pairs={{0,2},{2,0},{4,6},{6,4},{8,10},{10,8},{12,14},{14,12},{16,18},{18,... | collective-permute-start | bytes 786440 | tf_op jit(solution)/shard_map/ppermute | solution.py:416
  32.1 8.7 %collective-permute-start.13 = (bf16[256,512]{1,0:T(8,128)(2,1)S(1)}, bf16[256,512]{1,0:T(8,128)(2,1)S(1)}, u32[]{:S(2)}, u32[]{:S(2)}) collective-permute-start(bf16[256,512]{1,0:T(8,128)(2,1)S(1)} %collective-permute-done.10.refs_12_.refs_19_), channel_id=1, source_target_pairs={{0,4},{2,6},{4,0},{6,2},{8,12},{10,14},{12,8},{14,10},{16,20},{18,... | collective-permute-start | bytes 786440 | tf_op jit(solution)/shard_map/ppermute | solution.py:416
  40.8 1.9 %collective-permute-start.14 = (bf16[256,512]{1,0:T(8,128)(2,1)S(1)}, bf16[256,512]{1,0:T(8,128)(2,1)S(1)}, u32[]{:S(2)}, u32[]{:S(2)}) collective-permute-start(bf16[256,512]{1,0:T(8,128)(2,1)S(1)} %collective-permute-done.13.refs_1_.refs_14_.refs_21_), channel_id=1, source_target_pairs={{0,2},{2,0},{4,6},{6,4},{8,10},{10,8},{12,14},{14,12},{16,18},{18,... | collective-permute-start | bytes 786440 | tf_op jit(solution)/shard_map/ppermute | solution.py:416
  42.2 1.4 %collective-permute-start.15 = (f32[16,256]{1,0:T(8,128)S(1)}, f32[16,256]{1,0:T(8,128)S(1)}, u32[]{:S(2)}, u32[]{:S(2)}) collective-permute-start(f32[16,256]{1,0:T(8,128)S(1)} %partial_den.9.refs_2_), channel_id=1, source_target_pairs={{0,2},{2,0},{4,6},{6,4},{8,10},{10,8},{12,14},{14,12},{16,18},{18,... | collective-permute-start | bytes 49160 | tf_op jit(solution)/shard_map/ppermute | solution.py:416
  45.3 1.6 %collective-permute-start.17 = (bf16[256,512]{1,0:T(8,128)(2,1)S(1)}, bf16[256,512]{1,0:T(8,128)(2,1)S(1)}, u32[]{:S(2)}, u32[]{:S(2)}) collective-permute-start(bf16[256,512]{1,0:T(8,128)(2,1)S(1)} %get-tuple-element.59.refs_2_), channel_id=1, source_target_pairs={{0,2},{2,0},{4,6},{6,4},{8,10},{10,8},{12,14},{14,12},{16,18},{18,... | collective-permute-start | bytes 786440 | tf_op jit(solution)/shard_map/ppermute | solution.py:416
  47.5 7.4 %collective-permute-start.18 = (bf16[128,512]{1,0:T(8,128)(2,1)S(1)}, bf16[128,512]{1,0:T(8,128)(2,1)S(1)}, u32[]{:S(2)}, u32[]{:S(2)}) collective-permute-start(bf16[128,512]{1,0:T(8,128)(2,1)S(1)} %get-tuple-element.62), channel_id=1, source_target_pairs={{0,1},{1,0},{2,3},{3,2},{4,5},{5,4},{6,7},{7,6},{8,9},{9,8},{10,11... | collective-permute-start | bytes 393224 | tf_op jit(solution)/shard_map/ppermute | solution.py:416
  49.0 8.3 %collective-permute-start.19 = (bf16[128,512]{1,0:T(8,128)(2,1)S(1)}, bf16[128,512]{1,0:T(8,128)(2,1)S(1)}, u32[]{:S(2)}, u32[]{:S(2)}) collective-permute-start(bf16[128,512]{1,0:T(8,128)(2,1)S(1)} %get-tuple-element.63), channel_id=1, source_target_pairs={{0,4},{2,6},{4,0},{6,2},{8,12},{10,14},{12,8},{14,10},{16,20},{18,... | collective-permute-start | bytes 393224 | tf_op jit(solution)/shard_map/ppermute | solution.py:416
  50.8 7.3 %collective-permute-start.20 = (bf16[128,512]{1,0:T(8,128)(2,1)S(1)}, bf16[128,512]{1,0:T(8,128)(2,1)S(1)}, u32[]{:S(2)}, u32[]{:S(2)}) collective-permute-start(bf16[128,512]{1,0:T(8,128)(2,1)S(1)} %get-tuple-element.64), channel_id=1, source_target_pairs={{0,5},{1,4},{2,7},{3,6},{4,1},{5,0},{6,3},{7,2},{8,13},{9,12},{10,... | collective-permute-start | bytes 393224 | tf_op jit(solution)/shard_map/ppermute | solution.py:437
  51.5 13.2 %collective-permute-start.22 = (bf16[128,512]{1,0:T(8,128)(2,1)S(1)}, bf16[128,512]{1,0:T(8,128)(2,1)S(1)}, u32[]{:S(2)}, u32[]{:S(2)}) collective-permute-start(bf16[128,512]{1,0:T(8,128)(2,1)S(1)} %get-tuple-element.67), channel_id=1, source_target_pairs={{0,1},{1,0},{2,3},{3,2},{4,5},{5,4},{6,7},{7,6},{8,9},{9,8},{10,11... | collective-permute-start | bytes 393224 | tf_op jit(solution)/shard_map/ppermute | solution.py:416
  53.1 11.6 %collective-permute-start.23 = (bf16[128,512]{1,0:T(8,128)(2,1)S(1)}, bf16[128,512]{1,0:T(8,128)(2,1)S(1)}, u32[]{:S(2)}, u32[]{:S(2)}) collective-permute-start(bf16[128,512]{1,0:T(8,128)(2,1)S(1)} %get-tuple-element.68), channel_id=1, source_target_pairs={{0,4},{2,6},{4,0},{6,2},{8,12},{10,14},{12,8},{14,10},{16,20},{18,... | collective-permute-start | bytes 393224 | tf_op jit(solution)/shard_map/ppermute | solution.py:416
  54.8 9.9 %collective-permute-start.24 = (bf16[128,512]{1,0:T(8,128)(2,1)S(1)}, bf16[128,512]{1,0:T(8,128)(2,1)S(1)}, u32[]{:S(2)}, u32[]{:S(2)}) collective-permute-start(bf16[128,512]{1,0:T(8,128)(2,1)S(1)} %get-tuple-element.69), channel_id=1, source_target_pairs={{0,5},{1,4},{2,7},{3,6},{4,1},{5,0},{6,3},{7,2},{8,13},{9,12},{10,... | collective-permute-start | bytes 393224 | tf_op jit(solution)/shard_map/ppermute | solution.py:437
  58.2 6.5 %collective-permute-start.21 = (bf16[64,512]{1,0:T(8,128)(2,1)S(1)}, bf16[64,512]{1,0:T(8,128)(2,1)S(1)}, u32[]{:S(2)}, u32[]{:S(2)}) collective-permute-start(bf16[64,512]{1,0:T(8,128)(2,1)S(1)} %get-tuple-element.65), channel_id=1, source_target_pairs={{0,16},{2,18},{4,20},{6,22},{8,24},{10,26},{12,28},{14,30},{16,0},... | collective-permute-start | bytes 196616 | tf_op jit(solution)/shard_map/ppermute | solution.py:416
  60.7 6.3 %collective-permute-start.25 = (bf16[64,512]{1,0:T(8,128)(2,1)S(1)}, bf16[64,512]{1,0:T(8,128)(2,1)S(1)}, u32[]{:S(2)}, u32[]{:S(2)}) collective-permute-start(bf16[64,512]{1,0:T(8,128)(2,1)S(1)} %get-tuple-element.71), channel_id=1, source_target_pairs={{0,24},{2,26},{4,28},{6,30},{8,16},{10,18},{12,20},{14,22},{16,8},... | collective-permute-start | bytes 196616 | tf_op jit(solution)/shard_map/ppermute | solution.py:416
  64.8 4.8 %collective-permute-start.26 = (bf16[64,512]{1,0:T(8,128)(2,1)S(1)}, bf16[64,512]{1,0:T(8,128)(2,1)S(1)}, u32[]{:S(2)}, u32[]{:S(2)}) collective-permute-start(bf16[64,512]{1,0:T(8,128)(2,1)S(1)} %get-tuple-element.72), channel_id=1, source_target_pairs={{0,8},{2,10},{4,12},{6,14},{8,0},{10,2},{12,4},{14,6},{16,24},{18,... | collective-permute-start | bytes 196616 | tf_op jit(solution)/shard_map/ppermute | solution.py:416
  69.7 4.8 %collective-permute-start.35 = (bf16[64,512]{1,0:T(8,128)(2,1)S(1)}, bf16[64,512]{1,0:T(8,128)(2,1)S(1)}, u32[]{:S(2)}, u32[]{:S(2)}) collective-permute-start(bf16[64,512]{1,0:T(8,128)(2,1)S(1)} %add_convert_fusion), channel_id=1, source_target_pairs={{0,8},{2,10},{4,12},{6,14},{8,0},{10,2},{12,4},{14,6},{16,24},{18,... | collective-permute-start | bytes 196616 | tf_op jit(solution)/shard_map/ppermute | solution.py:416
  69.8 8.3 %collective-permute-start.28 = (bf16[64,512]{1,0:T(8,128)(2,1)S(1)}, bf16[64,512]{1,0:T(8,128)(2,1)S(1)}, u32[]{:S(2)}, u32[]{:S(2)}) collective-permute-start(bf16[64,512]{1,0:T(8,128)(2,1)S(1)} %add_convert_fusion), channel_id=1, source_target_pairs={{0,24},{2,26},{4,28},{6,30},{8,16},{10,18},{12,20},{14,22},{16,8},... | collective-permute-start | bytes 196616 | tf_op jit(solution)/shard_map/ppermute | solution.py:416
  72.0 6.0 %collective-permute-start.27 = (bf16[64,512]{1,0:T(8,128)(2,1)S(1)}, bf16[64,512]{1,0:T(8,128)(2,1)S(1)}, u32[]{:S(2)}, u32[]{:S(2)}) collective-permute-start(bf16[64,512]{1,0:T(8,128)(2,1)S(1)} %add_convert_fusion), channel_id=1, source_target_pairs={{0,16},{2,18},{4,20},{6,22},{8,24},{10,26},{12,28},{14,30},{16,0},... | collective-permute-start | bytes 196616 | tf_op jit(solution)/shard_map/ppermute | solution.py:416
  74.5 6.4 %collective-permute-start.36 = (bf16[2,64,512]{2,1,0:T(8,128)(2,1)S(1)}, bf16[2,64,512]{2,1,0:T(8,128)(2,1)S(1)}, u32[]{:S(2)}, u32[]{:S(2)}) collective-permute-start(bf16[2,64,512]{2,1,0:T(8,128)(2,1)S(1)} %pad_maximum_fusion.2), channel_id=1, source_target_pairs={{0,1},{1,0},{2,3},{3,2},{4,5},{5,4},{6,7},{7,6},{8,9},{9,8},{10,11... | collective-permute-start | bytes 393224 | tf_op jit(solution)/shard_map/ppermute | solution.py:416
  75.9 7.4 %collective-permute-start.37 = (bf16[2,64,512]{2,1,0:T(8,128)(2,1)S(1)}, bf16[2,64,512]{2,1,0:T(8,128)(2,1)S(1)}, u32[]{:S(2)}, u32[]{:S(2)}) collective-permute-start(bf16[2,64,512]{2,1,0:T(8,128)(2,1)S(1)} %pad_maximum_fusion.2), channel_id=1, source_target_pairs={{0,4},{2,6},{4,0},{6,2},{8,12},{10,14},{12,8},{14,10},{16,20},{18,... | collective-permute-start | bytes 393224 | tf_op jit(solution)/shard_map/ppermute | solution.py:416
  76.3 6.5 %collective-permute-start.38 = (bf16[2,64,512]{2,1,0:T(8,128)(2,1)S(1)}, bf16[2,64,512]{2,1,0:T(8,128)(2,1)S(1)}, u32[]{:S(2)}, u32[]{:S(2)}) collective-permute-start(bf16[2,64,512]{2,1,0:T(8,128)(2,1)S(1)} %pad_maximum_fusion.2), channel_id=1, source_target_pairs={{0,5},{1,4},{2,7},{3,6},{4,1},{5,0},{6,3},{7,2},{8,13},{9,12},{10,... | collective-permute-start | bytes 393224 | tf_op jit(solution)/shard_map/ppermute | solution.py:437
  78.1 5.7 %collective-permute-start.29 = (bf16[2,64,512]{2,1,0:T(8,128)(2,1)S(1)}, bf16[2,64,512]{2,1,0:T(8,128)(2,1)S(1)}, u32[]{:S(2)}, u32[]{:S(2)}) collective-permute-start(bf16[2,64,512]{2,1,0:T(8,128)(2,1)S(1)} %pad_maximum_fusion.1), channel_id=1, source_target_pairs={{0,1},{1,0},{2,3},{3,2},{4,5},{5,4},{6,7},{7,6},{8,9},{9,8},{10,11... | collective-permute-start | bytes 393224 | tf_op jit(solution)/shard_map/ppermute | solution.py:416
  79.9 5.0 %collective-permute-start.30 = (bf16[2,64,512]{2,1,0:T(8,128)(2,1)S(1)}, bf16[2,64,512]{2,1,0:T(8,128)(2,1)S(1)}, u32[]{:S(2)}, u32[]{:S(2)}) collective-permute-start(bf16[2,64,512]{2,1,0:T(8,128)(2,1)S(1)} %pad_maximum_fusion.1), channel_id=1, source_target_pairs={{0,4},{2,6},{4,0},{6,2},{8,12},{10,14},{12,8},{14,10},{16,20},{18,... | collective-permute-start | bytes 393224 | tf_op jit(solution)/shard_map/ppermute | solution.py:416
  81.0 5.9 %collective-permute-start.31 = (bf16[2,64,512]{2,1,0:T(8,128)(2,1)S(1)}, bf16[2,64,512]{2,1,0:T(8,128)(2,1)S(1)}, u32[]{:S(2)}, u32[]{:S(2)}) collective-permute-start(bf16[2,64,512]{2,1,0:T(8,128)(2,1)S(1)} %pad_maximum_fusion.1), channel_id=1, source_target_pairs={{0,5},{1,4},{2,7},{3,6},{4,1},{5,0},{6,3},{7,2},{8,13},{9,12},{10,... | collective-permute-start | bytes 393224 | tf_op jit(solution)/shard_map/ppermute | solution.py:437
  82.8 4.1 %collective-permute-start.39 = (bf16[2,64,512]{2,1,0:T(8,128)(2,1)S(1)}, bf16[2,64,512]{2,1,0:T(8,128)(2,1)S(1)}, u32[]{:S(2)}, u32[]{:S(2)}) collective-permute-start(bf16[2,64,512]{2,1,0:T(8,128)(2,1)S(1)} %collective-permute-done.36.refs_1_), channel_id=1, source_target_pairs={{0,2},{2,0},{4,6},{6,4},{8,10},{10,8},{12,14},{14,12},{16,18},{18,... | collective-permute-start | bytes 393224 | tf_op jit(solution)/shard_map/ppermute | solution.py:416
  83.3 4.9 %collective-permute-start.42 = (bf16[4,64,512]{2,1,0:T(8,128)(2,1)S(1)}, bf16[4,64,512]{2,1,0:T(8,128)(2,1)S(1)}, u32[]{:S(2)}, u32[]{:S(2)}) collective-permute-start(bf16[4,64,512]{2,1,0:T(8,128)(2,1)S(1)} %pad_maximum_fusion.refs_0_), channel_id=1, source_target_pairs={{0,2},{2,0},{4,6},{6,4},{8,10},{10,8},{12,14},{14,12},{16,18},{18,... | collective-permute-start | bytes 786440 | tf_op jit(solution)/shard_map/ppermute | solution.py:416
  83.8 3.6 %collective-permute-start.40 = (bf16[2,64,512]{2,1,0:T(8,128)(2,1)S(1)}, bf16[2,64,512]{2,1,0:T(8,128)(2,1)S(1)}, u32[]{:S(2)}, u32[]{:S(2)}) collective-permute-start(bf16[2,64,512]{2,1,0:T(8,128)(2,1)S(1)} %collective-permute-done.37.refs_2_), channel_id=1, source_target_pairs={{0,2},{2,0},{4,6},{6,4},{8,10},{10,8},{12,14},{14,12},{16,18},{18,... | collective-permute-start | bytes 393224 | tf_op jit(solution)/shard_map/ppermute | solution.py:416
  84.9 5.0 %collective-permute-start.32 = (bf16[2,64,512]{2,1,0:T(8,128)(2,1)S(1)}, bf16[2,64,512]{2,1,0:T(8,128)(2,1)S(1)}, u32[]{:S(2)}, u32[]{:S(2)}) collective-permute-start(bf16[2,64,512]{2,1,0:T(8,128)(2,1)S(1)} %collective-permute-done.29.refs_0_), channel_id=1, source_target_pairs={{0,2},{2,0},{4,6},{6,4},{8,10},{10,8},{12,14},{14,12},{16,18},{18,... | collective-permute-start | bytes 393224 | tf_op jit(solution)/shard_map/ppermute | solution.py:416
  86.9 1.3 %collective-permute-start.41 = (bf16[2,64,512]{2,1,0:T(8,128)(2,1)S(1)}, bf16[2,64,512]{2,1,0:T(8,128)(2,1)S(1)}, u32[]{:S(2)}, u32[]{:S(2)}) collective-permute-start(bf16[2,64,512]{2,1,0:T(8,128)(2,1)S(1)} %collective-permute-done.38.refs_3_), channel_id=1, source_target_pairs={{0,2},{2,0},{4,6},{6,4},{8,10},{10,8},{12,14},{14,12},{16,18},{18,... | collective-permute-start | bytes 393224 | tf_op jit(solution)/shard_map/ppermute | solution.py:416
  86.9 3.0 %collective-permute-start.33 = (bf16[2,64,512]{2,1,0:T(8,128)(2,1)S(1)}, bf16[2,64,512]{2,1,0:T(8,128)(2,1)S(1)}, u32[]{:S(2)}, u32[]{:S(2)}) collective-permute-start(bf16[2,64,512]{2,1,0:T(8,128)(2,1)S(1)} %collective-permute-done.30.refs_1_), channel_id=1, source_target_pairs={{0,2},{2,0},{4,6},{6,4},{8,10},{10,8},{12,14},{14,12},{16,18},{18,... | collective-permute-start | bytes 393224 | tf_op jit(solution)/shard_map/ppermute | solution.py:416
  87.4 2.5 %collective-permute-start.34 = (bf16[2,64,512]{2,1,0:T(8,128)(2,1)S(1)}, bf16[2,64,512]{2,1,0:T(8,128)(2,1)S(1)}, u32[]{:S(2)}, u32[]{:S(2)}) collective-permute-start(bf16[2,64,512]{2,1,0:T(8,128)(2,1)S(1)} %collective-permute-done.31.refs_2_), channel_id=1, source_target_pairs={{0,2},{2,0},{4,6},{6,4},{8,10},{10,8},{12,14},{14,12},{16,18},{18,... | collective-permute-start | bytes 393224 | tf_op jit(solution)/shard_map/ppermute | solution.py:416

commit v3 on v2

--- a/solution.py
+++ b/solution.py
@@ -466,7 +466,7 @@
         far_y = blk_swap(gate(far, dens[1]), Y)
         use(pair(over_y, Y), pair(far, 2 * Z0))
         mid_y = blk_swap(mid, Y)
-        use(pair(near_y, Z0 | Y), pair(far_y, 2 * Z0 | Y, mid), pair(mid, 3 * Z0, dens[2]))
+        use(pair(near_y, Z0 | Y), pair(far_y, 2 * Z0 | Y, mid), pair(mid, 3 * Z0))
         (pos,) = take_row(0)
         ending = pair(mid_y, 3 * Z0 | Y, dens[-1], es[-1])
     else:

time: 91.5 us -> 91 us (level)
    ppermute x39, starting transfers between devices: 33.6 us -> 32.1 us  [swap(): return lax.ppermute(x, axis, [(i, i ^ mask) for i in range(size)])]
  transfers between devices with their start and end apart: 43 -> 43, of which waited for: 19 -> 20; matrix products, arithmetic and copies ran while one was open for 0% -> 0% of each run, Pallas kernels for 15% -> 15%
where the time goes in v3:
time: 91 us; the launch traced here: 90.9 us
  starting transfers between devices  37.5 us (41%)
  waiting for transfers between devices  34.1 us (37%)
  Pallas kernels  18.1 us (20%)
  between operations  0.98 us (1%)
    ppermute x39, starting transfers between devices, swap(): return lax.ppermute(x, axis, [(i, i ^ mask) for i in range(size)])  32.1 us
    ppermute x39, waiting for transfers between devices, swap(): return lax.ppermute(x, axis, [(i, i ^ mask) for i in range(size)])  31.1 us
    pallas_call x5, Pallas kernels, partial_den(): pl.pallas_call(functools.partial(den_kernel, len(old), n_new, before is N...  6.88 us
    ppermute x4, starting transfers between devices, both_swap(): return lax.ppermute(x, ('blk', 'group'), moves)  5.44 us
    ppermute x4, waiting for transfers between devices, both_swap(): return lax.ppermute(x, ('blk', 'group'), moves)  3.04 us
    pallas_call x2, Pallas kernels, place(): pl.pallas_call(functools.partial(place_kernel, plan, planes), in_specs=[V...  2.92 us
    pallas_call x1, Pallas kernels, project(): pl.pallas_call(project_kernel, in_specs=[ANY] * 2, out_specs=[VMEM] * 2,...  2.46 us
    pallas_call x2, Pallas kernels, own_row(): pl.pallas_call(functools.partial(row_kernel, rs, first), in_specs=[VMEM]...  2.06 us
  transfers between devices with their start and end apart: 43, of which 20 were waited for; matrix products, arithmetic and copies ran while one was open for 0% of the time, Pallas kernels for 15%

profile of v3, /device:TPU:0, one launch (start us, length us, event | category | flops | bytes accessed | tf_op | source)
XLA Modules:
  0.0 90.9 jit_solution(10174992247856543111)
XLA Ops:
  0.7 2.5 %project.1 = (f32[256,512]{1,0:T(8,128)S(1)}, bf16[256,512]{1,0:T(8,128)(2,1)S(1)}) custom-call(bf16[256,2048]{1,0:T(8,128)(2,1)} %bitcast.6, bf16[2048,512]{1,0:T(8,128)(2,1)} %w_hbm.1), custom_call_target="tpu_custom_call" | custom-call | flops 536870912 | bytes 3145728 | tf_op jit(solution)/shard_map/project/pallas_call | solution.py:61
  3.1 3.1 %collective-permute-start.1 = (bf16[256,512]{1,0:T(8,128)(2,1)S(1)}, bf16[256,512]{1,0:T(8,128)(2,1)S(1)}, u32[]{:S(2)}, u32[]{:S(2)}) collective-permute-start(bf16[256,512]{1,0:T(8,128)(2,1)S(1)} %get-tuple-element.39.refs_0_.x_ref.refs_7_), channel_id=1, source_target_pairs={{0,8},{2,10},{4,12},{6,14},{8,0},{10,2},{12,4},{14,6},{16,24},{18,... | collective-permute-start | bytes 786440 | tf_op jit(solution)/shard_map/ppermute | solution.py:416
  6.2 1.5 %collective-permute-start.3 = (bf16[256,512]{1,0:T(8,128)(2,1)S(1)}, bf16[256,512]{1,0:T(8,128)(2,1)S(1)}, u32[]{:S(2)}, u32[]{:S(2)}) collective-permute-start(bf16[256,512]{1,0:T(8,128)(2,1)S(1)} %get-tuple-element.39.refs_0_.x_ref.refs_7_), channel_id=1, source_target_pairs={{0,4},{2,6},{4,0},{6,2},{8,12},{10,14},{12,8},{14,10},{16,20},{18,... | collective-permute-start | bytes 786440 | tf_op jit(solution)/shard_map/ppermute | solution.py:416
  7.7 2.6 %collective-permute-start.5 = (bf16[256,512]{1,0:T(8,128)(2,1)S(1)}, bf16[256,512]{1,0:T(8,128)(2,1)S(1)}, u32[]{:S(2)}, u32[]{:S(2)}) collective-permute-start(bf16[256,512]{1,0:T(8,128)(2,1)S(1)} %get-tuple-element.39.refs_0_.x_ref.refs_7_), channel_id=1, source_target_pairs={{0,16},{2,18},{4,20},{6,22},{8,24},{10,26},{12,28},{14,30},{16,0},... | collective-permute-start | bytes 786440 | tf_op jit(solution)/shard_map/ppermute | solution.py:416
  10.3 4.7 %collective-permute-done.1.refs_2_.refs_9_ = bf16[256,512]{1,0:T(8,128)(2,1)S(1)} collective-permute-done((bf16[256,512]{1,0:T(8,128)(2,1)S(1)}, bf16[256,512]{1,0:T(8,128)(2,1)S(1)}, u32[]{:S(2)}, u32[]{:S(2)}) %collective-permute-start.1) | collective-permute-done | bytes 262176 | tf_op jit(solution)/shard_map/ppermute | solution.py:416
  15.0 3.3 %collective-permute-start.7 = (bf16[256,512]{1,0:T(8,128)(2,1)S(1)}, bf16[256,512]{1,0:T(8,128)(2,1)S(1)}, u32[]{:S(2)}, u32[]{:S(2)}) collective-permute-start(bf16[256,512]{1,0:T(8,128)(2,1)S(1)} %collective-permute-done.1.refs_2_.refs_9_), channel_id=1, source_target_pairs={{0,4},{2,6},{4,0},{6,2},{8,12},{10,14},{12,8},{14,10},{16,20},{18,... | collective-permute-start | bytes 786440 | tf_op jit(solution)/shard_map/ppermute | solution.py:416
  18.2 0.5 partial_den.5.refs_4_
  18.7 4.3 %collective-permute-done.5.refs_6_.refs_13_ = bf16[256,512]{1,0:T(8,128)(2,1)S(1)} collective-permute-done((bf16[256,512]{1,0:T(8,128)(2,1)S(1)}, bf16[256,512]{1,0:T(8,128)(2,1)S(1)}, u32[]{:S(2)}, u32[]{:S(2)}) %collective-permute-start.5) | collective-permute-done | bytes 262176 | tf_op jit(solution)/shard_map/ppermute | solution.py:416
  23.0 0.6 partial_den.6.refs_8_
  23.6 0.5 collective-permute-start.9
  24.2 0.5 collective-permute-start.6
  24.7 0.6 collective-permute-done.7.refs_8_.refs_15_
  25.2 5.7 %collective-permute-done.10.refs_12_.refs_19_ = bf16[256,512]{1,0:T(8,128)(2,1)S(1)} collective-permute-done((bf16[256,512]{1,0:T(8,128)(2,1)S(1)}, bf16[256,512]{1,0:T(8,128)(2,1)S(1)}, u32[]{:S(2)}, u32[]{:S(2)}) %collective-permute-start.10) | collective-permute-done | bytes 262176 | tf_op jit(solution)/shard_map/ppermute | solution.py:416
  31.0 0.6 collective-permute-done.9.refs_10_.refs_17_
  31.6 0.5 collective-permute-start.11
  32.1 1.0 %collective-permute-start.13 = (bf16[256,512]{1,0:T(8,128)(2,1)S(1)}, bf16[256,512]{1,0:T(8,128)(2,1)S(1)}, u32[]{:S(2)}, u32[]{:S(2)}) collective-permute-start(bf16[256,512]{1,0:T(8,128)(2,1)S(1)} %collective-permute-done.10.refs_12_.refs_19_), channel_id=1, source_target_pairs={{0,4},{2,6},{4,0},{6,2},{8,12},{10,14},{12,8},{14,10},{16,20},{18,... | collective-permute-start | bytes 786440 | tf_op jit(solution)/shard_map/ppermute | solution.py:416
  33.1 1.3 %partial_den.7.refs_14_ = f32[16,256]{1,0:T(8,128)S(1)} custom-call(bf16[256,512]{1,0:T(8,128)(2,1)S(1)} %get-tuple-element.39.refs_0_.x_ref.refs_7_, bf16[256,512]{1,0:T(8,128)(2,1)S(1)} %collective-permute-done.refs_1_.refs_8_, bf16[256,512]{1,0:T(8,128)(2,1)S(1)} %collective-permute-done.1.refs_2_.refs_9_, ...), custom_call_target="tpu_custom_call" | custom-call | tf_op jit(solution)/shard_map/partial_den/pallas_call | solution.py:142
  34.5 1.5 %own_row.2 = (f32[256,3584]{1,0:T(8,128)S(1)}, f32[1,256]{1,0:T(1,128)S(1)}) custom-call(s32[1,256]{1,0:T(1,128)S(1)} %copy-done.1, bf16[256,512]{1,0:T(8,128)(2,1)S(1)} %get-tuple-element.39.refs_0_.x_ref.refs_7_, bf16[256,512]{1,0:T(8,128)(2,1)S(1)} %get-tuple-element.39.refs_0_.x_ref.refs_7_, bf16[256,512]{1,0:T(8,128)(2,1)S(1)} %collective-permute-done.refs_1_.refs_8_, ...), custom_call_target="tpu_custom_call" | custom-call | tf_op jit(solution)/shard_map/own_row/pallas_call | solution.py:208
  36.0 3.1 %partial_den.8.refs_15_ = f32[16,256]{1,0:T(8,128)S(1)} custom-call(bf16[256,512]{1,0:T(8,128)(2,1)S(1)} %get-tuple-element.39.refs_0_.x_ref.refs_7_, bf16[256,512]{1,0:T(8,128)(2,1)S(1)} %collective-permute-done.refs_1_.refs_8_, bf16[256,512]{1,0:T(8,128)(2,1)S(1)} %collective-permute-done.1.refs_2_.refs_9_, ...), custom_call_target="tpu_custom_call" | custom-call | tf_op jit(solution)/shard_map/partial_den/pallas_call | solution.py:142
  39.1 1.3 %collective-permute-done.13.refs_1_.refs_14_.refs_21_ = bf16[256,512]{1,0:T(8,128)(2,1)S(1)} collective-permute-done((bf16[256,512]{1,0:T(8,128)(2,1)S(1)}, bf16[256,512]{1,0:T(8,128)(2,1)S(1)}, u32[]{:S(2)}, u32[]{:S(2)}) %collective-permute-start.13) | collective-permute-done | bytes 262176 | tf_op jit(solution)/shard_map/ppermute | solution.py:416
  40.4 1.4 %partial_den.9.refs_2_ = f32[16,256]{1,0:T(8,128)S(1)} custom-call(bf16[256,512]{1,0:T(8,128)(2,1)S(1)} %get-tuple-element.39.refs_0_.x_ref.refs_7_, bf16[256,512]{1,0:T(8,128)(2,1)S(1)} %collective-permute-done.refs_1_.refs_8_, bf16[256,512]{1,0:T(8,128)(2,1)S(1)} %collective-permute-done.1.refs_2_.refs_9_, ...), custom_call_target="tpu_custom_call" | custom-call | tf_op jit(solution)/shard_map/partial_den/pallas_call | solution.py:142
  41.8 0.5 collective-permute-start.15
  42.3 0.5 own_row.3
  42.9 0.3 collective-permute-done.15.refs_3_
  43.2 1.8 %gradient.1 = (f32[1,256]{1,0:T(1,128)S(1)}, f32[256,512]{1,0:T(8,128)S(1)}, bf16[256,512]{1,0:T(8,128)(2,1)S(1)}) custom-call(s32[1,256]{1,0:T(1,128)S(1)} %copy-done.1, f32[256,512]{1,0:T(8,128)S(1)} %get-tuple-element.47.refs_1_, f32[16,256]{1,0:T(8,128)S(1)} %partial_den.9.refs_2_, f32[16,256]{1,0:T(8,128)S(1)} %collective-permute-done.15.refs_3_, ...), custom_call_target="tpu_custom_call" | custom-call | flops 1073741824 | bytes 12582912 | tf_op jit(solution)/shard_map/gradient/pallas_call | solution.py:268
  45.0 0.4 collective-permute-start.17
  45.4 1.2 %collective-permute-done.17.refs_3_ = bf16[256,512]{1,0:T(8,128)(2,1)S(1)} collective-permute-done((bf16[256,512]{1,0:T(8,128)(2,1)S(1)}, bf16[256,512]{1,0:T(8,128)(2,1)S(1)}, u32[]{:S(2)}, u32[]{:S(2)}) %collective-permute-start.17) | collective-permute-done | bytes 262176 | tf_op jit(solution)/shard_map/ppermute | solution.py:416
  46.6 0.5 head_partial.2
  47.1 1.6 %collective-permute-start.18 = (bf16[128,512]{1,0:T(8,128)(2,1)S(1)}, bf16[128,512]{1,0:T(8,128)(2,1)S(1)}, u32[]{:S(2)}, u32[]{:S(2)}) collective-permute-start(bf16[128,512]{1,0:T(8,128)(2,1)S(1)} %get-tuple-element.60), channel_id=1, source_target_pairs={{0,1},{1,0},{2,3},{3,2},{4,5},{5,4},{6,7},{7,6},{8,9},{9,8},{10,11... | collective-permute-start | bytes 393224 | tf_op jit(solution)/shard_map/ppermute | solution.py:416
  48.6 1.0 %collective-permute-start.19 = (bf16[128,512]{1,0:T(8,128)(2,1)S(1)}, bf16[128,512]{1,0:T(8,128)(2,1)S(1)}, u32[]{:S(2)}, u32[]{:S(2)}) collective-permute-start(bf16[128,512]{1,0:T(8,128)(2,1)S(1)} %get-tuple-element.61), channel_id=1, source_target_pairs={{0,4},{2,6},{4,0},{6,2},{8,12},{10,14},{12,8},{14,10},{16,20},{18,... | collective-permute-start | bytes 393224 | tf_op jit(solution)/shard_map/ppermute | solution.py:416
  49.6 1.0 %collective-permute-start.20 = (bf16[128,512]{1,0:T(8,128)(2,1)S(1)}, bf16[128,512]{1,0:T(8,128)(2,1)S(1)}, u32[]{:S(2)}, u32[]{:S(2)}) collective-permute-start(bf16[128,512]{1,0:T(8,128)(2,1)S(1)} %get-tuple-element.62), channel_id=1, source_target_pairs={{0,5},{1,4},{2,7},{3,6},{4,1},{5,0},{6,3},{7,2},{8,13},{9,12},{10,... | collective-permute-start | bytes 393224 | tf_op jit(solution)/shard_map/ppermute | solution.py:437
  50.6 0.5 head_partial.3
  51.1 1.5 %collective-permute-start.22 = (bf16[128,512]{1,0:T(8,128)(2,1)S(1)}, bf16[128,512]{1,0:T(8,128)(2,1)S(1)}, u32[]{:S(2)}, u32[]{:S(2)}) collective-permute-start(bf16[128,512]{1,0:T(8,128)(2,1)S(1)} %get-tuple-element.65), channel_id=1, source_target_pairs={{0,1},{1,0},{2,3},{3,2},{4,5},{5,4},{6,7},{7,6},{8,9},{9,8},{10,11... | collective-permute-start | bytes 393224 | tf_op jit(solution)/shard_map/ppermute | solution.py:416
  52.7 1.0 %collective-permute-start.23 = (bf16[128,512]{1,0:T(8,128)(2,1)S(1)}, bf16[128,512]{1,0:T(8,128)(2,1)S(1)}, u32[]{:S(2)}, u32[]{:S(2)}) collective-permute-start(bf16[128,512]{1,0:T(8,128)(2,1)S(1)} %get-tuple-element.66), channel_id=1, source_target_pairs={{0,4},{2,6},{4,0},{6,2},{8,12},{10,14},{12,8},{14,10},{16,20},{18,... | collective-permute-start | bytes 393224 | tf_op jit(solution)/shard_map/ppermute | solution.py:416
  53.7 1.7 %collective-permute-start.24 = (bf16[128,512]{1,0:T(8,128)(2,1)S(1)}, bf16[128,512]{1,0:T(8,128)(2,1)S(1)}, u32[]{:S(2)}, u32[]{:S(2)}) collective-permute-start(bf16[128,512]{1,0:T(8,128)(2,1)S(1)} %get-tuple-element.67), channel_id=1, source_target_pairs={{0,5},{1,4},{2,7},{3,6},{4,1},{5,0},{6,3},{7,2},{8,13},{9,12},{10,... | collective-permute-start | bytes 393224 | tf_op jit(solution)/shard_map/ppermute | solution.py:437
  55.4 0.8 hand_out.1
  56.2 1.3 %collective-permute-done.19.from_y = bf16[128,512]{1,0:T(8,128)(2,1)S(1)} collective-permute-done((bf16[128,512]{1,0:T(8,128)(2,1)S(1)}, bf16[128,512]{1,0:T(8,128)(2,1)S(1)}, u32[]{:S(2)}, u32[]{:S(2)}) %collective-permute-start.19) | collective-permute-done | bytes 131104 | tf_op jit(solution)/shard_map/ppermute | solution.py:416
  57.6 3.2 %collective-permute-start.21 = (bf16[64,512]{1,0:T(8,128)(2,1)S(1)}, bf16[64,512]{1,0:T(8,128)(2,1)S(1)}, u32[]{:S(2)}, u32[]{:S(2)}) collective-permute-start(bf16[64,512]{1,0:T(8,128)(2,1)S(1)} %get-tuple-element.63), channel_id=1, source_target_pairs={{0,16},{2,18},{4,20},{6,22},{8,24},{10,26},{12,28},{14,30},{16,0},... | collective-permute-start | bytes 196616 | tf_op jit(solution)/shard_map/ppermute | solution.py:416
  60.8 1.3 %collective-permute-start.25 = (bf16[64,512]{1,0:T(8,128)(2,1)S(1)}, bf16[64,512]{1,0:T(8,128)(2,1)S(1)}, u32[]{:S(2)}, u32[]{:S(2)}) collective-permute-start(bf16[64,512]{1,0:T(8,128)(2,1)S(1)} %get-tuple-element.69), channel_id=1, source_target_pairs={{0,24},{2,26},{4,28},{6,30},{8,16},{10,18},{12,20},{14,22},{16,8},... | collective-permute-start | bytes 196616 | tf_op jit(solution)/shard_map/ppermute | solution.py:416
  62.1 2.3 %collective-permute-done.21 = bf16[64,512]{1,0:T(8,128)(2,1)S(1)} collective-permute-done((bf16[64,512]{1,0:T(8,128)(2,1)S(1)}, bf16[64,512]{1,0:T(8,128)(2,1)S(1)}, u32[]{:S(2)}, u32[]{:S(2)}) %collective-permute-start.21) | collective-permute-done | bytes 65568 | tf_op jit(solution)/shard_map/ppermute | solution.py:416
  64.5 0.1 deal.3
  64.6 0.6 collective-permute-start.26
  65.1 2.0 %collective-permute-done.25 = bf16[64,512]{1,0:T(8,128)(2,1)S(1)} collective-permute-done((bf16[64,512]{1,0:T(8,128)(2,1)S(1)}, bf16[64,512]{1,0:T(8,128)(2,1)S(1)}, u32[]{:S(2)}, u32[]{:S(2)}) %collective-permute-start.25) | collective-permute-done | bytes 65568 | tf_op jit(solution)/shard_map/ppermute | solution.py:416
  67.1 2.3 %collective-permute-done.26 = bf16[64,512]{1,0:T(8,128)(2,1)S(1)} collective-permute-done((bf16[64,512]{1,0:T(8,128)(2,1)S(1)}, bf16[64,512]{1,0:T(8,128)(2,1)S(1)}, u32[]{:S(2)}, u32[]{:S(2)}) %collective-permute-start.26) | collective-permute-done | bytes 65568 | tf_op jit(solution)/shard_map/ppermute | solution.py:416
  69.5 2.5 %collective-permute-start.28 = (bf16[64,512]{1,0:T(8,128)(2,1)S(1)}, bf16[64,512]{1,0:T(8,128)(2,1)S(1)}, u32[]{:S(2)}, u32[]{:S(2)}) collective-permute-start(bf16[64,512]{1,0:T(8,128)(2,1)S(1)} %add_convert_fusion), channel_id=1, source_target_pairs={{0,24},{2,26},{4,28},{6,30},{8,16},{10,18},{12,20},{14,22},{16,8},... | collective-permute-start | bytes 196616 | tf_op jit(solution)/shard_map/ppermute | solution.py:416
  72.0 1.0 %collective-permute-start.27 = (bf16[64,512]{1,0:T(8,128)(2,1)S(1)}, bf16[64,512]{1,0:T(8,128)(2,1)S(1)}, u32[]{:S(2)}, u32[]{:S(2)}) collective-permute-start(bf16[64,512]{1,0:T(8,128)(2,1)S(1)} %add_convert_fusion), channel_id=1, source_target_pairs={{0,16},{2,18},{4,20},{6,22},{8,24},{10,26},{12,28},{14,30},{16,0},... | collective-permute-start | bytes 196616 | tf_op jit(solution)/shard_map/ppermute | solution.py:416
  73.0 1.2 %collective-permute-done.35 = bf16[64,512]{1,0:T(8,128)(2,1)S(1)} collective-permute-done((bf16[64,512]{1,0:T(8,128)(2,1)S(1)}, bf16[64,512]{1,0:T(8,128)(2,1)S(1)}, u32[]{:S(2)}, u32[]{:S(2)}) %collective-permute-start.35) | collective-permute-done | bytes 65568 | tf_op jit(solution)/shard_map/ppermute | solution.py:416
  74.2 0.4 collective-permute-start.36
  74.7 1.3 %collective-permute-start.37 = (bf16[2,64,512]{2,1,0:T(8,128)(2,1)S(1)}, bf16[2,64,512]{2,1,0:T(8,128)(2,1)S(1)}, u32[]{:S(2)}, u32[]{:S(2)}) collective-permute-start(bf16[2,64,512]{2,1,0:T(8,128)(2,1)S(1)} %pad_maximum_fusion.2), channel_id=1, source_target_pairs={{0,4},{2,6},{4,0},{6,2},{8,12},{10,14},{12,8},{14,10},{16,20},{18,... | collective-permute-start | bytes 393224 | tf_op jit(solution)/shard_map/ppermute | solution.py:416
  76.0 1.8 %collective-permute-start.38 = (bf16[2,64,512]{2,1,0:T(8,128)(2,1)S(1)}, bf16[2,64,512]{2,1,0:T(8,128)(2,1)S(1)}, u32[]{:S(2)}, u32[]{:S(2)}) collective-permute-start(bf16[2,64,512]{2,1,0:T(8,128)(2,1)S(1)} %pad_maximum_fusion.2), channel_id=1, source_target_pairs={{0,5},{1,4},{2,7},{3,6},{4,1},{5,0},{6,3},{7,2},{8,13},{9,12},{10,... | collective-permute-start | bytes 393224 | tf_op jit(solution)/shard_map/ppermute | solution.py:437
  77.8 1.2 %collective-permute-start.29 = (bf16[2,64,512]{2,1,0:T(8,128)(2,1)S(1)}, bf16[2,64,512]{2,1,0:T(8,128)(2,1)S(1)}, u32[]{:S(2)}, u32[]{:S(2)}) collective-permute-start(bf16[2,64,512]{2,1,0:T(8,128)(2,1)S(1)} %pad_maximum_fusion.1), channel_id=1, source_target_pairs={{0,1},{1,0},{2,3},{3,2},{4,5},{5,4},{6,7},{7,6},{8,9},{9,8},{10,11... | collective-permute-start | bytes 393224 | tf_op jit(solution)/shard_map/ppermute | solution.py:416
  79.0 0.6 collective-permute-start.30
  79.6 0.9 %collective-permute-done.36.refs_1_ = bf16[2,64,512]{2,1,0:T(8,128)(2,1)S(1)} collective-permute-done((bf16[2,64,512]{2,1,0:T(8,128)(2,1)S(1)}, bf16[2,64,512]{2,1,0:T(8,128)(2,1)S(1)}, u32[]{:S(2)}, u32[]{:S(2)}) %collective-permute-start.36) | collective-permute-done | bytes 131104 | tf_op jit(solution)/shard_map/ppermute | solution.py:416
  80.5 0.9 %collective-permute-start.31 = (bf16[2,64,512]{2,1,0:T(8,128)(2,1)S(1)}, bf16[2,64,512]{2,1,0:T(8,128)(2,1)S(1)}, u32[]{:S(2)}, u32[]{:S(2)}) collective-permute-start(bf16[2,64,512]{2,1,0:T(8,128)(2,1)S(1)} %pad_maximum_fusion.1), channel_id=1, source_target_pairs={{0,5},{1,4},{2,7},{3,6},{4,1},{5,0},{6,3},{7,2},{8,13},{9,12},{10,... | collective-permute-start | bytes 393224 | tf_op jit(solution)/shard_map/ppermute | solution.py:437
  81.5 0.7 collective-permute-done.38.refs_3_
  82.2 0.3 collective-permute-done.37.refs_2_
  82.4 0.3 collective-permute-start.42
  82.7 0.9 collective-permute-done.29.refs_0_
  83.5 0.4 collective-permute-done.30.refs_1_
  84.0 2.4 %collective-permute-done.31.refs_2_ = bf16[2,64,512]{2,1,0:T(8,128)(2,1)S(1)} collective-permute-done((bf16[2,64,512]{2,1,0:T(8,128)(2,1)S(1)}, bf16[2,64,512]{2,1,0:T(8,128)(2,1)S(1)}, u32[]{:S(2)}, u32[]{:S(2)}) %collective-permute-start.31) | collective-permute-done | bytes 131104 | tf_op jit(solution)/shard_map/ppermute | solution.py:437
  86.4 0.5 collective-permute-start.33
  87.0 0.8 collective-permute-done.41.refs_6_
  87.8 1.7 %place.2.refs_6_ = f32[2048,512]{1,0:T(8,128)} custom-call(bf16[4,64,512]{2,1,0:T(8,128)(2,1)S(1)} %pad_maximum_fusion.refs_0_, bf16[2,64,512]{2,1,0:T(8,128)(2,1)S(1)} %collective-permute-done.36.refs_1_, bf16[2,64,512]{2,1,0:T(8,128)(2,1)S(1)} %collective-permute-done.37.refs_2_, bf16[2,64,512]{2,1,0:T(8,128)(2,1)S(1)} %collective-permute-done.38.refs_3_, ...), custom_call_target="tpu_custom_call" | custom-call | tf_op jit(solution)/shard_map/place/pallas_call | solution.py:395
  89.5 1.3 %place.3 = f32[2048,512]{1,0:T(8,128)} custom-call(bf16[2,64,512]{2,1,0:T(8,128)(2,1)S(1)} %collective-permute-done.29.refs_0_, bf16[2,64,512]{2,1,0:T(8,128)(2,1)S(1)} %collective-permute-done.30.refs_1_, bf16[2,64,512]{2,1,0:T(8,128)(2,1)S(1)} %collective-permute-done.31.refs_2_, ...), custom_call_target="tpu_custom_call", output_to_operand_aliasing={{}: (6, {})} | custom-call | tf_op jit(solution)/shard_map/place/pallas_call | solution.py:395
  (46 shorter events, 0.5 us)
Async XLA Ops:
  0.6 24.6 %copy-start = (bf16[1,256,2048]{2,1,0:T(8,128)(2,1)S(1)}, bf16[1,256,2048]{2,1,0:T(8,128)(2,1)}, u32[]{:S(2)}) copy-start(bf16[1,256,2048]{2,1,0:T(8,128)(2,1)} %param.3) | copy-start | bytes 3145732
  0.6 33.8 %copy-start.1 = (s32[1,256]{1,0:T(1,128)S(1)}, s32[1,256]{1,0:T(1,128)}, u32[]{:S(2)}) copy-start(s32[1,256]{1,0:T(1,128)} %refs_0_.1) | copy-start | bytes 3076
  3.1 11.9 %collective-permute-start.1 = (bf16[256,512]{1,0:T(8,128)(2,1)S(1)}, bf16[256,512]{1,0:T(8,128)(2,1)S(1)}, u32[]{:S(2)}, u32[]{:S(2)}) collective-permute-start(bf16[256,512]{1,0:T(8,128)(2,1)S(1)} %get-tuple-element.39.refs_0_.x_ref.refs_7_), channel_id=1, source_target_pairs={{0,8},{2,10},{4,12},{6,14},{8,0},{10,2},{12,4},{14,6},{16,24},{18,... | collective-permute-start | bytes 786440 | tf_op jit(solution)/shard_map/ppermute | solution.py:416
  6.2 8.8 %collective-permute-start.3 = (bf16[256,512]{1,0:T(8,128)(2,1)S(1)}, bf16[256,512]{1,0:T(8,128)(2,1)S(1)}, u32[]{:S(2)}, u32[]{:S(2)}) collective-permute-start(bf16[256,512]{1,0:T(8,128)(2,1)S(1)} %get-tuple-element.39.refs_0_.x_ref.refs_7_), channel_id=1, source_target_pairs={{0,4},{2,6},{4,0},{6,2},{8,12},{10,14},{12,8},{14,10},{16,20},{18,... | collective-permute-start | bytes 786440 | tf_op jit(solution)/shard_map/ppermute | solution.py:416
  7.7 10.5 %collective-permute-start = (bf16[256,512]{1,0:T(8,128)(2,1)S(1)}, bf16[256,512]{1,0:T(8,128)(2,1)S(1)}, u32[]{:S(2)}, u32[]{:S(2)}) collective-permute-start(bf16[256,512]{1,0:T(8,128)(2,1)S(1)} %get-tuple-element.39.refs_0_.x_ref.refs_7_), channel_id=1, source_target_pairs={{0,2},{2,0},{4,6},{6,4},{8,10},{10,8},{12,14},{14,12},{16,18},{18,... | collective-permute-start | bytes 786440 | tf_op jit(solution)/shard_map/ppermute | solution.py:416
  7.7 15.3 %collective-permute-start.5 = (bf16[256,512]{1,0:T(8,128)(2,1)S(1)}, bf16[256,512]{1,0:T(8,128)(2,1)S(1)}, u32[]{:S(2)}, u32[]{:S(2)}) collective-permute-start(bf16[256,512]{1,0:T(8,128)(2,1)S(1)} %get-tuple-element.39.refs_0_.x_ref.refs_7_), channel_id=1, source_target_pairs={{0,16},{2,18},{4,20},{6,22},{8,24},{10,26},{12,28},{14,30},{16,0},... | collective-permute-start | bytes 786440 | tf_op jit(solution)/shard_map/ppermute | solution.py:416
  15.0 8.1 %collective-permute-start.2 = (bf16[256,512]{1,0:T(8,128)(2,1)S(1)}, bf16[256,512]{1,0:T(8,128)(2,1)S(1)}, u32[]{:S(2)}, u32[]{:S(2)}) collective-permute-start(bf16[256,512]{1,0:T(8,128)(2,1)S(1)} %collective-permute-done.1.refs_2_.refs_9_), channel_id=1, source_target_pairs={{0,2},{2,0},{4,6},{6,4},{8,10},{10,8},{12,14},{14,12},{16,18},{18,... | collective-permute-start | bytes 786440 | tf_op jit(solution)/shard_map/ppermute | solution.py:416
  15.0 10.2 %collective-permute-start.7 = (bf16[256,512]{1,0:T(8,128)(2,1)S(1)}, bf16[256,512]{1,0:T(8,128)(2,1)S(1)}, u32[]{:S(2)}, u32[]{:S(2)}) collective-permute-start(bf16[256,512]{1,0:T(8,128)(2,1)S(1)} %collective-permute-done.1.refs_2_.refs_9_), channel_id=1, source_target_pairs={{0,4},{2,6},{4,0},{6,2},{8,12},{10,14},{12,8},{14,10},{16,20},{18,... | collective-permute-start | bytes 786440 | tf_op jit(solution)/shard_map/ppermute | solution.py:416
  23.0 7.9 %collective-permute-start.10 = (bf16[256,512]{1,0:T(8,128)(2,1)S(1)}, bf16[256,512]{1,0:T(8,128)(2,1)S(1)}, u32[]{:S(2)}, u32[]{:S(2)}) collective-permute-start(bf16[256,512]{1,0:T(8,128)(2,1)S(1)} %collective-permute-done.5.refs_6_.refs_13_), channel_id=1, source_target_pairs={{0,8},{2,10},{4,12},{6,14},{8,0},{10,2},{12,4},{14,6},{16,24},{18,... | collective-permute-start | bytes 786440 | tf_op jit(solution)/shard_map/ppermute | solution.py:416
  23.6 8.0 %collective-permute-start.9 = (bf16[256,512]{1,0:T(8,128)(2,1)S(1)}, bf16[256,512]{1,0:T(8,128)(2,1)S(1)}, u32[]{:S(2)}, u32[]{:S(2)}) collective-permute-start(bf16[256,512]{1,0:T(8,128)(2,1)S(1)} %collective-permute-done.5.refs_6_.refs_13_), channel_id=1, source_target_pairs={{0,4},{2,6},{4,0},{6,2},{8,12},{10,14},{12,8},{14,10},{16,20},{18,... | collective-permute-start | bytes 786440 | tf_op jit(solution)/shard_map/ppermute | solution.py:416
  24.1 7.5 %collective-permute-start.4 = (bf16[256,512]{1,0:T(8,128)(2,1)S(1)}, bf16[256,512]{1,0:T(8,128)(2,1)S(1)}, u32[]{:S(2)}, u32[]{:S(2)}) collective-permute-start(bf16[256,512]{1,0:T(8,128)(2,1)S(1)} %collective-permute-done.3.refs_4_.refs_11_), channel_id=1, source_target_pairs={{0,2},{2,0},{4,6},{6,4},{8,10},{10,8},{12,14},{14,12},{16,18},{18,... | collective-permute-start | bytes 786440 | tf_op jit(solution)/shard_map/ppermute | solution.py:416
  24.2 8.0 %collective-permute-start.6 = (bf16[256,512]{1,0:T(8,128)(2,1)S(1)}, bf16[256,512]{1,0:T(8,128)(2,1)S(1)}, u32[]{:S(2)}, u32[]{:S(2)}) collective-permute-start(bf16[256,512]{1,0:T(8,128)(2,1)S(1)} %collective-permute-done.5.refs_6_.refs_13_), channel_id=1, source_target_pairs={{0,2},{2,0},{4,6},{6,4},{8,10},{10,8},{12,14},{14,12},{16,18},{18,... | collective-permute-start | bytes 786440 | tf_op jit(solution)/shard_map/ppermute | solution.py:416
  25.2 20.2 %collective-permute-start.16 = (bf16[256,2048]{1,0:T(8,128)(2,1)S(1)}, bf16[256,2048]{1,0:T(8,128)(2,1)S(1)}, u32[]{:S(2)}, u32[]{:S(2)}) collective-permute-start(bf16[256,2048]{1,0:T(8,128)(2,1)S(1)} %bitcast.7), channel_id=1, source_target_pairs={{0,2},{2,0},{4,6},{6,4},{8,10},{10,8},{12,14},{14,12},{16,18},{18,... | collective-permute-start | bytes 3145736 | tf_op jit(solution)/shard_map/ppermute | solution.py:416
  31.0 3.5 %collective-permute-start.8 = (bf16[256,512]{1,0:T(8,128)(2,1)S(1)}, bf16[256,512]{1,0:T(8,128)(2,1)S(1)}, u32[]{:S(2)}, u32[]{:S(2)}) collective-permute-start(bf16[256,512]{1,0:T(8,128)(2,1)S(1)} %collective-permute-done.7.refs_8_.refs_15_), channel_id=1, source_target_pairs={{0,2},{2,0},{4,6},{6,4},{8,10},{10,8},{12,14},{14,12},{16,18},{18,... | collective-permute-start | bytes 786440 | tf_op jit(solution)/shard_map/ppermute | solution.py:416
  31.6 2.8 %collective-permute-start.12 = (bf16[256,512]{1,0:T(8,128)(2,1)S(1)}, bf16[256,512]{1,0:T(8,128)(2,1)S(1)}, u32[]{:S(2)}, u32[]{:S(2)}) collective-permute-start(bf16[256,512]{1,0:T(8,128)(2,1)S(1)} %collective-permute-done.10.refs_12_.refs_19_), channel_id=1, source_target_pairs={{0,2},{2,0},{4,6},{6,4},{8,10},{10,8},{12,14},{14,12},{16,18},{18,... | collective-permute-start | bytes 786440 | tf_op jit(solution)/shard_map/ppermute | solution.py:416
  31.6 2.8 %collective-permute-start.11 = (bf16[256,512]{1,0:T(8,128)(2,1)S(1)}, bf16[256,512]{1,0:T(8,128)(2,1)S(1)}, u32[]{:S(2)}, u32[]{:S(2)}) collective-permute-start(bf16[256,512]{1,0:T(8,128)(2,1)S(1)} %collective-permute-done.9.refs_10_.refs_17_), channel_id=1, source_target_pairs={{0,2},{2,0},{4,6},{6,4},{8,10},{10,8},{12,14},{14,12},{16,18},{18,... | collective-permute-start | bytes 786440 | tf_op jit(solution)/shard_map/ppermute | solution.py:416
  32.1 8.3 %collective-permute-start.13 = (bf16[256,512]{1,0:T(8,128)(2,1)S(1)}, bf16[256,512]{1,0:T(8,128)(2,1)S(1)}, u32[]{:S(2)}, u32[]{:S(2)}) collective-permute-start(bf16[256,512]{1,0:T(8,128)(2,1)S(1)} %collective-permute-done.10.refs_12_.refs_19_), channel_id=1, source_target_pairs={{0,4},{2,6},{4,0},{6,2},{8,12},{10,14},{12,8},{14,10},{16,20},{18,... | collective-permute-start | bytes 786440 | tf_op jit(solution)/shard_map/ppermute | solution.py:416
  40.4 1.9 %collective-permute-start.14 = (bf16[256,512]{1,0:T(8,128)(2,1)S(1)}, bf16[256,512]{1,0:T(8,128)(2,1)S(1)}, u32[]{:S(2)}, u32[]{:S(2)}) collective-permute-start(bf16[256,512]{1,0:T(8,128)(2,1)S(1)} %collective-permute-done.13.refs_1_.refs_14_.refs_21_), channel_id=1, source_target_pairs={{0,2},{2,0},{4,6},{6,4},{8,10},{10,8},{12,14},{14,12},{16,18},{18,... | collective-permute-start | bytes 786440 | tf_op jit(solution)/shard_map/ppermute | solution.py:416
  41.8 1.4 %collective-permute-start.15 = (f32[16,256]{1,0:T(8,128)S(1)}, f32[16,256]{1,0:T(8,128)S(1)}, u32[]{:S(2)}, u32[]{:S(2)}) collective-permute-start(f32[16,256]{1,0:T(8,128)S(1)} %partial_den.9.refs_2_), channel_id=1, source_target_pairs={{0,2},{2,0},{4,6},{6,4},{8,10},{10,8},{12,14},{14,12},{16,18},{18,... | collective-permute-start | bytes 49160 | tf_op jit(solution)/shard_map/ppermute | solution.py:416
  45.0 1.6 %collective-permute-start.17 = (bf16[256,512]{1,0:T(8,128)(2,1)S(1)}, bf16[256,512]{1,0:T(8,128)(2,1)S(1)}, u32[]{:S(2)}, u32[]{:S(2)}) collective-permute-start(bf16[256,512]{1,0:T(8,128)(2,1)S(1)} %get-tuple-element.57.refs_2_), channel_id=1, source_target_pairs={{0,2},{2,0},{4,6},{6,4},{8,10},{10,8},{12,14},{14,12},{16,18},{18,... | collective-permute-start | bytes 786440 | tf_op jit(solution)/shard_map/ppermute | solution.py:416
  47.1 6.6 %collective-permute-start.18 = (bf16[128,512]{1,0:T(8,128)(2,1)S(1)}, bf16[128,512]{1,0:T(8,128)(2,1)S(1)}, u32[]{:S(2)}, u32[]{:S(2)}) collective-permute-start(bf16[128,512]{1,0:T(8,128)(2,1)S(1)} %get-tuple-element.60), channel_id=1, source_target_pairs={{0,1},{1,0},{2,3},{3,2},{4,5},{5,4},{6,7},{7,6},{8,9},{9,8},{10,11... | collective-permute-start | bytes 393224 | tf_op jit(solution)/shard_map/ppermute | solution.py:416
  48.6 8.9 %collective-permute-start.19 = (bf16[128,512]{1,0:T(8,128)(2,1)S(1)}, bf16[128,512]{1,0:T(8,128)(2,1)S(1)}, u32[]{:S(2)}, u32[]{:S(2)}) collective-permute-start(bf16[128,512]{1,0:T(8,128)(2,1)S(1)} %get-tuple-element.61), channel_id=1, source_target_pairs={{0,4},{2,6},{4,0},{6,2},{8,12},{10,14},{12,8},{14,10},{16,20},{18,... | collective-permute-start | bytes 393224 | tf_op jit(solution)/shard_map/ppermute | solution.py:416
  49.6 7.9 %collective-permute-start.20 = (bf16[128,512]{1,0:T(8,128)(2,1)S(1)}, bf16[128,512]{1,0:T(8,128)(2,1)S(1)}, u32[]{:S(2)}, u32[]{:S(2)}) collective-permute-start(bf16[128,512]{1,0:T(8,128)(2,1)S(1)} %get-tuple-element.62), channel_id=1, source_target_pairs={{0,5},{1,4},{2,7},{3,6},{4,1},{5,0},{6,3},{7,2},{8,13},{9,12},{10,... | collective-permute-start | bytes 393224 | tf_op jit(solution)/shard_map/ppermute | solution.py:437
  51.1 13.3 %collective-permute-start.22 = (bf16[128,512]{1,0:T(8,128)(2,1)S(1)}, bf16[128,512]{1,0:T(8,128)(2,1)S(1)}, u32[]{:S(2)}, u32[]{:S(2)}) collective-permute-start(bf16[128,512]{1,0:T(8,128)(2,1)S(1)} %get-tuple-element.65), channel_id=1, source_target_pairs={{0,1},{1,0},{2,3},{3,2},{4,5},{5,4},{6,7},{7,6},{8,9},{9,8},{10,11... | collective-permute-start | bytes 393224 | tf_op jit(solution)/shard_map/ppermute | solution.py:416
  52.7 11.8 %collective-permute-start.23 = (bf16[128,512]{1,0:T(8,128)(2,1)S(1)}, bf16[128,512]{1,0:T(8,128)(2,1)S(1)}, u32[]{:S(2)}, u32[]{:S(2)}) collective-permute-start(bf16[128,512]{1,0:T(8,128)(2,1)S(1)} %get-tuple-element.66), channel_id=1, source_target_pairs={{0,4},{2,6},{4,0},{6,2},{8,12},{10,14},{12,8},{14,10},{16,20},{18,... | collective-permute-start | bytes 393224 | tf_op jit(solution)/shard_map/ppermute | solution.py:416
  53.7 10.8 %collective-permute-start.24 = (bf16[128,512]{1,0:T(8,128)(2,1)S(1)}, bf16[128,512]{1,0:T(8,128)(2,1)S(1)}, u32[]{:S(2)}, u32[]{:S(2)}) collective-permute-start(bf16[128,512]{1,0:T(8,128)(2,1)S(1)} %get-tuple-element.67), channel_id=1, source_target_pairs={{0,5},{1,4},{2,7},{3,6},{4,1},{5,0},{6,3},{7,2},{8,13},{9,12},{10,... | collective-permute-start | bytes 393224 | tf_op jit(solution)/shard_map/ppermute | solution.py:437
  57.6 6.8 %collective-permute-start.21 = (bf16[64,512]{1,0:T(8,128)(2,1)S(1)}, bf16[64,512]{1,0:T(8,128)(2,1)S(1)}, u32[]{:S(2)}, u32[]{:S(2)}) collective-permute-start(bf16[64,512]{1,0:T(8,128)(2,1)S(1)} %get-tuple-element.63), channel_id=1, source_target_pairs={{0,16},{2,18},{4,20},{6,22},{8,24},{10,26},{12,28},{14,30},{16,0},... | collective-permute-start | bytes 196616 | tf_op jit(solution)/shard_map/ppermute | solution.py:416
  60.8 6.3 %collective-permute-start.25 = (bf16[64,512]{1,0:T(8,128)(2,1)S(1)}, bf16[64,512]{1,0:T(8,128)(2,1)S(1)}, u32[]{:S(2)}, u32[]{:S(2)}) collective-permute-start(bf16[64,512]{1,0:T(8,128)(2,1)S(1)} %get-tuple-element.69), channel_id=1, source_target_pairs={{0,24},{2,26},{4,28},{6,30},{8,16},{10,18},{12,20},{14,22},{16,8},... | collective-permute-start | bytes 196616 | tf_op jit(solution)/shard_map/ppermute | solution.py:416
  64.6 4.8 %collective-permute-start.26 = (bf16[64,512]{1,0:T(8,128)(2,1)S(1)}, bf16[64,512]{1,0:T(8,128)(2,1)S(1)}, u32[]{:S(2)}, u32[]{:S(2)}) collective-permute-start(bf16[64,512]{1,0:T(8,128)(2,1)S(1)} %get-tuple-element.70), channel_id=1, source_target_pairs={{0,8},{2,10},{4,12},{6,14},{8,0},{10,2},{12,4},{14,6},{16,24},{18,... | collective-permute-start | bytes 196616 | tf_op jit(solution)/shard_map/ppermute | solution.py:416
  69.4 4.8 %collective-permute-start.35 = (bf16[64,512]{1,0:T(8,128)(2,1)S(1)}, bf16[64,512]{1,0:T(8,128)(2,1)S(1)}, u32[]{:S(2)}, u32[]{:S(2)}) collective-permute-start(bf16[64,512]{1,0:T(8,128)(2,1)S(1)} %add_convert_fusion), channel_id=1, source_target_pairs={{0,8},{2,10},{4,12},{6,14},{8,0},{10,2},{12,4},{14,6},{16,24},{18,... | collective-permute-start | bytes 196616 | tf_op jit(solution)/shard_map/ppermute | solution.py:416
  69.5 8.3 %collective-permute-start.28 = (bf16[64,512]{1,0:T(8,128)(2,1)S(1)}, bf16[64,512]{1,0:T(8,128)(2,1)S(1)}, u32[]{:S(2)}, u32[]{:S(2)}) collective-permute-start(bf16[64,512]{1,0:T(8,128)(2,1)S(1)} %add_convert_fusion), channel_id=1, source_target_pairs={{0,24},{2,26},{4,28},{6,30},{8,16},{10,18},{12,20},{14,22},{16,8},... | collective-permute-start | bytes 196616 | tf_op jit(solution)/shard_map/ppermute | solution.py:416
  72.0 5.8 %collective-permute-start.27 = (bf16[64,512]{1,0:T(8,128)(2,1)S(1)}, bf16[64,512]{1,0:T(8,128)(2,1)S(1)}, u32[]{:S(2)}, u32[]{:S(2)}) collective-permute-start(bf16[64,512]{1,0:T(8,128)(2,1)S(1)} %add_convert_fusion), channel_id=1, source_target_pairs={{0,16},{2,18},{4,20},{6,22},{8,24},{10,26},{12,28},{14,30},{16,0},... | collective-permute-start | bytes 196616 | tf_op jit(solution)/shard_map/ppermute | solution.py:416
  74.2 6.3 %collective-permute-start.36 = (bf16[2,64,512]{2,1,0:T(8,128)(2,1)S(1)}, bf16[2,64,512]{2,1,0:T(8,128)(2,1)S(1)}, u32[]{:S(2)}, u32[]{:S(2)}) collective-permute-start(bf16[2,64,512]{2,1,0:T(8,128)(2,1)S(1)} %pad_maximum_fusion.2), channel_id=1, source_target_pairs={{0,1},{1,0},{2,3},{3,2},{4,5},{5,4},{6,7},{7,6},{8,9},{9,8},{10,11... | collective-permute-start | bytes 393224 | tf_op jit(solution)/shard_map/ppermute | solution.py:416
  74.7 7.7 %collective-permute-start.37 = (bf16[2,64,512]{2,1,0:T(8,128)(2,1)S(1)}, bf16[2,64,512]{2,1,0:T(8,128)(2,1)S(1)}, u32[]{:S(2)}, u32[]{:S(2)}) collective-permute-start(bf16[2,64,512]{2,1,0:T(8,128)(2,1)S(1)} %pad_maximum_fusion.2), channel_id=1, source_target_pairs={{0,4},{2,6},{4,0},{6,2},{8,12},{10,14},{12,8},{14,10},{16,20},{18,... | collective-permute-start | bytes 393224 | tf_op jit(solution)/shard_map/ppermute | solution.py:416
  76.0 6.2 %collective-permute-start.38 = (bf16[2,64,512]{2,1,0:T(8,128)(2,1)S(1)}, bf16[2,64,512]{2,1,0:T(8,128)(2,1)S(1)}, u32[]{:S(2)}, u32[]{:S(2)}) collective-permute-start(bf16[2,64,512]{2,1,0:T(8,128)(2,1)S(1)} %pad_maximum_fusion.2), channel_id=1, source_target_pairs={{0,5},{1,4},{2,7},{3,6},{4,1},{5,0},{6,3},{7,2},{8,13},{9,12},{10,... | collective-permute-start | bytes 393224 | tf_op jit(solution)/shard_map/ppermute | solution.py:437
  77.8 5.7 %collective-permute-start.29 = (bf16[2,64,512]{2,1,0:T(8,128)(2,1)S(1)}, bf16[2,64,512]{2,1,0:T(8,128)(2,1)S(1)}, u32[]{:S(2)}, u32[]{:S(2)}) collective-permute-start(bf16[2,64,512]{2,1,0:T(8,128)(2,1)S(1)} %pad_maximum_fusion.1), channel_id=1, source_target_pairs={{0,1},{1,0},{2,3},{3,2},{4,5},{5,4},{6,7},{7,6},{8,9},{9,8},{10,11... | collective-permute-start | bytes 393224 | tf_op jit(solution)/shard_map/ppermute | solution.py:416
  79.0 5.0 %collective-permute-start.30 = (bf16[2,64,512]{2,1,0:T(8,128)(2,1)S(1)}, bf16[2,64,512]{2,1,0:T(8,128)(2,1)S(1)}, u32[]{:S(2)}, u32[]{:S(2)}) collective-permute-start(bf16[2,64,512]{2,1,0:T(8,128)(2,1)S(1)} %pad_maximum_fusion.1), channel_id=1, source_target_pairs={{0,4},{2,6},{4,0},{6,2},{8,12},{10,14},{12,8},{14,10},{16,20},{18,... | collective-permute-start | bytes 393224 | tf_op jit(solution)/shard_map/ppermute | solution.py:416
  80.5 5.9 %collective-permute-start.31 = (bf16[2,64,512]{2,1,0:T(8,128)(2,1)S(1)}, bf16[2,64,512]{2,1,0:T(8,128)(2,1)S(1)}, u32[]{:S(2)}, u32[]{:S(2)}) collective-permute-start(bf16[2,64,512]{2,1,0:T(8,128)(2,1)S(1)} %pad_maximum_fusion.1), channel_id=1, source_target_pairs={{0,5},{1,4},{2,7},{3,6},{4,1},{5,0},{6,3},{7,2},{8,13},{9,12},{10,... | collective-permute-start | bytes 393224 | tf_op jit(solution)/shard_map/ppermute | solution.py:437
  82.2 4.3 %collective-permute-start.39 = (bf16[2,64,512]{2,1,0:T(8,128)(2,1)S(1)}, bf16[2,64,512]{2,1,0:T(8,128)(2,1)S(1)}, u32[]{:S(2)}, u32[]{:S(2)}) collective-permute-start(bf16[2,64,512]{2,1,0:T(8,128)(2,1)S(1)} %collective-permute-done.36.refs_1_), channel_id=1, source_target_pairs={{0,2},{2,0},{4,6},{6,4},{8,10},{10,8},{12,14},{14,12},{16,18},{18,... | collective-permute-start | bytes 393224 | tf_op jit(solution)/shard_map/ppermute | solution.py:416
  82.4 5.3 %collective-permute-start.42 = (bf16[4,64,512]{2,1,0:T(8,128)(2,1)S(1)}, bf16[4,64,512]{2,1,0:T(8,128)(2,1)S(1)}, u32[]{:S(2)}, u32[]{:S(2)}) collective-permute-start(bf16[4,64,512]{2,1,0:T(8,128)(2,1)S(1)} %pad_maximum_fusion.refs_0_), channel_id=1, source_target_pairs={{0,2},{2,0},{4,6},{6,4},{8,10},{10,8},{12,14},{14,12},{16,18},{18,... | collective-permute-start | bytes 786440 | tf_op jit(solution)/shard_map/ppermute | solution.py:416
  83.5 3.4 %collective-permute-start.40 = (bf16[2,64,512]{2,1,0:T(8,128)(2,1)S(1)}, bf16[2,64,512]{2,1,0:T(8,128)(2,1)S(1)}, u32[]{:S(2)}, u32[]{:S(2)}) collective-permute-start(bf16[2,64,512]{2,1,0:T(8,128)(2,1)S(1)} %collective-permute-done.37.refs_2_), channel_id=1, source_target_pairs={{0,2},{2,0},{4,6},{6,4},{8,10},{10,8},{12,14},{14,12},{16,18},{18,... | collective-permute-start | bytes 393224 | tf_op jit(solution)/shard_map/ppermute | solution.py:416
  84.0 5.5 %collective-permute-start.32 = (bf16[2,64,512]{2,1,0:T(8,128)(2,1)S(1)}, bf16[2,64,512]{2,1,0:T(8,128)(2,1)S(1)}, u32[]{:S(2)}, u32[]{:S(2)}) collective-permute-start(bf16[2,64,512]{2,1,0:T(8,128)(2,1)S(1)} %collective-permute-done.29.refs_0_), channel_id=1, source_target_pairs={{0,2},{2,0},{4,6},{6,4},{8,10},{10,8},{12,14},{14,12},{16,18},{18,... | collective-permute-start | bytes 393224 | tf_op jit(solution)/shard_map/ppermute | solution.py:416
  86.4 1.3 %collective-permute-start.41 = (bf16[2,64,512]{2,1,0:T(8,128)(2,1)S(1)}, bf16[2,64,512]{2,1,0:T(8,128)(2,1)S(1)}, u32[]{:S(2)}, u32[]{:S(2)}) collective-permute-start(bf16[2,64,512]{2,1,0:T(8,128)(2,1)S(1)} %collective-permute-done.38.refs_3_), channel_id=1, source_target_pairs={{0,2},{2,0},{4,6},{6,4},{8,10},{10,8},{12,14},{14,12},{16,18},{18,... | collective-permute-start | bytes 393224 | tf_op jit(solution)/shard_map/ppermute | solution.py:416
  86.4 3.0 %collective-permute-start.33 = (bf16[2,64,512]{2,1,0:T(8,128)(2,1)S(1)}, bf16[2,64,512]{2,1,0:T(8,128)(2,1)S(1)}, u32[]{:S(2)}, u32[]{:S(2)}) collective-permute-start(bf16[2,64,512]{2,1,0:T(8,128)(2,1)S(1)} %collective-permute-done.30.refs_1_), channel_id=1, source_target_pairs={{0,2},{2,0},{4,6},{6,4},{8,10},{10,8},{12,14},{14,12},{16,18},{18,... | collective-permute-start | bytes 393224 | tf_op jit(solution)/shard_map/ppermute | solution.py:416
  86.9 2.5 %collective-permute-start.34 = (bf16[2,64,512]{2,1,0:T(8,128)(2,1)S(1)}, bf16[2,64,512]{2,1,0:T(8,128)(2,1)S(1)}, u32[]{:S(2)}, u32[]{:S(2)}) collective-permute-start(bf16[2,64,512]{2,1,0:T(8,128)(2,1)S(1)} %collective-permute-done.31.refs_2_), channel_id=1, source_target_pairs={{0,2},{2,0},{4,6},{6,4},{8,10},{10,8},{12,14},{14,12},{16,18},{18,... | collective-permute-start | bytes 393224 | tf_op jit(solution)/shard_map/ppermute | solution.py:416

commit v4 on v3

--- a/solution.py
+++ b/solution.py
@@ -464,7 +464,7 @@
         near_y = blk_swap(gate(near, over_y), Y)
         use(pair(near, Z0))
         far_y = blk_swap(gate(far, dens[1]), Y)
-        use(pair(over_y, Y), pair(far, 2 * Z0))
+        use(pair(over_y, Y), pair(far, 2 * Z0, near_y))
         mid_y = blk_swap(mid, Y)
         use(pair(near_y, Z0 | Y), pair(far_y, 2 * Z0 | Y, mid), pair(mid, 3 * Z0))
         (pos,) = take_row(0)

time: 91 us -> 91 us (level)
  no operation moved by 1% of the time
where the time goes in v4:
time: 91 us; the launch traced here: 90.9 us
  starting transfers between devices  37.5 us (41%)
  waiting for transfers between devices  34.1 us (37%)
  Pallas kernels  18.1 us (20%)
  between operations  0.98 us (1%)
    ppermute x39, starting transfers between devices, swap(): return lax.ppermute(x, axis, [(i, i ^ mask) for i in range(size)])  32.1 us
    ppermute x39, waiting for transfers between devices, swap(): return lax.ppermute(x, axis, [(i, i ^ mask) for i in range(size)])  31.1 us
    pallas_call x5, Pallas kernels, partial_den(): pl.pallas_call(functools.partial(den_kernel, len(old), n_new, before is N...  6.88 us
    ppermute x4, starting transfers between devices, both_swap(): return lax.ppermute(x, ('blk', 'group'), moves)  5.44 us
    ppermute x4, waiting for transfers between devices, both_swap(): return lax.ppermute(x, ('blk', 'group'), moves)  3.04 us
    pallas_call x2, Pallas kernels, place(): pl.pallas_call(functools.partial(place_kernel, plan, planes), in_specs=[V...  2.92 us
    pallas_call x1, Pallas kernels, project(): pl.pallas_call(project_kernel, in_specs=[ANY] * 2, out_specs=[VMEM] * 2,...  2.46 us
    pallas_call x2, Pallas kernels, own_row(): pl.pallas_call(functools.partial(row_kernel, rs, first), in_specs=[VMEM]...  2.06 us
  transfers between devices with their start and end apart: 43, of which 20 were waited for; matrix products, arithmetic and copies ran while one was open for 0% of the time, Pallas kernels for 15%

profile of v4, /device:TPU:0, one launch (start us, length us, event | category | flops | bytes accessed | tf_op | source)
XLA Modules:
  0.0 90.9 jit_solution(2596342820920948266)
XLA Ops:
  0.7 2.5 %project.1 = (f32[256,512]{1,0:T(8,128)S(1)}, bf16[256,512]{1,0:T(8,128)(2,1)S(1)}) custom-call(bf16[256,2048]{1,0:T(8,128)(2,1)} %bitcast.6, bf16[2048,512]{1,0:T(8,128)(2,1)} %w_hbm.1), custom_call_target="tpu_custom_call" | custom-call | flops 536870912 | bytes 3145728 | tf_op jit(solution)/shard_map/project/pallas_call | solution.py:61
  3.1 3.1 %collective-permute-start.1 = (bf16[256,512]{1,0:T(8,128)(2,1)S(1)}, bf16[256,512]{1,0:T(8,128)(2,1)S(1)}, u32[]{:S(2)}, u32[]{:S(2)}) collective-permute-start(bf16[256,512]{1,0:T(8,128)(2,1)S(1)} %get-tuple-element.40.refs_0_.x_ref.refs_7_), channel_id=1, source_target_pairs={{0,8},{2,10},{4,12},{6,14},{8,0},{10,2},{12,4},{14,6},{16,24},{18,... | collective-permute-start | bytes 786440 | tf_op jit(solution)/shard_map/ppermute | solution.py:416
  6.2 1.5 %collective-permute-start.3 = (bf16[256,512]{1,0:T(8,128)(2,1)S(1)}, bf16[256,512]{1,0:T(8,128)(2,1)S(1)}, u32[]{:S(2)}, u32[]{:S(2)}) collective-permute-start(bf16[256,512]{1,0:T(8,128)(2,1)S(1)} %get-tuple-element.40.refs_0_.x_ref.refs_7_), channel_id=1, source_target_pairs={{0,4},{2,6},{4,0},{6,2},{8,12},{10,14},{12,8},{14,10},{16,20},{18,... | collective-permute-start | bytes 786440 | tf_op jit(solution)/shard_map/ppermute | solution.py:416
  7.7 2.6 %collective-permute-start.5 = (bf16[256,512]{1,0:T(8,128)(2,1)S(1)}, bf16[256,512]{1,0:T(8,128)(2,1)S(1)}, u32[]{:S(2)}, u32[]{:S(2)}) collective-permute-start(bf16[256,512]{1,0:T(8,128)(2,1)S(1)} %get-tuple-element.40.refs_0_.x_ref.refs_7_), channel_id=1, source_target_pairs={{0,16},{2,18},{4,20},{6,22},{8,24},{10,26},{12,28},{14,30},{16,0},... | collective-permute-start | bytes 786440 | tf_op jit(solution)/shard_map/ppermute | solution.py:416
  10.3 4.7 %collective-permute-done.1.refs_2_.refs_9_ = bf16[256,512]{1,0:T(8,128)(2,1)S(1)} collective-permute-done((bf16[256,512]{1,0:T(8,128)(2,1)S(1)}, bf16[256,512]{1,0:T(8,128)(2,1)S(1)}, u32[]{:S(2)}, u32[]{:S(2)}) %collective-permute-start.1) | collective-permute-done | bytes 262176 | tf_op jit(solution)/shard_map/ppermute | solution.py:416
  15.0 3.3 %collective-permute-start.6 = (bf16[256,512]{1,0:T(8,128)(2,1)S(1)}, bf16[256,512]{1,0:T(8,128)(2,1)S(1)}, u32[]{:S(2)}, u32[]{:S(2)}) collective-permute-start(bf16[256,512]{1,0:T(8,128)(2,1)S(1)} %collective-permute-done.1.refs_2_.refs_9_), channel_id=1, source_target_pairs={{0,4},{2,6},{4,0},{6,2},{8,12},{10,14},{12,8},{14,10},{16,20},{18,... | collective-permute-start | bytes 786440 | tf_op jit(solution)/shard_map/ppermute | solution.py:416
  18.2 0.5 partial_den.5.refs_4_
  18.7 4.3 %collective-permute-done.5.refs_6_.refs_13_ = bf16[256,512]{1,0:T(8,128)(2,1)S(1)} collective-permute-done((bf16[256,512]{1,0:T(8,128)(2,1)S(1)}, bf16[256,512]{1,0:T(8,128)(2,1)S(1)}, u32[]{:S(2)}, u32[]{:S(2)}) %collective-permute-start.5) | collective-permute-done | bytes 262176 | tf_op jit(solution)/shard_map/ppermute | solution.py:416
  23.0 0.6 partial_den.6.refs_8_
  23.6 0.5 collective-permute-start.9
  24.2 1.1 %collective-permute-done.6.refs_8_.refs_15_ = bf16[256,512]{1,0:T(8,128)(2,1)S(1)} collective-permute-done((bf16[256,512]{1,0:T(8,128)(2,1)S(1)}, bf16[256,512]{1,0:T(8,128)(2,1)S(1)}, u32[]{:S(2)}, u32[]{:S(2)}) %collective-permute-start.6) | collective-permute-done | bytes 262176 | tf_op jit(solution)/shard_map/ppermute | solution.py:416
  25.2 0.5 collective-permute-start.16
  25.7 5.2 %collective-permute-done.10.refs_12_.refs_19_ = bf16[256,512]{1,0:T(8,128)(2,1)S(1)} collective-permute-done((bf16[256,512]{1,0:T(8,128)(2,1)S(1)}, bf16[256,512]{1,0:T(8,128)(2,1)S(1)}, u32[]{:S(2)}, u32[]{:S(2)}) %collective-permute-start.10) | collective-permute-done | bytes 262176 | tf_op jit(solution)/shard_map/ppermute | solution.py:416
  31.0 0.6 collective-permute-done.9.refs_10_.refs_17_
  31.6 0.5 collective-permute-start.11
  32.1 1.0 %collective-permute-start.13 = (bf16[256,512]{1,0:T(8,128)(2,1)S(1)}, bf16[256,512]{1,0:T(8,128)(2,1)S(1)}, u32[]{:S(2)}, u32[]{:S(2)}) collective-permute-start(bf16[256,512]{1,0:T(8,128)(2,1)S(1)} %collective-permute-done.10.refs_12_.refs_19_), channel_id=1, source_target_pairs={{0,4},{2,6},{4,0},{6,2},{8,12},{10,14},{12,8},{14,10},{16,20},{18,... | collective-permute-start | bytes 786440 | tf_op jit(solution)/shard_map/ppermute | solution.py:416
  33.1 1.3 %partial_den.7.refs_14_ = f32[16,256]{1,0:T(8,128)S(1)} custom-call(bf16[256,512]{1,0:T(8,128)(2,1)S(1)} %get-tuple-element.40.refs_0_.x_ref.refs_7_, bf16[256,512]{1,0:T(8,128)(2,1)S(1)} %collective-permute-done.refs_1_.refs_8_, bf16[256,512]{1,0:T(8,128)(2,1)S(1)} %collective-permute-done.1.refs_2_.refs_9_, ...), custom_call_target="tpu_custom_call" | custom-call | tf_op jit(solution)/shard_map/partial_den/pallas_call | solution.py:142
  34.5 1.5 %own_row.2 = (f32[256,3584]{1,0:T(8,128)S(1)}, f32[1,256]{1,0:T(1,128)S(1)}) custom-call(s32[1,256]{1,0:T(1,128)S(1)} %copy-done.1, bf16[256,512]{1,0:T(8,128)(2,1)S(1)} %get-tuple-element.40.refs_0_.x_ref.refs_7_, bf16[256,512]{1,0:T(8,128)(2,1)S(1)} %get-tuple-element.40.refs_0_.x_ref.refs_7_, bf16[256,512]{1,0:T(8,128)(2,1)S(1)} %collective-permute-done.refs_1_.refs_8_, ...), custom_call_target="tpu_custom_call" | custom-call | tf_op jit(solution)/shard_map/own_row/pallas_call | solution.py:208
  36.0 3.1 %partial_den.8.refs_15_ = f32[16,256]{1,0:T(8,128)S(1)} custom-call(bf16[256,512]{1,0:T(8,128)(2,1)S(1)} %get-tuple-element.40.refs_0_.x_ref.refs_7_, bf16[256,512]{1,0:T(8,128)(2,1)S(1)} %collective-permute-done.refs_1_.refs_8_, bf16[256,512]{1,0:T(8,128)(2,1)S(1)} %collective-permute-done.1.refs_2_.refs_9_, ...), custom_call_target="tpu_custom_call" | custom-call | tf_op jit(solution)/shard_map/partial_den/pallas_call | solution.py:142
  39.1 1.3 %collective-permute-done.13.refs_1_.refs_14_.refs_21_ = bf16[256,512]{1,0:T(8,128)(2,1)S(1)} collective-permute-done((bf16[256,512]{1,0:T(8,128)(2,1)S(1)}, bf16[256,512]{1,0:T(8,128)(2,1)S(1)}, u32[]{:S(2)}, u32[]{:S(2)}) %collective-permute-start.13) | collective-permute-done | bytes 262176 | tf_op jit(solution)/shard_map/ppermute | solution.py:416
  40.4 1.4 %partial_den.9.refs_2_ = f32[16,256]{1,0:T(8,128)S(1)} custom-call(bf16[256,512]{1,0:T(8,128)(2,1)S(1)} %get-tuple-element.40.refs_0_.x_ref.refs_7_, bf16[256,512]{1,0:T(8,128)(2,1)S(1)} %collective-permute-done.refs_1_.refs_8_, bf16[256,512]{1,0:T(8,128)(2,1)S(1)} %collective-permute-done.1.refs_2_.refs_9_, ...), custom_call_target="tpu_custom_call" | custom-call | tf_op jit(solution)/shard_map/partial_den/pallas_call | solution.py:142
  41.8 0.5 collective-permute-start.15
  42.3 0.5 own_row.3
  42.9 0.3 collective-permute-done.15.refs_3_
  43.2 1.8 %gradient.1 = (f32[1,256]{1,0:T(1,128)S(1)}, f32[256,512]{1,0:T(8,128)S(1)}, bf16[256,512]{1,0:T(8,128)(2,1)S(1)}) custom-call(s32[1,256]{1,0:T(1,128)S(1)} %copy-done.1, f32[256,512]{1,0:T(8,128)S(1)} %get-tuple-element.49.refs_1_, f32[16,256]{1,0:T(8,128)S(1)} %partial_den.9.refs_2_, f32[16,256]{1,0:T(8,128)S(1)} %collective-permute-done.15.refs_3_, ...), custom_call_target="tpu_custom_call" | custom-call | flops 1073741824 | bytes 12582912 | tf_op jit(solution)/shard_map/gradient/pallas_call | solution.py:268
  45.0 0.4 collective-permute-start.17
  45.4 1.2 %collective-permute-done.17.refs_3_ = bf16[256,512]{1,0:T(8,128)(2,1)S(1)} collective-permute-done((bf16[256,512]{1,0:T(8,128)(2,1)S(1)}, bf16[256,512]{1,0:T(8,128)(2,1)S(1)}, u32[]{:S(2)}, u32[]{:S(2)}) %collective-permute-start.17) | collective-permute-done | bytes 262176 | tf_op jit(solution)/shard_map/ppermute | solution.py:416
  46.6 0.5 head_partial.2
  47.1 1.6 %collective-permute-start.18 = (bf16[128,512]{1,0:T(8,128)(2,1)S(1)}, bf16[128,512]{1,0:T(8,128)(2,1)S(1)}, u32[]{:S(2)}, u32[]{:S(2)}) collective-permute-start(bf16[128,512]{1,0:T(8,128)(2,1)S(1)} %get-tuple-element.62), channel_id=1, source_target_pairs={{0,1},{1,0},{2,3},{3,2},{4,5},{5,4},{6,7},{7,6},{8,9},{9,8},{10,11... | collective-permute-start | bytes 393224 | tf_op jit(solution)/shard_map/ppermute | solution.py:416
  48.6 1.0 %collective-permute-start.19 = (bf16[128,512]{1,0:T(8,128)(2,1)S(1)}, bf16[128,512]{1,0:T(8,128)(2,1)S(1)}, u32[]{:S(2)}, u32[]{:S(2)}) collective-permute-start(bf16[128,512]{1,0:T(8,128)(2,1)S(1)} %get-tuple-element.63), channel_id=1, source_target_pairs={{0,4},{2,6},{4,0},{6,2},{8,12},{10,14},{12,8},{14,10},{16,20},{18,... | collective-permute-start | bytes 393224 | tf_op jit(solution)/shard_map/ppermute | solution.py:416
  49.6 1.0 %collective-permute-start.20 = (bf16[128,512]{1,0:T(8,128)(2,1)S(1)}, bf16[128,512]{1,0:T(8,128)(2,1)S(1)}, u32[]{:S(2)}, u32[]{:S(2)}) collective-permute-start(bf16[128,512]{1,0:T(8,128)(2,1)S(1)} %get-tuple-element.64), channel_id=1, source_target_pairs={{0,5},{1,4},{2,7},{3,6},{4,1},{5,0},{6,3},{7,2},{8,13},{9,12},{10,... | collective-permute-start | bytes 393224 | tf_op jit(solution)/shard_map/ppermute | solution.py:437
  50.6 0.5 head_partial.3
  51.1 1.5 %collective-permute-start.22 = (bf16[128,512]{1,0:T(8,128)(2,1)S(1)}, bf16[128,512]{1,0:T(8,128)(2,1)S(1)}, u32[]{:S(2)}, u32[]{:S(2)}) collective-permute-start(bf16[128,512]{1,0:T(8,128)(2,1)S(1)} %get-tuple-element.67), channel_id=1, source_target_pairs={{0,1},{1,0},{2,3},{3,2},{4,5},{5,4},{6,7},{7,6},{8,9},{9,8},{10,11... | collective-permute-start | bytes 393224 | tf_op jit(solution)/shard_map/ppermute | solution.py:416
  52.7 1.0 %collective-permute-start.23 = (bf16[128,512]{1,0:T(8,128)(2,1)S(1)}, bf16[128,512]{1,0:T(8,128)(2,1)S(1)}, u32[]{:S(2)}, u32[]{:S(2)}) collective-permute-start(bf16[128,512]{1,0:T(8,128)(2,1)S(1)} %get-tuple-element.68), channel_id=1, source_target_pairs={{0,4},{2,6},{4,0},{6,2},{8,12},{10,14},{12,8},{14,10},{16,20},{18,... | collective-permute-start | bytes 393224 | tf_op jit(solution)/shard_map/ppermute | solution.py:416
  53.7 1.7 %collective-permute-start.24 = (bf16[128,512]{1,0:T(8,128)(2,1)S(1)}, bf16[128,512]{1,0:T(8,128)(2,1)S(1)}, u32[]{:S(2)}, u32[]{:S(2)}) collective-permute-start(bf16[128,512]{1,0:T(8,128)(2,1)S(1)} %get-tuple-element.69), channel_id=1, source_target_pairs={{0,5},{1,4},{2,7},{3,6},{4,1},{5,0},{6,3},{7,2},{8,13},{9,12},{10,... | collective-permute-start | bytes 393224 | tf_op jit(solution)/shard_map/ppermute | solution.py:437
  55.4 0.8 hand_out.1
  56.2 1.3 %collective-permute-done.19.from_y = bf16[128,512]{1,0:T(8,128)(2,1)S(1)} collective-permute-done((bf16[128,512]{1,0:T(8,128)(2,1)S(1)}, bf16[128,512]{1,0:T(8,128)(2,1)S(1)}, u32[]{:S(2)}, u32[]{:S(2)}) %collective-permute-start.19) | collective-permute-done | bytes 131104 | tf_op jit(solution)/shard_map/ppermute | solution.py:416
  57.6 3.2 %collective-permute-start.21 = (bf16[64,512]{1,0:T(8,128)(2,1)S(1)}, bf16[64,512]{1,0:T(8,128)(2,1)S(1)}, u32[]{:S(2)}, u32[]{:S(2)}) collective-permute-start(bf16[64,512]{1,0:T(8,128)(2,1)S(1)} %get-tuple-element.65), channel_id=1, source_target_pairs={{0,16},{2,18},{4,20},{6,22},{8,24},{10,26},{12,28},{14,30},{16,0},... | collective-permute-start | bytes 196616 | tf_op jit(solution)/shard_map/ppermute | solution.py:416
  60.8 1.3 %collective-permute-start.25 = (bf16[64,512]{1,0:T(8,128)(2,1)S(1)}, bf16[64,512]{1,0:T(8,128)(2,1)S(1)}, u32[]{:S(2)}, u32[]{:S(2)}) collective-permute-start(bf16[64,512]{1,0:T(8,128)(2,1)S(1)} %get-tuple-element.71), channel_id=1, source_target_pairs={{0,24},{2,26},{4,28},{6,30},{8,16},{10,18},{12,20},{14,22},{16,8},... | collective-permute-start | bytes 196616 | tf_op jit(solution)/shard_map/ppermute | solution.py:416
  62.1 2.3 %collective-permute-done.21 = bf16[64,512]{1,0:T(8,128)(2,1)S(1)} collective-permute-done((bf16[64,512]{1,0:T(8,128)(2,1)S(1)}, bf16[64,512]{1,0:T(8,128)(2,1)S(1)}, u32[]{:S(2)}, u32[]{:S(2)}) %collective-permute-start.21) | collective-permute-done | bytes 65568 | tf_op jit(solution)/shard_map/ppermute | solution.py:416
  64.5 0.1 deal.3
  64.6 0.6 collective-permute-start.26
  65.1 2.0 %collective-permute-done.25 = bf16[64,512]{1,0:T(8,128)(2,1)S(1)} collective-permute-done((bf16[64,512]{1,0:T(8,128)(2,1)S(1)}, bf16[64,512]{1,0:T(8,128)(2,1)S(1)}, u32[]{:S(2)}, u32[]{:S(2)}) %collective-permute-start.25) | collective-permute-done | bytes 65568 | tf_op jit(solution)/shard_map/ppermute | solution.py:416
  67.1 2.3 %collective-permute-done.26 = bf16[64,512]{1,0:T(8,128)(2,1)S(1)} collective-permute-done((bf16[64,512]{1,0:T(8,128)(2,1)S(1)}, bf16[64,512]{1,0:T(8,128)(2,1)S(1)}, u32[]{:S(2)}, u32[]{:S(2)}) %collective-permute-start.26) | collective-permute-done | bytes 65568 | tf_op jit(solution)/shard_map/ppermute | solution.py:416
  69.5 2.5 %collective-permute-start.28 = (bf16[64,512]{1,0:T(8,128)(2,1)S(1)}, bf16[64,512]{1,0:T(8,128)(2,1)S(1)}, u32[]{:S(2)}, u32[]{:S(2)}) collective-permute-start(bf16[64,512]{1,0:T(8,128)(2,1)S(1)} %add_convert_fusion), channel_id=1, source_target_pairs={{0,24},{2,26},{4,28},{6,30},{8,16},{10,18},{12,20},{14,22},{16,8},... | collective-permute-start | bytes 196616 | tf_op jit(solution)/shard_map/ppermute | solution.py:416
  72.0 1.0 %collective-permute-start.27 = (bf16[64,512]{1,0:T(8,128)(2,1)S(1)}, bf16[64,512]{1,0:T(8,128)(2,1)S(1)}, u32[]{:S(2)}, u32[]{:S(2)}) collective-permute-start(bf16[64,512]{1,0:T(8,128)(2,1)S(1)} %add_convert_fusion), channel_id=1, source_target_pairs={{0,16},{2,18},{4,20},{6,22},{8,24},{10,26},{12,28},{14,30},{16,0},... | collective-permute-start | bytes 196616 | tf_op jit(solution)/shard_map/ppermute | solution.py:416
  73.0 1.2 %collective-permute-done.35 = bf16[64,512]{1,0:T(8,128)(2,1)S(1)} collective-permute-done((bf16[64,512]{1,0:T(8,128)(2,1)S(1)}, bf16[64,512]{1,0:T(8,128)(2,1)S(1)}, u32[]{:S(2)}, u32[]{:S(2)}) %collective-permute-start.35) | collective-permute-done | bytes 65568 | tf_op jit(solution)/shard_map/ppermute | solution.py:416
  74.2 0.4 collective-permute-start.36
  74.7 1.3 %collective-permute-start.37 = (bf16[2,64,512]{2,1,0:T(8,128)(2,1)S(1)}, bf16[2,64,512]{2,1,0:T(8,128)(2,1)S(1)}, u32[]{:S(2)}, u32[]{:S(2)}) collective-permute-start(bf16[2,64,512]{2,1,0:T(8,128)(2,1)S(1)} %pad_maximum_fusion.2), channel_id=1, source_target_pairs={{0,4},{2,6},{4,0},{6,2},{8,12},{10,14},{12,8},{14,10},{16,20},{18,... | collective-permute-start | bytes 393224 | tf_op jit(solution)/shard_map/ppermute | solution.py:416
  76.0 1.8 %collective-permute-start.38 = (bf16[2,64,512]{2,1,0:T(8,128)(2,1)S(1)}, bf16[2,64,512]{2,1,0:T(8,128)(2,1)S(1)}, u32[]{:S(2)}, u32[]{:S(2)}) collective-permute-start(bf16[2,64,512]{2,1,0:T(8,128)(2,1)S(1)} %pad_maximum_fusion.2), channel_id=1, source_target_pairs={{0,5},{1,4},{2,7},{3,6},{4,1},{5,0},{6,3},{7,2},{8,13},{9,12},{10,... | collective-permute-start | bytes 393224 | tf_op jit(solution)/shard_map/ppermute | solution.py:437
  77.8 1.2 %collective-permute-start.29 = (bf16[2,64,512]{2,1,0:T(8,128)(2,1)S(1)}, bf16[2,64,512]{2,1,0:T(8,128)(2,1)S(1)}, u32[]{:S(2)}, u32[]{:S(2)}) collective-permute-start(bf16[2,64,512]{2,1,0:T(8,128)(2,1)S(1)} %pad_maximum_fusion.1), channel_id=1, source_target_pairs={{0,1},{1,0},{2,3},{3,2},{4,5},{5,4},{6,7},{7,6},{8,9},{9,8},{10,11... | collective-permute-start | bytes 393224 | tf_op jit(solution)/shard_map/ppermute | solution.py:416
  79.0 0.6 collective-permute-start.30
  79.6 0.9 %collective-permute-done.36.refs_1_ = bf16[2,64,512]{2,1,0:T(8,128)(2,1)S(1)} collective-permute-done((bf16[2,64,512]{2,1,0:T(8,128)(2,1)S(1)}, bf16[2,64,512]{2,1,0:T(8,128)(2,1)S(1)}, u32[]{:S(2)}, u32[]{:S(2)}) %collective-permute-start.36) | collective-permute-done | bytes 131104 | tf_op jit(solution)/shard_map/ppermute | solution.py:416
  80.5 0.9 %collective-permute-start.31 = (bf16[2,64,512]{2,1,0:T(8,128)(2,1)S(1)}, bf16[2,64,512]{2,1,0:T(8,128)(2,1)S(1)}, u32[]{:S(2)}, u32[]{:S(2)}) collective-permute-start(bf16[2,64,512]{2,1,0:T(8,128)(2,1)S(1)} %pad_maximum_fusion.1), channel_id=1, source_target_pairs={{0,5},{1,4},{2,7},{3,6},{4,1},{5,0},{6,3},{7,2},{8,13},{9,12},{10,... | collective-permute-start | bytes 393224 | tf_op jit(solution)/shard_map/ppermute | solution.py:437
  81.5 0.7 collective-permute-done.38.refs_3_
  82.2 0.3 collective-permute-done.37.refs_2_
  82.4 0.3 collective-permute-start.42
  82.7 0.9 collective-permute-done.29.refs_0_
  83.5 0.4 collective-permute-done.30.refs_1_
  84.0 2.4 %collective-permute-done.31.refs_2_ = bf16[2,64,512]{2,1,0:T(8,128)(2,1)S(1)} collective-permute-done((bf16[2,64,512]{2,1,0:T(8,128)(2,1)S(1)}, bf16[2,64,512]{2,1,0:T(8,128)(2,1)S(1)}, u32[]{:S(2)}, u32[]{:S(2)}) %collective-permute-start.31) | collective-permute-done | bytes 131104 | tf_op jit(solution)/shard_map/ppermute | solution.py:437
  86.4 0.5 collective-permute-start.33
  87.0 0.8 collective-permute-done.41.refs_6_
  87.8 1.7 %place.2.refs_6_ = f32[2048,512]{1,0:T(8,128)} custom-call(bf16[4,64,512]{2,1,0:T(8,128)(2,1)S(1)} %pad_maximum_fusion.refs_0_, bf16[2,64,512]{2,1,0:T(8,128)(2,1)S(1)} %collective-permute-done.36.refs_1_, bf16[2,64,512]{2,1,0:T(8,128)(2,1)S(1)} %collective-permute-done.37.refs_2_, bf16[2,64,512]{2,1,0:T(8,128)(2,1)S(1)} %collective-permute-done.38.refs_3_, ...), custom_call_target="tpu_custom_call" | custom-call | tf_op jit(solution)/shard_map/place/pallas_call | solution.py:395
  89.5 1.3 %place.3 = f32[2048,512]{1,0:T(8,128)} custom-call(bf16[2,64,512]{2,1,0:T(8,128)(2,1)S(1)} %collective-permute-done.29.refs_0_, bf16[2,64,512]{2,1,0:T(8,128)(2,1)S(1)} %collective-permute-done.30.refs_1_, bf16[2,64,512]{2,1,0:T(8,128)(2,1)S(1)} %collective-permute-done.31.refs_2_, ...), custom_call_target="tpu_custom_call", output_to_operand_aliasing={{}: (6, {})} | custom-call | tf_op jit(solution)/shard_map/place/pallas_call | solution.py:395
  (46 shorter events, 0.5 us)
Async XLA Ops:
  0.6 24.6 %copy-start = (bf16[1,256,2048]{2,1,0:T(8,128)(2,1)S(1)}, bf16[1,256,2048]{2,1,0:T(8,128)(2,1)}, u32[]{:S(2)}) copy-start(bf16[1,256,2048]{2,1,0:T(8,128)(2,1)} %param.3) | copy-start | bytes 3145732
  0.6 33.8 %copy-start.1 = (s32[1,256]{1,0:T(1,128)S(1)}, s32[1,256]{1,0:T(1,128)}, u32[]{:S(2)}) copy-start(s32[1,256]{1,0:T(1,128)} %refs_0_.1) | copy-start | bytes 3076
  3.1 11.9 %collective-permute-start.1 = (bf16[256,512]{1,0:T(8,128)(2,1)S(1)}, bf16[256,512]{1,0:T(8,128)(2,1)S(1)}, u32[]{:S(2)}, u32[]{:S(2)}) collective-permute-start(bf16[256,512]{1,0:T(8,128)(2,1)S(1)} %get-tuple-element.40.refs_0_.x_ref.refs_7_), channel_id=1, source_target_pairs={{0,8},{2,10},{4,12},{6,14},{8,0},{10,2},{12,4},{14,6},{16,24},{18,... | collective-permute-start | bytes 786440 | tf_op jit(solution)/shard_map/ppermute | solution.py:416
  6.2 8.8 %collective-permute-start.3 = (bf16[256,512]{1,0:T(8,128)(2,1)S(1)}, bf16[256,512]{1,0:T(8,128)(2,1)S(1)}, u32[]{:S(2)}, u32[]{:S(2)}) collective-permute-start(bf16[256,512]{1,0:T(8,128)(2,1)S(1)} %get-tuple-element.40.refs_0_.x_ref.refs_7_), channel_id=1, source_target_pairs={{0,4},{2,6},{4,0},{6,2},{8,12},{10,14},{12,8},{14,10},{16,20},{18,... | collective-permute-start | bytes 786440 | tf_op jit(solution)/shard_map/ppermute | solution.py:416
  7.7 10.5 %collective-permute-start = (bf16[256,512]{1,0:T(8,128)(2,1)S(1)}, bf16[256,512]{1,0:T(8,128)(2,1)S(1)}, u32[]{:S(2)}, u32[]{:S(2)}) collective-permute-start(bf16[256,512]{1,0:T(8,128)(2,1)S(1)} %get-tuple-element.40.refs_0_.x_ref.refs_7_), channel_id=1, source_target_pairs={{0,2},{2,0},{4,6},{6,4},{8,10},{10,8},{12,14},{14,12},{16,18},{18,... | collective-permute-start | bytes 786440 | tf_op jit(solution)/shard_map/ppermute | solution.py:416
  7.7 15.3 %collective-permute-start.5 = (bf16[256,512]{1,0:T(8,128)(2,1)S(1)}, bf16[256,512]{1,0:T(8,128)(2,1)S(1)}, u32[]{:S(2)}, u32[]{:S(2)}) collective-permute-start(bf16[256,512]{1,0:T(8,128)(2,1)S(1)} %get-tuple-element.40.refs_0_.x_ref.refs_7_), channel_id=1, source_target_pairs={{0,16},{2,18},{4,20},{6,22},{8,24},{10,26},{12,28},{14,30},{16,0},... | collective-permute-start | bytes 786440 | tf_op jit(solution)/shard_map/ppermute | solution.py:416
  15.0 8.1 %collective-permute-start.2 = (bf16[256,512]{1,0:T(8,128)(2,1)S(1)}, bf16[256,512]{1,0:T(8,128)(2,1)S(1)}, u32[]{:S(2)}, u32[]{:S(2)}) collective-permute-start(bf16[256,512]{1,0:T(8,128)(2,1)S(1)} %collective-permute-done.1.refs_2_.refs_9_), channel_id=1, source_target_pairs={{0,2},{2,0},{4,6},{6,4},{8,10},{10,8},{12,14},{14,12},{16,18},{18,... | collective-permute-start | bytes 786440 | tf_op jit(solution)/shard_map/ppermute | solution.py:416
  15.0 10.2 %collective-permute-start.6 = (bf16[256,512]{1,0:T(8,128)(2,1)S(1)}, bf16[256,512]{1,0:T(8,128)(2,1)S(1)}, u32[]{:S(2)}, u32[]{:S(2)}) collective-permute-start(bf16[256,512]{1,0:T(8,128)(2,1)S(1)} %collective-permute-done.1.refs_2_.refs_9_), channel_id=1, source_target_pairs={{0,4},{2,6},{4,0},{6,2},{8,12},{10,14},{12,8},{14,10},{16,20},{18,... | collective-permute-start | bytes 786440 | tf_op jit(solution)/shard_map/ppermute | solution.py:416
  23.0 7.9 %collective-permute-start.10 = (bf16[256,512]{1,0:T(8,128)(2,1)S(1)}, bf16[256,512]{1,0:T(8,128)(2,1)S(1)}, u32[]{:S(2)}, u32[]{:S(2)}) collective-permute-start(bf16[256,512]{1,0:T(8,128)(2,1)S(1)} %collective-permute-done.5.refs_6_.refs_13_), channel_id=1, source_target_pairs={{0,8},{2,10},{4,12},{6,14},{8,0},{10,2},{12,4},{14,6},{16,24},{18,... | collective-permute-start | bytes 786440 | tf_op jit(solution)/shard_map/ppermute | solution.py:416
  23.6 8.0 %collective-permute-start.9 = (bf16[256,512]{1,0:T(8,128)(2,1)S(1)}, bf16[256,512]{1,0:T(8,128)(2,1)S(1)}, u32[]{:S(2)}, u32[]{:S(2)}) collective-permute-start(bf16[256,512]{1,0:T(8,128)(2,1)S(1)} %collective-permute-done.5.refs_6_.refs_13_), channel_id=1, source_target_pairs={{0,4},{2,6},{4,0},{6,2},{8,12},{10,14},{12,8},{14,10},{16,20},{18,... | collective-permute-start | bytes 786440 | tf_op jit(solution)/shard_map/ppermute | solution.py:416
  24.1 7.5 %collective-permute-start.4 = (bf16[256,512]{1,0:T(8,128)(2,1)S(1)}, bf16[256,512]{1,0:T(8,128)(2,1)S(1)}, u32[]{:S(2)}, u32[]{:S(2)}) collective-permute-start(bf16[256,512]{1,0:T(8,128)(2,1)S(1)} %collective-permute-done.3.refs_4_.refs_11_), channel_id=1, source_target_pairs={{0,2},{2,0},{4,6},{6,4},{8,10},{10,8},{12,14},{14,12},{16,18},{18,... | collective-permute-start | bytes 786440 | tf_op jit(solution)/shard_map/ppermute | solution.py:416
  25.2 6.9 %collective-permute-start.7 = (bf16[256,512]{1,0:T(8,128)(2,1)S(1)}, bf16[256,512]{1,0:T(8,128)(2,1)S(1)}, u32[]{:S(2)}, u32[]{:S(2)}) collective-permute-start(bf16[256,512]{1,0:T(8,128)(2,1)S(1)} %collective-permute-done.5.refs_6_.refs_13_), channel_id=1, source_target_pairs={{0,2},{2,0},{4,6},{6,4},{8,10},{10,8},{12,14},{14,12},{16,18},{18,... | collective-permute-start | bytes 786440 | tf_op jit(solution)/shard_map/ppermute | solution.py:416
  25.2 20.1 %collective-permute-start.16 = (bf16[256,2048]{1,0:T(8,128)(2,1)S(1)}, bf16[256,2048]{1,0:T(8,128)(2,1)S(1)}, u32[]{:S(2)}, u32[]{:S(2)}) collective-permute-start(bf16[256,2048]{1,0:T(8,128)(2,1)S(1)} %bitcast.7), channel_id=1, source_target_pairs={{0,2},{2,0},{4,6},{6,4},{8,10},{10,8},{12,14},{14,12},{16,18},{18,... | collective-permute-start | bytes 3145736 | tf_op jit(solution)/shard_map/ppermute | solution.py:416
  31.0 3.5 %collective-permute-start.8 = (bf16[256,512]{1,0:T(8,128)(2,1)S(1)}, bf16[256,512]{1,0:T(8,128)(2,1)S(1)}, u32[]{:S(2)}, u32[]{:S(2)}) collective-permute-start(bf16[256,512]{1,0:T(8,128)(2,1)S(1)} %collective-permute-done.6.refs_8_.refs_15_), channel_id=1, source_target_pairs={{0,2},{2,0},{4,6},{6,4},{8,10},{10,8},{12,14},{14,12},{16,18},{18,... | collective-permute-start | bytes 786440 | tf_op jit(solution)/shard_map/ppermute | solution.py:416
  31.6 2.8 %collective-permute-start.12 = (bf16[256,512]{1,0:T(8,128)(2,1)S(1)}, bf16[256,512]{1,0:T(8,128)(2,1)S(1)}, u32[]{:S(2)}, u32[]{:S(2)}) collective-permute-start(bf16[256,512]{1,0:T(8,128)(2,1)S(1)} %collective-permute-done.10.refs_12_.refs_19_), channel_id=1, source_target_pairs={{0,2},{2,0},{4,6},{6,4},{8,10},{10,8},{12,14},{14,12},{16,18},{18,... | collective-permute-start | bytes 786440 | tf_op jit(solution)/shard_map/ppermute | solution.py:416
  31.6 2.8 %collective-permute-start.11 = (bf16[256,512]{1,0:T(8,128)(2,1)S(1)}, bf16[256,512]{1,0:T(8,128)(2,1)S(1)}, u32[]{:S(2)}, u32[]{:S(2)}) collective-permute-start(bf16[256,512]{1,0:T(8,128)(2,1)S(1)} %collective-permute-done.9.refs_10_.refs_17_), channel_id=1, source_target_pairs={{0,2},{2,0},{4,6},{6,4},{8,10},{10,8},{12,14},{14,12},{16,18},{18,... | collective-permute-start | bytes 786440 | tf_op jit(solution)/shard_map/ppermute | solution.py:416
  32.1 8.3 %collective-permute-start.13 = (bf16[256,512]{1,0:T(8,128)(2,1)S(1)}, bf16[256,512]{1,0:T(8,128)(2,1)S(1)}, u32[]{:S(2)}, u32[]{:S(2)}) collective-permute-start(bf16[256,512]{1,0:T(8,128)(2,1)S(1)} %collective-permute-done.10.refs_12_.refs_19_), channel_id=1, source_target_pairs={{0,4},{2,6},{4,0},{6,2},{8,12},{10,14},{12,8},{14,10},{16,20},{18,... | collective-permute-start | bytes 786440 | tf_op jit(solution)/shard_map/ppermute | solution.py:416
  40.4 1.9 %collective-permute-start.14 = (bf16[256,512]{1,0:T(8,128)(2,1)S(1)}, bf16[256,512]{1,0:T(8,128)(2,1)S(1)}, u32[]{:S(2)}, u32[]{:S(2)}) collective-permute-start(bf16[256,512]{1,0:T(8,128)(2,1)S(1)} %collective-permute-done.13.refs_1_.refs_14_.refs_21_), channel_id=1, source_target_pairs={{0,2},{2,0},{4,6},{6,4},{8,10},{10,8},{12,14},{14,12},{16,18},{18,... | collective-permute-start | bytes 786440 | tf_op jit(solution)/shard_map/ppermute | solution.py:416
  41.8 1.4 %collective-permute-start.15 = (f32[16,256]{1,0:T(8,128)S(1)}, f32[16,256]{1,0:T(8,128)S(1)}, u32[]{:S(2)}, u32[]{:S(2)}) collective-permute-start(f32[16,256]{1,0:T(8,128)S(1)} %partial_den.9.refs_2_), channel_id=1, source_target_pairs={{0,2},{2,0},{4,6},{6,4},{8,10},{10,8},{12,14},{14,12},{16,18},{18,... | collective-permute-start | bytes 49160 | tf_op jit(solution)/shard_map/ppermute | solution.py:416
  45.0 1.6 %collective-permute-start.17 = (bf16[256,512]{1,0:T(8,128)(2,1)S(1)}, bf16[256,512]{1,0:T(8,128)(2,1)S(1)}, u32[]{:S(2)}, u32[]{:S(2)}) collective-permute-start(bf16[256,512]{1,0:T(8,128)(2,1)S(1)} %get-tuple-element.59.refs_2_), channel_id=1, source_target_pairs={{0,2},{2,0},{4,6},{6,4},{8,10},{10,8},{12,14},{14,12},{16,18},{18,... | collective-permute-start | bytes 786440 | tf_op jit(solution)/shard_map/ppermute | solution.py:416
  47.1 6.6 %collective-permute-start.18 = (bf16[128,512]{1,0:T(8,128)(2,1)S(1)}, bf16[128,512]{1,0:T(8,128)(2,1)S(1)}, u32[]{:S(2)}, u32[]{:S(2)}) collective-permute-start(bf16[128,512]{1,0:T(8,128)(2,1)S(1)} %get-tuple-element.62), channel_id=1, source_target_pairs={{0,1},{1,0},{2,3},{3,2},{4,5},{5,4},{6,7},{7,6},{8,9},{9,8},{10,11... | collective-permute-start | bytes 393224 | tf_op jit(solution)/shard_map/ppermute | solution.py:416
  48.6 8.9 %collective-permute-start.19 = (bf16[128,512]{1,0:T(8,128)(2,1)S(1)}, bf16[128,512]{1,0:T(8,128)(2,1)S(1)}, u32[]{:S(2)}, u32[]{:S(2)}) collective-permute-start(bf16[128,512]{1,0:T(8,128)(2,1)S(1)} %get-tuple-element.63), channel_id=1, source_target_pairs={{0,4},{2,6},{4,0},{6,2},{8,12},{10,14},{12,8},{14,10},{16,20},{18,... | collective-permute-start | bytes 393224 | tf_op jit(solution)/shard_map/ppermute | solution.py:416
  49.6 7.9 %collective-permute-start.20 = (bf16[128,512]{1,0:T(8,128)(2,1)S(1)}, bf16[128,512]{1,0:T(8,128)(2,1)S(1)}, u32[]{:S(2)}, u32[]{:S(2)}) collective-permute-start(bf16[128,512]{1,0:T(8,128)(2,1)S(1)} %get-tuple-element.64), channel_id=1, source_target_pairs={{0,5},{1,4},{2,7},{3,6},{4,1},{5,0},{6,3},{7,2},{8,13},{9,12},{10,... | collective-permute-start | bytes 393224 | tf_op jit(solution)/shard_map/ppermute | solution.py:437
  51.1 13.3 %collective-permute-start.22 = (bf16[128,512]{1,0:T(8,128)(2,1)S(1)}, bf16[128,512]{1,0:T(8,128)(2,1)S(1)}, u32[]{:S(2)}, u32[]{:S(2)}) collective-permute-start(bf16[128,512]{1,0:T(8,128)(2,1)S(1)} %get-tuple-element.67), channel_id=1, source_target_pairs={{0,1},{1,0},{2,3},{3,2},{4,5},{5,4},{6,7},{7,6},{8,9},{9,8},{10,11... | collective-permute-start | bytes 393224 | tf_op jit(solution)/shard_map/ppermute | solution.py:416
  52.7 11.8 %collective-permute-start.23 = (bf16[128,512]{1,0:T(8,128)(2,1)S(1)}, bf16[128,512]{1,0:T(8,128)(2,1)S(1)}, u32[]{:S(2)}, u32[]{:S(2)}) collective-permute-start(bf16[128,512]{1,0:T(8,128)(2,1)S(1)} %get-tuple-element.68), channel_id=1, source_target_pairs={{0,4},{2,6},{4,0},{6,2},{8,12},{10,14},{12,8},{14,10},{16,20},{18,... | collective-permute-start | bytes 393224 | tf_op jit(solution)/shard_map/ppermute | solution.py:416
  53.7 10.8 %collective-permute-start.24 = (bf16[128,512]{1,0:T(8,128)(2,1)S(1)}, bf16[128,512]{1,0:T(8,128)(2,1)S(1)}, u32[]{:S(2)}, u32[]{:S(2)}) collective-permute-start(bf16[128,512]{1,0:T(8,128)(2,1)S(1)} %get-tuple-element.69), channel_id=1, source_target_pairs={{0,5},{1,4},{2,7},{3,6},{4,1},{5,0},{6,3},{7,2},{8,13},{9,12},{10,... | collective-permute-start | bytes 393224 | tf_op jit(solution)/shard_map/ppermute | solution.py:437
  57.6 6.8 %collective-permute-start.21 = (bf16[64,512]{1,0:T(8,128)(2,1)S(1)}, bf16[64,512]{1,0:T(8,128)(2,1)S(1)}, u32[]{:S(2)}, u32[]{:S(2)}) collective-permute-start(bf16[64,512]{1,0:T(8,128)(2,1)S(1)} %get-tuple-element.65), channel_id=1, source_target_pairs={{0,16},{2,18},{4,20},{6,22},{8,24},{10,26},{12,28},{14,30},{16,0},... | collective-permute-start | bytes 196616 | tf_op jit(solution)/shard_map/ppermute | solution.py:416
  60.8 6.3 %collective-permute-start.25 = (bf16[64,512]{1,0:T(8,128)(2,1)S(1)}, bf16[64,512]{1,0:T(8,128)(2,1)S(1)}, u32[]{:S(2)}, u32[]{:S(2)}) collective-permute-start(bf16[64,512]{1,0:T(8,128)(2,1)S(1)} %get-tuple-element.71), channel_id=1, source_target_pairs={{0,24},{2,26},{4,28},{6,30},{8,16},{10,18},{12,20},{14,22},{16,8},... | collective-permute-start | bytes 196616 | tf_op jit(solution)/shard_map/ppermute | solution.py:416
  64.6 4.8 %collective-permute-start.26 = (bf16[64,512]{1,0:T(8,128)(2,1)S(1)}, bf16[64,512]{1,0:T(8,128)(2,1)S(1)}, u32[]{:S(2)}, u32[]{:S(2)}) collective-permute-start(bf16[64,512]{1,0:T(8,128)(2,1)S(1)} %get-tuple-element.72), channel_id=1, source_target_pairs={{0,8},{2,10},{4,12},{6,14},{8,0},{10,2},{12,4},{14,6},{16,24},{18,... | collective-permute-start | bytes 196616 | tf_op jit(solution)/shard_map/ppermute | solution.py:416
  69.4 4.8 %collective-permute-start.35 = (bf16[64,512]{1,0:T(8,128)(2,1)S(1)}, bf16[64,512]{1,0:T(8,128)(2,1)S(1)}, u32[]{:S(2)}, u32[]{:S(2)}) collective-permute-start(bf16[64,512]{1,0:T(8,128)(2,1)S(1)} %add_convert_fusion), channel_id=1, source_target_pairs={{0,8},{2,10},{4,12},{6,14},{8,0},{10,2},{12,4},{14,6},{16,24},{18,... | collective-permute-start | bytes 196616 | tf_op jit(solution)/shard_map/ppermute | solution.py:416
  69.5 8.3 %collective-permute-start.28 = (bf16[64,512]{1,0:T(8,128)(2,1)S(1)}, bf16[64,512]{1,0:T(8,128)(2,1)S(1)}, u32[]{:S(2)}, u32[]{:S(2)}) collective-permute-start(bf16[64,512]{1,0:T(8,128)(2,1)S(1)} %add_convert_fusion), channel_id=1, source_target_pairs={{0,24},{2,26},{4,28},{6,30},{8,16},{10,18},{12,20},{14,22},{16,8},... | collective-permute-start | bytes 196616 | tf_op jit(solution)/shard_map/ppermute | solution.py:416
  72.0 5.8 %collective-permute-start.27 = (bf16[64,512]{1,0:T(8,128)(2,1)S(1)}, bf16[64,512]{1,0:T(8,128)(2,1)S(1)}, u32[]{:S(2)}, u32[]{:S(2)}) collective-permute-start(bf16[64,512]{1,0:T(8,128)(2,1)S(1)} %add_convert_fusion), channel_id=1, source_target_pairs={{0,16},{2,18},{4,20},{6,22},{8,24},{10,26},{12,28},{14,30},{16,0},... | collective-permute-start | bytes 196616 | tf_op jit(solution)/shard_map/ppermute | solution.py:416
  74.2 6.3 %collective-permute-start.36 = (bf16[2,64,512]{2,1,0:T(8,128)(2,1)S(1)}, bf16[2,64,512]{2,1,0:T(8,128)(2,1)S(1)}, u32[]{:S(2)}, u32[]{:S(2)}) collective-permute-start(bf16[2,64,512]{2,1,0:T(8,128)(2,1)S(1)} %pad_maximum_fusion.2), channel_id=1, source_target_pairs={{0,1},{1,0},{2,3},{3,2},{4,5},{5,4},{6,7},{7,6},{8,9},{9,8},{10,11... | collective-permute-start | bytes 393224 | tf_op jit(solution)/shard_map/ppermute | solution.py:416
  74.7 7.7 %collective-permute-start.37 = (bf16[2,64,512]{2,1,0:T(8,128)(2,1)S(1)}, bf16[2,64,512]{2,1,0:T(8,128)(2,1)S(1)}, u32[]{:S(2)}, u32[]{:S(2)}) collective-permute-start(bf16[2,64,512]{2,1,0:T(8,128)(2,1)S(1)} %pad_maximum_fusion.2), channel_id=1, source_target_pairs={{0,4},{2,6},{4,0},{6,2},{8,12},{10,14},{12,8},{14,10},{16,20},{18,... | collective-permute-start | bytes 393224 | tf_op jit(solution)/shard_map/ppermute | solution.py:416
  76.0 6.2 %collective-permute-start.38 = (bf16[2,64,512]{2,1,0:T(8,128)(2,1)S(1)}, bf16[2,64,512]{2,1,0:T(8,128)(2,1)S(1)}, u32[]{:S(2)}, u32[]{:S(2)}) collective-permute-start(bf16[2,64,512]{2,1,0:T(8,128)(2,1)S(1)} %pad_maximum_fusion.2), channel_id=1, source_target_pairs={{0,5},{1,4},{2,7},{3,6},{4,1},{5,0},{6,3},{7,2},{8,13},{9,12},{10,... | collective-permute-start | bytes 393224 | tf_op jit(solution)/shard_map/ppermute | solution.py:437
  77.8 5.7 %collective-permute-start.29 = (bf16[2,64,512]{2,1,0:T(8,128)(2,1)S(1)}, bf16[2,64,512]{2,1,0:T(8,128)(2,1)S(1)}, u32[]{:S(2)}, u32[]{:S(2)}) collective-permute-start(bf16[2,64,512]{2,1,0:T(8,128)(2,1)S(1)} %pad_maximum_fusion.1), channel_id=1, source_target_pairs={{0,1},{1,0},{2,3},{3,2},{4,5},{5,4},{6,7},{7,6},{8,9},{9,8},{10,11... | collective-permute-start | bytes 393224 | tf_op jit(solution)/shard_map/ppermute | solution.py:416
  79.0 5.0 %collective-permute-start.30 = (bf16[2,64,512]{2,1,0:T(8,128)(2,1)S(1)}, bf16[2,64,512]{2,1,0:T(8,128)(2,1)S(1)}, u32[]{:S(2)}, u32[]{:S(2)}) collective-permute-start(bf16[2,64,512]{2,1,0:T(8,128)(2,1)S(1)} %pad_maximum_fusion.1), channel_id=1, source_target_pairs={{0,4},{2,6},{4,0},{6,2},{8,12},{10,14},{12,8},{14,10},{16,20},{18,... | collective-permute-start | bytes 393224 | tf_op jit(solution)/shard_map/ppermute | solution.py:416
  80.5 5.9 %collective-permute-start.31 = (bf16[2,64,512]{2,1,0:T(8,128)(2,1)S(1)}, bf16[2,64,512]{2,1,0:T(8,128)(2,1)S(1)}, u32[]{:S(2)}, u32[]{:S(2)}) collective-permute-start(bf16[2,64,512]{2,1,0:T(8,128)(2,1)S(1)} %pad_maximum_fusion.1), channel_id=1, source_target_pairs={{0,5},{1,4},{2,7},{3,6},{4,1},{5,0},{6,3},{7,2},{8,13},{9,12},{10,... | collective-permute-start | bytes 393224 | tf_op jit(solution)/shard_map/ppermute | solution.py:437
  82.2 4.3 %collective-permute-start.39 = (bf16[2,64,512]{2,1,0:T(8,128)(2,1)S(1)}, bf16[2,64,512]{2,1,0:T(8,128)(2,1)S(1)}, u32[]{:S(2)}, u32[]{:S(2)}) collective-permute-start(bf16[2,64,512]{2,1,0:T(8,128)(2,1)S(1)} %collective-permute-done.36.refs_1_), channel_id=1, source_target_pairs={{0,2},{2,0},{4,6},{6,4},{8,10},{10,8},{12,14},{14,12},{16,18},{18,... | collective-permute-start | bytes 393224 | tf_op jit(solution)/shard_map/ppermute | solution.py:416
  82.4 5.3 %collective-permute-start.42 = (bf16[4,64,512]{2,1,0:T(8,128)(2,1)S(1)}, bf16[4,64,512]{2,1,0:T(8,128)(2,1)S(1)}, u32[]{:S(2)}, u32[]{:S(2)}) collective-permute-start(bf16[4,64,512]{2,1,0:T(8,128)(2,1)S(1)} %pad_maximum_fusion.refs_0_), channel_id=1, source_target_pairs={{0,2},{2,0},{4,6},{6,4},{8,10},{10,8},{12,14},{14,12},{16,18},{18,... | collective-permute-start | bytes 786440 | tf_op jit(solution)/shard_map/ppermute | solution.py:416
  83.5 3.4 %collective-permute-start.40 = (bf16[2,64,512]{2,1,0:T(8,128)(2,1)S(1)}, bf16[2,64,512]{2,1,0:T(8,128)(2,1)S(1)}, u32[]{:S(2)}, u32[]{:S(2)}) collective-permute-start(bf16[2,64,512]{2,1,0:T(8,128)(2,1)S(1)} %collective-permute-done.37.refs_2_), channel_id=1, source_target_pairs={{0,2},{2,0},{4,6},{6,4},{8,10},{10,8},{12,14},{14,12},{16,18},{18,... | collective-permute-start | bytes 393224 | tf_op jit(solution)/shard_map/ppermute | solution.py:416
  84.0 5.5 %collective-permute-start.32 = (bf16[2,64,512]{2,1,0:T(8,128)(2,1)S(1)}, bf16[2,64,512]{2,1,0:T(8,128)(2,1)S(1)}, u32[]{:S(2)}, u32[]{:S(2)}) collective-permute-start(bf16[2,64,512]{2,1,0:T(8,128)(2,1)S(1)} %collective-permute-done.29.refs_0_), channel_id=1, source_target_pairs={{0,2},{2,0},{4,6},{6,4},{8,10},{10,8},{12,14},{14,12},{16,18},{18,... | collective-permute-start | bytes 393224 | tf_op jit(solution)/shard_map/ppermute | solution.py:416
  86.4 1.3 %collective-permute-start.41 = (bf16[2,64,512]{2,1,0:T(8,128)(2,1)S(1)}, bf16[2,64,512]{2,1,0:T(8,128)(2,1)S(1)}, u32[]{:S(2)}, u32[]{:S(2)}) collective-permute-start(bf16[2,64,512]{2,1,0:T(8,128)(2,1)S(1)} %collective-permute-done.38.refs_3_), channel_id=1, source_target_pairs={{0,2},{2,0},{4,6},{6,4},{8,10},{10,8},{12,14},{14,12},{16,18},{18,... | collective-permute-start | bytes 393224 | tf_op jit(solution)/shard_map/ppermute | solution.py:416
  86.4 3.0 %collective-permute-start.33 = (bf16[2,64,512]{2,1,0:T(8,128)(2,1)S(1)}, bf16[2,64,512]{2,1,0:T(8,128)(2,1)S(1)}, u32[]{:S(2)}, u32[]{:S(2)}) collective-permute-start(bf16[2,64,512]{2,1,0:T(8,128)(2,1)S(1)} %collective-permute-done.30.refs_1_), channel_id=1, source_target_pairs={{0,2},{2,0},{4,6},{6,4},{8,10},{10,8},{12,14},{14,12},{16,18},{18,... | collective-permute-start | bytes 393224 | tf_op jit(solution)/shard_map/ppermute | solution.py:416
  86.9 2.5 %collective-permute-start.34 = (bf16[2,64,512]{2,1,0:T(8,128)(2,1)S(1)}, bf16[2,64,512]{2,1,0:T(8,128)(2,1)S(1)}, u32[]{:S(2)}, u32[]{:S(2)}) collective-permute-start(bf16[2,64,512]{2,1,0:T(8,128)(2,1)S(1)} %collective-permute-done.31.refs_2_), channel_id=1, source_target_pairs={{0,2},{2,0},{4,6},{6,4},{8,10},{10,8},{12,14},{14,12},{16,18},{18,... | collective-permute-start | bytes 393224 | tf_op jit(solution)/shard_map/ppermute | solution.py:416
